TPU v7x, 32 devices: a whole 2x2x4 slice. The times are simulated.
32 devices in a mesh: dp: 8 (over z, x), tensor: 4 (over y, core).
Axes of the slice: x: 2, y: 2, z: 4, core: 2. Of those that a mesh axis runs over, the one named last changes fastest.
Arguments:
- tokens: bfloat16 [16384, 2048], P('dp'), may hold values from -43 to 43
- cotangent: bfloat16 [16384, 2048], P('dp'), may hold values from -12 to 12
- doc_ids: int32 [16, 1024], P('dp'), may hold values from 0 to 7, never falling along the last dimension, each value on 1 to 512 neighbouring positions
- tile_slots: int32 [4, 384], P('tensor'), may hold values from 0 to 383, each once within a row
- matrix_tiles: float32 [4, 384, 128, 128], P('tensor', 'dp'), may hold values from -0.125 to 0.125
- left_stats: float32 [4, 384, 128, 128], P('tensor', 'dp'), may hold values from -2097152 to 4194304
- right_stats: float32 [4, 384, 128, 128], P('tensor', 'dp'), may hold values from -2097152 to 4194304
- left_roots: float32 [4, 384, 128, 128], P('tensor', 'dp'), may hold values from -1 to 2
- right_roots: float32 [4, 384, 128, 128], P('tensor', 'dp'), may hold values from -1 to 2
- side_weight: float32 [2048, 320], P('dp'), may hold values from -0.125 to 0.125
- side_moment: float32 [2048, 320], P('dp'), may hold values from -24 to 24
- side_second: float32 [2048, 320], P('dp'), may hold values from 81.92 to 327.68
- vector_params: float32 [4, 7024], P('tensor'), may hold values from -7 to 5
- vector_moment: float32 [4, 7024], P('tensor'), may hold values from -40 to 40
- vector_second: float32 [4, 7024], P('tensor'), may hold values from 212.992 to 851.968
Outputs:
- mixed: bfloat16 [16384, 2048], P('dp')
- input_grad: float32 [16384, 2048], P('dp')
- tile_grads: float32 [4, 384, 128, 128], P('tensor', 'dp')
- left_new: float32 [4, 384, 128, 128], P('tensor', 'dp')
- right_new: float32 [4, 384, 128, 128], P('tensor', 'dp')
- tiles_new: float32 [4, 384, 128, 128], P('tensor', 'dp')
- tiles_copy: bfloat16 [4, 384, 128, 128], P('tensor', 'dp')
- side_moment_new: float32 [2048, 320], P('dp')
- side_second_new: float32 [2048, 320], P('dp')
- side_new: float32 [2048, 320], P('dp')
- vector_moment_new: float32 [4, 7024], P('tensor')
- vector_second_new: float32 [4, 7024], P('tensor')
- vector_new: float32 [4, 7024], P('tensor')
Inputs may be any that keep to these rules, and one draw needn't show every extreme that they name: `doc_ids`: within each sequence the document number starts at 0, never falls and rises by one where a document starts; no document is longer than 512 positions. For each tensor index t, a permutation: tile k of t is kept in slot tile_slots[t, k] of matrix_tiles, of the statistics, of the roots and of the tile outputs.
All inputs are finite; a program needn't handle non-finite values.
Results may differ from a plain program's by a relative error of at most 0.0045.
The roundings to bfloat16 on the way count: a program that leaves them out, or rounds other values in their place, can miss the bound.
Values may be sent and summed in bfloat16 or wider, within the bound.
No kernel may reach another device: no remote copies, remote signals or barrier semaphores. Data moves between devices by JAX's collectives and lax.ppermute only.
A program may use at most 320 MiB of HBM per device.

v0:
```python
import jax
import jax.numpy as jnp
from jax import lax
from jax.sharding import PartitionSpec as P

D = 2048
HEADS = 64
NS = 128
CONV = 4
SSD_BLOCK = 256
SEQ = 1024
SEQS_DEV = 1
MICRO = 2
TILE = 128
STEP = 10
DI = 4096
SIDE = 320


EPS = 1e-05
HIGH = lax.Precision.HIGHEST
STAT_DECAY = 0.5
LR_MAT = 0.25
LR_SIDE = 0.02
LR_VEC = 0.25
BETA_ONE = 0.9
BETA_TWO = 0.95
ADAM_EPS = 1e-08
DECAY_WD = 0.1


def segment_bounds(di_local, heads_local, model_local, bc_local, tap_count):
    widths = [
        tap_count * di_local,
        di_local,
        di_local,
        heads_local,
        heads_local,
        heads_local,
        model_local,
        tap_count * bc_local,
        bc_local,
    ]
    bounds = [0]
    for item in widths:
        bounds.append(bounds[-1] + item)
    return bounds


def causal_conv(values, kernel, offsets, documents):
    tap_count = kernel.shape[0]
    seq_len = values.shape[1]
    padded = jnp.pad(values, ((0, 0), (tap_count - 1, 0), (0, 0)))
    doc_pad = jnp.pad(documents, ((0, 0), (tap_count - 1, 0)), constant_values=-1)
    summed = jnp.zeros_like(values) + offsets
    for k in range(tap_count):
        matches = (doc_pad[:, k : k + seq_len] == documents)[:, :, None]
        summed = summed + kernel[k] * jnp.where(matches, padded[:, k : k + seq_len], 0.0)
    return summed


def block_scan(activated, step_sizes, decay_rate, in_states, out_states, segment):
    length = activated.shape[0]
    blocks = length // SSD_BLOCK
    head_count = activated.shape[1]
    x_blocks = activated.reshape(blocks, SSD_BLOCK, head_count, -1)
    dt_blocks = step_sizes.reshape(blocks, SSD_BLOCK, head_count)
    b_blocks = in_states.reshape(blocks, SSD_BLOCK, -1)
    c_blocks = out_states.reshape(blocks, SSD_BLOCK, -1)
    doc_blocks = segment.reshape(blocks, SSD_BLOCK)
    before = jnp.concatenate([jnp.full((1,), -1, jnp.int32), doc_blocks[:-1, -1]])
    positions = jnp.arange(SSD_BLOCK)
    causal_ok = positions[:, None] >= positions[None, :]

    def advance(carry_state, block):
        span_x, span_dt, span_b, span_c, span_doc, prev_doc = block
        cumulative = jnp.cumsum(span_dt * decay_rate, axis=0)
        allowed = (causal_ok & (span_doc[:, None] == span_doc[None, :]))[:, :, None]
        spread = cumulative[:, None, :] - cumulative[None, :, :]
        decays = jnp.where(allowed, jnp.exp(jnp.where(allowed, spread, 0.0)), 0.0)
        scores = jnp.dot(span_c, span_b.T, precision=HIGH, preferred_element_type=jnp.float32)
        weights = scores[:, :, None] * decays * span_dt[None, :, :]
        output = jnp.einsum("tsh,shp->thp", weights, span_x, precision=HIGH)
        carried = jnp.where((span_doc == prev_doc)[:, None], jnp.exp(cumulative), 0.0)
        output = (
            output
            + jnp.einsum("tn,hnp->thp", span_c, carry_state, precision=HIGH) * carried[:, :, None]
        )
        last_cum = cumulative[-1]
        tail_ok = (span_doc == span_doc[-1])[:, None]
        tail_decay = jnp.where(
            tail_ok, jnp.exp(jnp.where(tail_ok, last_cum[None, :] - cumulative, 0.0)), 0.0
        )
        new_part = jnp.einsum(
            "sn,shp->hnp", span_b, span_x * (tail_decay * span_dt)[:, :, None], precision=HIGH
        )
        keep_decay = jnp.where(span_doc[-1] == prev_doc, jnp.exp(last_cum), 0.0)
        return (keep_decay[:, None, None] * carry_state + new_part, output)

    initial = jnp.zeros((head_count, in_states.shape[1], activated.shape[2]), jnp.float32)
    _, outputs = lax.scan(
        jax.checkpoint(advance),
        initial,
        (x_blocks, dt_blocks, b_blocks, c_blocks, doc_blocks, before),
    )
    return outputs.reshape(length, head_count, -1)


def one_sequence(items, decay_rate):
    seq_x, seq_dt, seq_states, seq_doc = items
    half_width = seq_states.shape[1] // 2
    head_count = decay_rate.shape[0]
    shaped = seq_x.reshape(seq_x.shape[0], head_count, -1)
    return block_scan(
        shaped, seq_dt, decay_rate, seq_states[:, :half_width], seq_states[:, half_width:], seq_doc
    )


def mixer(
    x_proj, dt_raw, bc_act, conv_kernel, conv_offset, log_rate, skip_gain, dt_offset, documents
):
    sequences = documents.shape[0]
    width = x_proj.shape[1]
    row_count = x_proj.shape[0]
    head_count = log_rate.shape[0]
    conv_out = causal_conv(
        x_proj.reshape(sequences, -1, width), conv_kernel, conv_offset, documents
    )
    activated = jax.nn.silu(conv_out)
    step_sizes = jax.nn.softplus(dt_raw + dt_offset).reshape(sequences, -1, head_count)
    decay_rate = -jnp.exp(log_rate)
    states = bc_act.reshape(sequences, -1, bc_act.shape[1])
    checked = jax.checkpoint(one_sequence)
    scanned = lax.map(
        lambda items: checked(items, decay_rate), (activated, step_sizes, states, documents)
    )
    flat_act = activated.reshape(row_count, width)
    return scanned.reshape(row_count, width) + jnp.repeat(skip_gain, width // head_count) * flat_act


def adam_update(weight, moment, second, gradient, learn_rate):
    moment_new = BETA_ONE * moment + (1.0 - BETA_ONE) * gradient
    second_new = BETA_TWO * second + (1.0 - BETA_TWO) * gradient * gradient
    corrected = moment_new / (1.0 - BETA_ONE**STEP)
    scaled = jnp.sqrt(second_new / (1.0 - BETA_TWO**STEP)) + ADAM_EPS
    return (moment_new, second_new, weight - learn_rate * (corrected / scaled + DECAY_WD * weight))


def contract_rows(left, right):
    return lax.dot_general(
        left, right, (((0,), (0,)), ((), ())), preferred_element_type=jnp.float32
    )


def contract_cols(left, right):
    return lax.dot_general(
        left, right, (((1,), (1,)), ((), ())), preferred_element_type=jnp.float32
    )


def silu_slope(values):
    sigma = jax.nn.sigmoid(values)
    return sigma * (1.0 + values * (1.0 - sigma))


def on_device(
    tokens,
    cotangent,
    doc_ids,
    tile_slots,
    matrix_tiles,
    left_stats,
    right_stats,
    left_roots,
    right_roots,
    side_weight,
    side_moment,
    side_second,
    vector_params,
    vector_moment,
    vector_second,
):
    n_tensor = lax.axis_size("tensor")
    tensor_rank = lax.axis_index("tensor")
    di_local = DI // n_tensor
    heads_local = HEADS // n_tensor
    model_local = D // n_tensor
    bc_local = 2 * NS // n_tensor
    batch_rows = SEQS_DEV * SEQ
    share_rows = batch_rows // n_tensor
    row_tiles = D // TILE
    col_tiles = di_local // TILE
    per_block = row_tiles * col_tiles
    slot_map = tile_slots[0]
    tile_count = slot_map.shape[0]
    inverse_slots = (
        jnp.zeros((tile_count,), jnp.int32)
        .at[slot_map]
        .set(jnp.arange(tile_count, dtype=jnp.int32))
    )
    vector = vector_params[0]
    bounds = segment_bounds(di_local, heads_local, model_local, bc_local, CONV)

    def segment_of(index):
        return vector[bounds[index] : bounds[index + 1]]

    conv_kernel = segment_of(0).reshape(CONV, di_local)
    conv_offset = segment_of(1)
    gate_gain = segment_of(2)
    log_rate = segment_of(3)
    skip_gain = segment_of(4)
    dt_offset = segment_of(5)
    shared = lax.all_gather(vector[bounds[6] :][None, :], "tensor", axis=0, tiled=True)
    pre_gain = shared[:, :model_local].reshape(D)
    bc_kernel = (
        shared[:, model_local : model_local + CONV * bc_local]
        .reshape(n_tensor, CONV, bc_local)
        .transpose(1, 0, 2)
        .reshape(CONV, 2 * NS)
    )
    bc_offset = shared[:, model_local + CONV * bc_local :].reshape(2 * NS)
    grad_gate = jnp.zeros((D, di_local), jnp.float32)
    grad_input = jnp.zeros((D, di_local), jnp.float32)
    grad_output = jnp.zeros((di_local, D), jnp.float32)
    grad_side = jnp.zeros((D, SIDE), jnp.float32)
    grad_kernel = jnp.zeros_like(conv_kernel)
    grad_offset = jnp.zeros_like(conv_offset)
    grad_gain = jnp.zeros_like(gate_gain)
    grad_rate = jnp.zeros_like(log_rate)
    grad_skip = jnp.zeros_like(skip_gain)
    grad_dtoff = jnp.zeros_like(dt_offset)
    grad_pre = jnp.zeros((D,), jnp.float32)
    grad_bckern = jnp.zeros((CONV, 2 * NS), jnp.float32)
    grad_bcoff = jnp.zeros((2 * NS,), jnp.float32)
    mixed_parts = []
    input_parts = []
    for micro in range(MICRO):
        all_tiles = lax.all_gather(matrix_tiles[0].astype(jnp.bfloat16), "dp", axis=0, tiled=True)
        side_copy = lax.all_gather(side_weight.astype(jnp.bfloat16), "dp", axis=0, tiled=True)
        ordered = all_tiles[slot_map]
        w_gate = (
            ordered[:per_block]
            .reshape(row_tiles, col_tiles, TILE, TILE)
            .transpose(0, 2, 1, 3)
            .reshape(D, di_local)
        )
        w_input = (
            ordered[per_block : 2 * per_block]
            .reshape(row_tiles, col_tiles, TILE, TILE)
            .transpose(0, 2, 1, 3)
            .reshape(D, di_local)
        )
        gather_w_output = (
            ordered[2 * per_block :]
            .reshape(col_tiles, row_tiles, TILE, TILE)
            .transpose(0, 2, 1, 3)
            .reshape(di_local, D)
        )
        weights_now = (w_gate, w_input, gather_w_output, side_copy)
        w_gate, w_input, w_output, side_copy = weights_now
        first_row = micro * batch_rows
        residual = tokens[first_row : first_row + batch_rows].astype(jnp.float32)
        upstream = cotangent[first_row : first_row + batch_rows]
        documents = doc_ids[micro * SEQS_DEV : (micro + 1) * SEQS_DEV]
        inverse = lax.rsqrt(jnp.mean(residual * residual, axis=1, keepdims=True) + EPS)
        normed = (residual * inverse * pre_gain).astype(jnp.bfloat16)
        gate_pre = jnp.dot(normed, w_gate, preferred_element_type=jnp.float32)
        x_proj = jnp.dot(normed, w_input, preferred_element_type=jnp.float32)
        side_out = jnp.dot(normed, side_copy, preferred_element_type=jnp.float32)
        dt_raw = lax.dynamic_slice_in_dim(
            side_out, 2 * NS + tensor_rank * heads_local, heads_local, 1
        )

        def bc_path(raw_states, kernel_in, offset_in):
            convolved = causal_conv(
                raw_states.reshape(SEQS_DEV, SEQ, -1), kernel_in, offset_in, documents
            )
            return jax.nn.silu(convolved).reshape(batch_rows, -1)

        bc_act, bc_pull = jax.vjp(bc_path, side_out[:, : 2 * NS], bc_kernel, bc_offset)

        def ssd_path(
            proj_in, raw_steps, states_in, kernel_in, offset_in, rate_in, skip_in, steps_off
        ):
            return mixer(
                proj_in,
                raw_steps,
                states_in,
                kernel_in,
                offset_in,
                rate_in,
                skip_in,
                steps_off,
                documents,
            )

        ssd, ssd_pull = jax.vjp(
            ssd_path,
            x_proj,
            dt_raw,
            bc_act,
            conv_kernel,
            conv_offset,
            log_rate,
            skip_gain,
            dt_offset,
        )
        gate_act = jax.nn.silu(gate_pre)
        gated = ssd * gate_act
        square_sum = lax.psum(jnp.sum(gated * gated, axis=1), "tensor")
        scale_rows = lax.rsqrt(square_sum / DI + EPS)[:, None]
        hidden = (gated * scale_rows * gate_gain).astype(jnp.bfloat16)
        own_rows = lax.psum_scatter(
            jnp.dot(hidden, w_output, preferred_element_type=jnp.float32),
            "tensor",
            scatter_dimension=0,
            tiled=True,
        )
        base_rows = lax.dynamic_slice_in_dim(residual, tensor_rank * share_rows, share_rows, 0)
        mixed_parts.append(
            lax.all_gather(
                (base_rows + own_rows).astype(jnp.bfloat16), "tensor", axis=0, tiled=True
            )
        )
        d_hidden = contract_cols(upstream, w_output)
        grad_output = grad_output + contract_rows(hidden, upstream)
        weighted = d_hidden * gate_gain
        grad_gain = grad_gain + jnp.sum(d_hidden * gated * scale_rows, axis=0)
        inner_sum = lax.psum(jnp.sum(weighted * gated, axis=1), "tensor")
        d_gated = scale_rows * weighted - gated * scale_rows**3 * (inner_sum / DI)[:, None]
        d_ssd = d_gated * gate_act
        d_gate = (d_gated * ssd * silu_slope(gate_pre)).astype(jnp.bfloat16)
        d_xproj, d_dtraw, d_bcact, g_kernel, g_offset, g_rate, g_skip, g_dtoff = ssd_pull(d_ssd)
        grad_kernel = grad_kernel + g_kernel
        grad_offset = grad_offset + g_offset
        grad_rate = grad_rate + g_rate
        grad_skip = grad_skip + g_skip
        grad_dtoff = grad_dtoff + g_dtoff
        dt_wide = lax.dynamic_update_slice_in_dim(
            jnp.zeros((batch_rows, HEADS), jnp.float32), d_dtraw, tensor_rank * heads_local, 1
        )
        bc_total, dt_total = lax.psum((d_bcact, dt_wide), "tensor")
        d_bcraw, g_bckern, g_bcoff = bc_pull(bc_total)
        grad_bckern = grad_bckern + g_bckern
        grad_bcoff = grad_bcoff + g_bcoff
        d_side = jnp.concatenate([d_bcraw, dt_total], axis=1).astype(jnp.bfloat16)
        d_input = d_xproj.astype(jnp.bfloat16)
        grad_gate = grad_gate + contract_rows(normed, d_gate)
        grad_input = grad_input + contract_rows(normed, d_input)
        grad_side = grad_side + contract_rows(normed, d_side)
        local_sum = contract_cols(d_gate, w_gate) + contract_cols(d_input, w_input)
        d_normed = lax.psum(local_sum, "tensor") + contract_cols(d_side, side_copy)
        weighted_in = d_normed * pre_gain
        grad_pre = grad_pre + jnp.sum(d_normed * residual * inverse, axis=0)
        input_parts.append(
            upstream.astype(jnp.float32)
            + inverse * weighted_in
            - residual * inverse**3 * jnp.mean(weighted_in * residual, axis=1, keepdims=True)
        )
    pre_share = lax.dynamic_slice_in_dim(grad_pre, tensor_rank * model_local, model_local, 0)
    kern_share = lax.dynamic_slice_in_dim(grad_bckern, tensor_rank * bc_local, bc_local, 1)
    off_share = lax.dynamic_slice_in_dim(grad_bcoff, tensor_rank * bc_local, bc_local, 0)
    packed_grad = jnp.concatenate(
        [
            grad_kernel.reshape(-1),
            grad_offset,
            grad_gain,
            grad_rate,
            grad_skip,
            grad_dtoff,
            pre_share,
            kern_share.reshape(-1),
            off_share,
        ]
    )
    vector_total = lax.psum(packed_grad[None, :], "dp")
    tiles_gate = (
        grad_gate.reshape(row_tiles, TILE, col_tiles, TILE)
        .transpose(0, 2, 1, 3)
        .reshape(per_block, TILE, TILE)
    )
    tiles_input = (
        grad_input.reshape(row_tiles, TILE, col_tiles, TILE)
        .transpose(0, 2, 1, 3)
        .reshape(per_block, TILE, TILE)
    )
    tiles_output = (
        grad_output.reshape(col_tiles, TILE, row_tiles, TILE)
        .transpose(0, 2, 1, 3)
        .reshape(per_block, TILE, TILE)
    )
    in_slots = jnp.concatenate([tiles_gate, tiles_input, tiles_output], axis=0)[inverse_slots]
    tile_share, side_share = (
        lax.psum_scatter(in_slots, "dp", scatter_dimension=0, tiled=True),
        lax.psum_scatter(grad_side, "dp", scatter_dimension=0, tiled=True),
    )
    gram_left = jnp.einsum("kab,kcb->kac", tile_share, tile_share, precision=HIGH)
    gram_right = jnp.einsum("kba,kbc->kac", tile_share, tile_share, precision=HIGH)
    left_new = STAT_DECAY * left_stats[0] + (1.0 - STAT_DECAY) * gram_left
    right_new = STAT_DECAY * right_stats[0] + (1.0 - STAT_DECAY) * gram_right
    shaped = jnp.einsum("kab,kbc->kac", left_roots[0], tile_share, precision=HIGH)
    shaped = jnp.einsum("kab,kbc->kac", shaped, right_roots[0], precision=HIGH)
    tiles_new = matrix_tiles[0] - LR_MAT * shaped
    side_m, side_v, side_new = adam_update(
        side_weight, side_moment, side_second, side_share, LR_SIDE
    )
    vec_m, vec_v, vec_new = adam_update(
        vector_params, vector_moment, vector_second, vector_total, LR_VEC
    )
    mixed = jnp.concatenate(mixed_parts, axis=0)
    input_grad = jnp.concatenate(input_parts, axis=0)
    return (
        mixed,
        input_grad,
        tile_share[None],
        left_new[None],
        right_new[None],
        tiles_new[None],
        tiles_new.astype(jnp.bfloat16)[None],
        side_m,
        side_v,
        side_new,
        vec_m,
        vec_v,
        vec_new,
    )


def solution(mesh):
    return jax.shard_map(
        on_device,
        mesh=mesh,
        in_specs=(
            P("dp", None),
            P("dp", None),
            P("dp", None),
            P("tensor", None),
            P("tensor", "dp", None, None),
            P("tensor", "dp", None, None),
            P("tensor", "dp", None, None),
            P("tensor", "dp", None, None),
            P("tensor", "dp", None, None),
            P("dp", None),
            P("dp", None),
            P("dp", None),
            P("tensor", None),
            P("tensor", None),
            P("tensor", None),
        ),
        out_specs=(
            P("dp", None),
            P("dp", None),
            P("tensor", "dp", None, None),
            P("tensor", "dp", None, None),
            P("tensor", "dp", None, None),
            P("tensor", "dp", None, None),
            P("tensor", "dp", None, None),
            P("dp", None),
            P("dp", None),
            P("dp", None),
            P("tensor", None),
            P("tensor", None),
            P("tensor", None),
        ),
        check_vma=False,
    )
```

profile of v0, /device:TPU:0, one launch (start us, length us, event | category | flops | bytes accessed | tf_op | source)
XLA Modules:
  0.0 2793.8 jit_solution(14198164591201949055)
XLA Ops:
  28.3 27.4 all-gather.8.cloned.1.call-done
  83.0 150.5 %all-gather.6.cloned.1.call-done = bf16[384,128,128]{2,1,0:T(8,128)(2,1)} async-done(((bf16[48,128,128]{2,1,0:T(8,128)(2,1)}), bf16[384,128,128]{2,1,0:T(8,128)(2,1)}) %all-gather.6.cloned.1.call-update) | async-done | bytes 12582928 | tf_op jit(solution)/shard_map/all_gather | solution.py:238
  233.5 16.0 gather_fusion
  249.5 9.4 fusion.350
  275.4 9.7 fusion.334
  308.0 100.7 %while.155 = (s32[]{:T(128)}, f32[16,128,64]{1,2,0:T(8,128)}, f32[4,256,16,64]{1,3,2,0:T(8,128)}, f32[4,256,16,64]{1,3,2,0:T(8,128)}, f32[4,256,16]{1,0,2:T(4,12...) while((s32[]{:T(128)}, f32[16,128,64]{1,2,0:T(8,128)}, ...), condition=%wide.region_12.14_spmd.clone, body=%wide.region_9.13_spmd.clone.sunk | while | flops 1718448640 | bytes 14212321 | solution.py:135
  447.5 101.1 %while.154 = (s32[]{:T(128)}, f32[16,128,64]{1,2,0:T(8,128)}, f32[4,256,16,64]{1,3,2,0:T(8,128)}, f32[4,256,16,64]{1,3,2,0:T(8,128)}, f32[4,256,16]{1,0,2:T(4,12...) while((s32[]{:T(128)}, f32[16,128,64]{1,2,0:T(8,128)}, ...), condition=%wide.region_4.6_spmd.clone, body=%wide.region_1.5_spmd.clone.sunk | while | flops 1718448640 | bytes 14212321 | solution.py:135
  572.1 8.4 fusion.220
  580.6 18.5 multiply_reduce_fusion.21
  611.0 10.1 fusion.208
  621.2 11.0 fusion.237
  638.3 19.9 multiply_reduce_fusion.8
  693.6 50.4 %while.156 = (s32[]{:T(128)}, f32[16,128,64]{1,2,0:T(8,128)}, f32[4,16,128,64]{2,3,1,0:T(8,128)}, s32[4,256]{1,0:T(4,128)}, s32[4]{0:T(128)}, /*index=5*/f32[4,2...) while((s32[]{:T(128)}, f32[16,128,64]{1,2,0:T(8,128)}, ...), condition=%wide.region_21.23_spmd.clone, body=%wide.region_18.22_spmd.clone.sunk | while | flops 403988800 | bytes 3478218 | solution.py:101
  756.6 372.4 %while.157 = (s32[]{:T(128)}, f32[16]{0:T(128)}, f32[16,128,64]{1,2,0:T(8,128)}, f32[4,256,16,64]{1,3,2,0:T(8,128)}, f32[4,256,16]{2,1,0:T(8,128)}, /*index=5*/f...) while((s32[]{:T(128)}, f32[16]{0:T(128)}, ...), condition=%wide.region_36.38_spmd.clone, body=%wide.region_22.37_spmd.clone.sunk | while | flops 3951219200 | bytes 36960852 | solution.py:101
  799.5 9.0 fusion.535
  892.6 9.0 fusion.535
  986.3 9.0 fusion.535
  1079.4 9.0 fusion.535
  1148.8 15.2 multiply_reduce_fusion.16
  1186.3 50.8 %while.158 = (s32[]{:T(128)}, f32[16,128,64]{1,2,0:T(8,128)}, f32[4,16,128,64]{2,3,1,0:T(8,128)}, s32[4,256]{1,0:T(4,128)}, s32[4]{0:T(128)}, /*index=5*/f32[4,2...) while((s32[]{:T(128)}, f32[16,128,64]{1,2,0:T(8,128)}, ...), condition=%wide.region_46.48_spmd.clone, body=%wide.region_43.47_spmd.clone.sunk | while | flops 403988800 | bytes 3478218 | solution.py:101
  1249.8 371.6 %while.159 = (s32[]{:T(128)}, f32[16]{0:T(128)}, f32[16,128,64]{1,2,0:T(8,128)}, f32[4,256,16,64]{1,3,2,0:T(8,128)}, f32[4,256,16]{2,1,0:T(8,128)}, /*index=5*/f...) while((s32[]{:T(128)}, f32[16]{0:T(128)}, ...), condition=%wide.region_61.63_spmd.clone, body=%wide.region_47.62_spmd.clone.sunk | while | flops 3951219200 | bytes 36960852 | solution.py:101
  1292.6 9.0 fusion.563
  1385.4 9.0 fusion.563
  1478.9 9.0 fusion.563
  1571.8 9.0 fusion.563
  1637.2 16.0 multiply_reduce_fusion.12
  1664.2 10.9 fusion.216
  1676.3 9.2 broadcast_multiply_fusion.2
  1693.6 11.0 fusion.242
  1712.7 10.2 fusion.245
  1723.6 12.1 fusion.214
  1736.3 11.5 fusion.212
  1752.9 27.2 all-reduce.52
  1780.0 272.6 %all-reduce.51.cloned.1.call-done = (f32[1024,2048]{1,0:T(8,128)}, f32[1,1024,256]{1,2,0:T(8,128)}, f32[1024,2048]{1,0:T(8,128)}, f32[1,1024,256]{1,2,0:T(8,128)}) async-done(((f32[1024,2048]{1,0:T(8,128)}, f32[1,1024,256]{1,2,0:T(8,128)}, f32[1024,2048]{1,0:T(8,128)}, f32[1,1024,256]{1,2,0:T(8,128)}), (f32[1024,2048]{1,0:T(8,128)}, f32[1,1024,256]{1,2,0:T(8,128)}, f32[1024,2048]{1,0:T(8,128)}, ...) | async-done | bytes 18874384 | tf_op jit(solution)/shard_map/psum | solution.py:352
  2067.2 12.8 slice_convert_fusion.1
  2080.0 47.2 %reduce-scatter.5.cloned.1.call-done = f32[256,2048]{1,0:T(8,128)} async-done(((f32[1024,2048]{1,0:T(8,128)}), f32[256,2048]{1,0:T(8,128)}) %reduce-scatter.5.cloned.1.call-update) | async-done | bytes 2097168 | tf_op jit(solution)/shard_map/reduce_scatter | solution.py:313
  2134.0 12.2 fusion.326
  2146.2 55.7 %reduce-scatter.7.cloned.1.call-done = f32[256,2048]{1,0:T(8,128)} async-done(((f32[1024,2048]{1,0:T(8,128)}), f32[256,2048]{1,0:T(8,128)}) %reduce-scatter.7.cloned.1.call-update) | async-done | bytes 2097168 | tf_op jit(solution)/shard_map/reduce_scatter | solution.py:313
  2205.5 10.4 add_bitcast_fusion.5
  2223.7 9.8 fusion.250
  2233.5 9.5 add_bitcast_fusion.4
  2278.0 16.2 pad_maximum_fusion
  2294.2 23.5 gather_fusion.1
  2327.9 14.8 fusion.203
  2342.9 38.0 %psum.87 = f32[1,7024]{1,0:T(1,128)S(1)} all-reduce(f32[1,7024]{1,0:T(1,128)S(1)} %broadcast_in_dim.763), channel_id=1, replica_groups=mesh['dp'=8,'tensor'=4] {'dp'}, use_global_device_ids=true, to_apply=%region_99.101 | all-reduce | flops 7024 | bytes 56192 | tf_op jit(solution)/shard_map/psum | solution.py:376
  2380.9 13.1 fusion.192
  2403.7 8.8 pad_maximum_fusion.2
  2412.6 345.3 %reduce-scatter.9.cloned.1.call-done = f32[48,128,128]{2,1,0:T(8,128)} async-done(((f32[384,128,128]{2,1,0:T(8,128)}), f32[48,128,128]{2,1,0:T(8,128)}) %reduce-scatter.9.cloned.1.call-update) | async-done | bytes 3145744 | tf_op jit(solution)/shard_map/reduce_scatter | solution.py:394
  (1492 shorter events, 1377.8 us)
Async XLA Ops:
  7.2 2750.7 %copy-start = (f32[1,48,128,128]{3,2,1,0:T(8,128)S(1)}, f32[1,48,128,128]{3,2,1,0:T(8,128)}, u32[]{:S(2)}) copy-start(f32[1,48,128,128]{3,2,1,0:T(8,128)} %param.35) | copy-start | bytes 9437188
  7.2 48.4 %all-gather.8.cloned.1.call-start = ((), (), s32[]{:S(2)}) async-start(), calls=%async_computation.5 | async-start | bytes 1474560 | tf_op jit(solution)/shard_map/all_gather | solution.py:239
  9.1 224.4 %all-gather.6.cloned.1.call-start = ((), (), s32[]{:S(2)}) async-start(), calls=%async_computation.4 | async-start | bytes 14155776 | tf_op jit(solution)/shard_map/all_gather | solution.py:238
  12.5 2040.2 %all-reduce.51.cloned.1.call-start = ((), (), s32[]{:S(2)}) async-start(), calls=%async_computation.12 | async-start | bytes 37748736 | tf_op jit(solution)/shard_map/psum | solution.py:352
  18.9 561.7 %copy-start.109 = (f32[1,4,4,128]{3,1,2,0:T(4,128)}, f32[1,4,4,128]{3,1,2,0:T(4,128)S(1)}, u32[]{:S(2)}) copy-start(f32[1,4,4,128]{3,1,2,0:T(4,128)S(1)} %copy.649) | copy-start | bytes 24580
  19.1 45.7 %copy-start.146 = (f32[256]{0:T(256)}, f32[256]{0:T(256)S(1)}, u32[]{:S(2)}) copy-start(f32[256]{0:T(256)S(1)} %mul.1601) | copy-start | bytes 3076
  19.2 45.6 %copy-start.148 = (f32[256]{0:T(256)}, f32[256]{0:T(256)S(1)}, u32[]{:S(2)}) copy-start(f32[256]{0:T(256)S(1)} %mul.1604) | copy-start | bytes 3076
  19.3 45.5 %copy-start.150 = (f32[256]{0:T(256)}, f32[256]{0:T(256)S(1)}, u32[]{:S(2)}) copy-start(f32[256]{0:T(256)S(1)} %mul.1607) | copy-start | bytes 3076
  19.4 45.4 %copy-start.152 = (f32[256]{0:T(256)}, f32[256]{0:T(256)S(1)}, u32[]{:S(2)}) copy-start(f32[256]{0:T(256)S(1)} %mul.1610) | copy-start | bytes 3076
  19.6 54.6 %copy-start.156 = (f32[16]{0:T(128)}, f32[16]{0:T(128)S(1)}, u32[]{:S(2)}) copy-start(f32[16]{0:T(128)S(1)} %get-tuple-element.2319) | copy-start | bytes 196
  21.1 254.2 %copy-start.80 = (pred[1024]{0:T(1024)(128)(4,1)}, pred[1024]{0:T(1024)(128)(4,1)S(1)}, u32[]{:S(2)}) copy-start(pred[1024]{0:T(1024)(128)(4,1)S(1)} %get-tuple-element.2055) | copy-start | bytes 3076
  21.1 254.2 %copy-start.83 = (pred[1024]{0:T(1024)(128)(4,1)}, pred[1024]{0:T(1024)(128)(4,1)S(1)}, u32[]{:S(2)}) copy-start(pred[1024]{0:T(1024)(128)(4,1)S(1)} %get-tuple-element.2056) | copy-start | bytes 3076
  21.1 254.2 %copy-start.86 = (pred[1024]{0:T(1024)(128)(4,1)}, pred[1024]{0:T(1024)(128)(4,1)S(1)}, u32[]{:S(2)}) copy-start(pred[1024]{0:T(1024)(128)(4,1)S(1)} %get-tuple-element.2057) | copy-start | bytes 3076
  21.4 253.8 %copy-start.89 = (pred[1024]{0:T(1024)(128)(4,1)}, pred[1024]{0:T(1024)(128)(4,1)S(1)}, u32[]{:S(2)}) copy-start(pred[1024]{0:T(1024)(128)(4,1)S(1)} %get-tuple-element.2058) | copy-start | bytes 3076
  21.5 253.9 %copy-start.91 = (pred[1024]{0:T(1024)(128)(4,1)}, pred[1024]{0:T(1024)(128)(4,1)S(1)}, u32[]{:S(2)}) copy-start(pred[1024]{0:T(1024)(128)(4,1)S(1)} %get-tuple-element.2059) | copy-start | bytes 3076
  21.5 253.9 %copy-start.94 = (pred[1024]{0:T(1024)(128)(4,1)}, pred[1024]{0:T(1024)(128)(4,1)S(1)}, u32[]{:S(2)}) copy-start(pred[1024]{0:T(1024)(128)(4,1)S(1)} %get-tuple-element.2060) | copy-start | bytes 3076
  27.0 543.2 %copy-start.141 = (f32[1024]{0:T(1024)}, f32[1024]{0:T(1024)S(1)}, u32[]{:S(2)}) copy-start(f32[1024]{0:T(1024)S(1)} %get-tuple-element.2340) | copy-start | bytes 12292
  27.6 553.0 %copy-start.144 = (f32[1024]{0:T(1024)}, f32[1024]{0:T(1024)S(1)}, u32[]{:S(2)}) copy-start(f32[1024]{0:T(1024)S(1)} %get-tuple-element.2338) | copy-start | bytes 12292
  28.2 247.1 %copy-start.97 = (f32[1,1024]{1,0:T(1,128)}, f32[1,1024]{1,0:T(1,128)S(1)}, u32[]{:S(2)}) copy-start(f32[1,1024]{1,0:T(1,128)S(1)} %get-tuple-element.2313) | copy-start | bytes 12292
  28.2 247.1 %copy-start.99 = (f32[1,1024]{1,0:T(1,128)}, f32[1,1024]{1,0:T(1,128)S(1)}, u32[]{:S(2)}) copy-start(f32[1,1024]{1,0:T(1,128)S(1)} %get-tuple-element.2314) | copy-start | bytes 12292
  28.2 247.1 %copy-start.101 = (f32[1,1024]{1,0:T(1,128)}, f32[1,1024]{1,0:T(1,128)S(1)}, u32[]{:S(2)}) copy-start(f32[1,1024]{1,0:T(1,128)S(1)} %get-tuple-element.2315) | copy-start | bytes 12292
  28.2 247.1 %copy-start.103 = (f32[1,1024]{1,0:T(1,128)}, f32[1,1024]{1,0:T(1,128)S(1)}, u32[]{:S(2)}) copy-start(f32[1,1024]{1,0:T(1,128)S(1)} %get-tuple-element.2316) | copy-start | bytes 12292
  75.3 174.3 %copy-start.57 = (f32[1024,16]{0,1:T(8,128)}, f32[1024,16]{0,1:T(8,128)S(1)}, u32[]{:S(2)}) copy-start(f32[1024,16]{0,1:T(8,128)S(1)} %get-tuple-element.1230) | copy-start | bytes 196612
  75.3 174.3 %copy-start.59 = (f32[1024,16]{0,1:T(8,128)}, f32[1024,16]{0,1:T(8,128)S(1)}, u32[]{:S(2)}) copy-start(f32[1024,16]{0,1:T(8,128)S(1)} %get-tuple-element.1218) | copy-start | bytes 196612
  605.8 32.4 %copy-start.124 = (f32[1024]{0:T(1024)}, f32[1024]{0:T(1024)S(1)}, u32[]{:S(2)}) copy-start(f32[1024]{0:T(1024)S(1)} %get-tuple-element.2342) | copy-start | bytes 12292
  605.9 32.4 %copy-start.127 = (f32[1024]{0:T(1024)}, f32[1024]{0:T(1024)S(1)}, u32[]{:S(2)}) copy-start(f32[1024]{0:T(1024)S(1)} %get-tuple-element.2344) | copy-start | bytes 12292
  763.8 23.8 copy-start.13
  821.3 17.9 copy-start.66
  855.9 24.8 copy-start.13
  914.4 17.9 copy-start.66
  948.9 24.8 copy-start.13
  1008.1 17.9 copy-start.66
  1042.7 24.8 copy-start.13
  1101.2 17.9 copy-start.66
  1257.1 23.7 copy-start.14
  1348.9 24.7 copy-start.14
  1441.7 24.7 copy-start.14
  1500.7 17.9 copy-start.69
  1535.2 24.7 copy-start.14
  1593.6 17.9 copy-start.69
  1722.9 404.3 %reduce-scatter.5.cloned.1.call-start = ((), (), s32[]{:S(2)}) async-start(), calls=%async_computation.6 | async-start | bytes 10485760 | tf_op jit(solution)/shard_map/reduce_scatter | solution.py:313
  1735.7 466.3 %reduce-scatter.7.cloned.1.call-start = ((), (), s32[]{:S(2)}) async-start(), calls=%async_computation.8 | async-start | bytes 10485760 | tf_op jit(solution)/shard_map/reduce_scatter | solution.py:313
  1747.9 653.6 %reduce-scatter.11.cloned.1.call-start = ((), (), s32[]{:S(2)}) async-start(), calls=%async_computation.11 | async-start | bytes 2949120 | tf_op jit(solution)/shard_map/reduce_scatter | solution.py:395
  2067.2 336.6 %all-gather.10.cloned.1.call-start = ((), (), s32[]{:S(2)}) async-start(), calls=%async_computation.7 | async-start | bytes 5242880 | tf_op jit(solution)/shard_map/all_gather | solution.py:321
  2130.7 273.1 %all-gather.12.cloned.1.call-start = ((), (), s32[]{:S(2)}) async-start(), calls=%async_computation.9 | async-start | bytes 5242880 | tf_op jit(solution)/shard_map/all_gather | solution.py:321
  2205.5 552.4 %reduce-scatter.9.cloned.1.call-start = ((), (), s32[]{:S(2)}) async-start(), calls=%async_computation.10 | async-start | bytes 28311552 | tf_op jit(solution)/shard_map/reduce_scatter | solution.py:394
  2327.8 53.0 %copy-start.140 = (f32[1024]{0:T(1024)S(1)}, f32[1024]{0:T(1024)}, u32[]{:S(2)}) copy-start(f32[1024]{0:T(1024)} %get-tuple-element.2339) | copy-start | bytes 12292
  2327.9 53.0 %copy-start.143 = (f32[1024]{0:T(1024)S(1)}, f32[1024]{0:T(1024)}, u32[]{:S(2)}) copy-start(f32[1024]{0:T(1024)} %get-tuple-element.2337) | copy-start | bytes 12292
  (223 other events, 1512.3 us)
Sparse Core Ops, SparseCore 0:
  10.7 44.9 all-gather.7
  58.4 175.0 all-gather.5
  1723.0 329.5 all-reduce.50
  2055.3 71.8 reduce-scatter.4
  2130.2 71.7 reduce-scatter.6
  2206.3 70.8 reduce-scatter.10
  2278.8 33.4 all-gather.9
  2314.6 34.4 all-gather.11
  2354.1 403.7 reduce-scatter.8
where the time goes:
time: 2820 us; the launch traced here: 2790 us
  waiting for transfers between devices  899 us (32%)
  matrix products  661 us (23%)
  local copies, waits for them, and re-layouts  637 us (23%)
  other arithmetic  461 us (16%)
  blocking collectives  84.2 us (3%)
  loops' own time  34 us (1%)
    reduce_scatter x1, waiting for transfers between devices, on_device(): lax.psum_scatter(in_slots, 'dp', scatter_dimension=0, tiled=True)  345 us
    psum x1, waiting for transfers between devices, on_device(): d_normed = lax.psum(local_sum, 'tensor') + contract_cols(d_side, side_copy)  273 us
    dot_general x24, matrix products, advance(): output = jnp.einsum('tsh,shp->thp', weights, span_x, precision=HIGH)  184 us
    all_gather x1, waiting for transfers between devices, on_device(): lax.all_gather(matrix_tiles[0].astype(jnp.bfloat16), 'dp', axis=0, tiled=...  151 us
    reduce_scatter x2, waiting for transfers between devices, on_device(): lax.psum_scatter(jnp.dot(hidden, w_output, preferred_element_type=jnp.flo...  103 us
    dot_general x32, matrix products, advance(): jnp.einsum('sn,shp->hnp', span_b, span_x * (tail_decay * span_dt)[:, :, N...  103 us
    another operation x112, other arithmetic  89.7 us
    another operation x118, local copies, waits for them, and re-layouts  87 us
  transfers between devices with their start and end apart: 9, of which 6 were waited for; matrix products, arithmetic and copies ran while one was open for 10% of the time, Pallas kernels for 0%

commit v1 on v0

v1 whole, which is shorter than its diff:
```python
import functools

import jax
import jax.numpy as jnp
from jax import lax
from jax.experimental import pallas as pl
from jax.experimental.pallas import tpu as pltpu
from jax.sharding import PartitionSpec as P

D = 2048
HEADS = 64
NS = 128
CONV = 4
TILE = 128
STEP = 10
DI = 4096
SIDE = 320
BLK = 128
LANES = 128
MID_ROWS = 512
TILES_STEP = 6
COPY_ROWS = 16
SLACK = 2
ONE_PASS = True

EPS = 1e-05
HIGH = lax.Precision.HIGHEST
STAT_DECAY = 0.5
LR_MAT = 0.25
LR_SIDE = 0.02
LR_VEC = 0.25
BETA_ONE = 0.9
BETA_TWO = 0.95
ADAM_EPS = 1e-08
DECAY_WD = 0.1
LOG2E = 1.4426950408889634
FAR = -1e30
VMEM_LIMIT = 60 * 1024 * 1024

F32 = jnp.float32
BF16 = jnp.bfloat16

NN = (((1,), (0,)), ((), ()))
NT = (((1,), (1,)), ((), ()))


def segment_bounds(di_local, heads_local, model_local, bc_local, tap_count):
    widths = [
        tap_count * di_local,
        di_local,
        di_local,
        heads_local,
        heads_local,
        heads_local,
        model_local,
        tap_count * bc_local,
        bc_local,
    ]
    bounds = [0]
    for item in widths:
        bounds.append(bounds[-1] + item)
    return bounds


def adam_update(weight, moment, second, gradient, learn_rate):
    moment_new = BETA_ONE * moment + (1.0 - BETA_ONE) * gradient
    second_new = BETA_TWO * second + (1.0 - BETA_TWO) * gradient * gradient
    corrected = moment_new / (1.0 - BETA_ONE**STEP)
    scaled = jnp.sqrt(second_new / (1.0 - BETA_TWO**STEP)) + ADAM_EPS
    return (moment_new, second_new, weight - learn_rate * (corrected / scaled + DECAY_WD * weight))


def contract_rows(left, right):
    return lax.dot_general(left, right, (((0,), (0,)), ((), ())), preferred_element_type=F32)


def contract_cols(left, right):
    return lax.dot_general(left, right, NT, preferred_element_type=F32)


def swap(value, axis, bit):
    size = lax.axis_size(axis)
    return lax.ppermute(value, axis, [(i, i ^ bit) for i in range(size)])


def sum_over(value, axis):
    bit = 1
    while bit < lax.axis_size(axis):
        value = value + swap(value, axis, bit)
        bit *= 2
    return value


class SharedSums:
    def __init__(self, owned, shared):
        self.owned, self.shared = owned, shared
        self.bit = lax.axis_size("dp") // 2

    def exchange(self):
        if self.bit == 0:
            return
        upper = (lax.axis_index("dp") // self.bit) % 2
        pairs = self.owned.reshape(2, -1, self.owned.shape[1])
        sent = lax.dynamic_index_in_dim(pairs, 1 - upper, 0, keepdims=False)
        kept = lax.dynamic_index_in_dim(pairs, upper, 0, keepdims=False)
        arrived = swap(
            jnp.concatenate([sent.reshape(-1), self.shared])[None], "dp", self.bit
        )[0]
        self.owned = kept + arrived[: kept.size].reshape(kept.shape)
        self.shared = self.shared + arrived[kept.size :]
        self.bit //= 2

    def exchange_rest(self):
        while self.bit > 0:
            self.exchange()


class OwnerSum:
    def __init__(self, grads, groups):
        owners = lax.axis_size("dp")
        self.grads = grads.reshape(owners, -1, TILE)
        self.lined = owners == 8
        if not self.lined:
            return
        me = lax.axis_index("dp")
        x, z = me % 2, me // 2
        self.low = z < 2
        order = [jnp.where(self.low, z + 3 - k, z + 1 + k) % 4 for k in range(4)]
        self.own = [self.part(seg, x) for seg in order]
        self.found = [(i, group.index(k)) for k in range(4) for i, group in enumerate(groups) if k in group]
        self.groups = [
            swap(jnp.concatenate([self.part(order[k], 1 - x) for k in group]), "dp", 1)
            for group in groups
        ]

    def part(self, seg, x):
        return lax.dynamic_index_in_dim(self.grads, seg * 2 + x, 0, keepdims=False)

    def pair_sum(self, k):
        rows = self.own[k].shape[0]
        group, place = self.found[k]
        arrived = self.groups[group][place * rows : (place + 1) * rows]
        return self.own[k].astype(F32) + arrived.astype(F32)

    def hop(self, value, moves):
        pairs = [(2 * a + x, 2 * b + x) for a, b in moves for x in (0, 1)]
        return lax.ppermute(value.astype(BF16), "dp", pairs)


    def first(self, other):
        if self.lined:
            self.groups[0], other = tied(self.groups[0], other)
            self.ahead = self.hop(self.pair_sum(0), [(0, 1), (3, 2)])
        return other

    def second(self, other):
        if self.lined:
            needed = self.found[1][0]
            self.ahead, self.groups[needed], other = tied(self.ahead, self.groups[needed], other)
            value = self.pair_sum(1) + self.ahead.astype(F32)
            self.up = self.hop(value, [(0, 1), (1, 2)])
            self.down = self.hop(value, [(3, 2), (2, 1)])
        return other

    def third(self, other):
        if self.lined:
            self.up, self.down, self.groups[-1], other = tied(
                self.up, self.down, self.groups[-1], other
            )
            near, far = self.pair_sum(2), self.pair_sum(0)
            up = jnp.where(self.low, near, far) + self.up.astype(F32)
            down = jnp.where(self.low, far, near) + self.down.astype(F32)
            self.up = self.hop(up, [(0, 1), (1, 2), (2, 3)])
            self.down = self.hop(down, [(3, 2), (2, 1), (1, 0)])
        return other

    def total(self, other):
        if not self.lined:
            flat = self.grads.reshape(-1, TILE)
            return lax.psum_scatter(flat, "dp", scatter_dimension=0, tiled=True).astype(F32), other
        self.up, self.down, other = tied(self.up, self.down, other)
        return self.pair_sum(3) + (self.up.astype(F32) + self.down.astype(F32)), other


def tied(*values):
    return lax.optimization_barrier(values)


def halves(value):
    high = value.astype(BF16)
    return high, (value - high.astype(F32)).astype(BF16)


def dot(left, right, dims=NN):
    return lax.dot_general(left, right, dims, preferred_element_type=F32)


def product(left, right, dims=NN):
    return dot(left.astype(BF16), right.astype(BF16), dims)


def by_halves(left, right):
    both = dot(left.astype(BF16), jnp.concatenate(halves(right), axis=1))
    return both[:, : right.shape[1]] + both[:, right.shape[1] :]


def careful(left, right, dims=NN):
    left_high, left_low = halves(left)
    right_high, right_low = halves(right)
    return dot(
        jnp.concatenate([left_high, left_low, left_high], axis=1),
        jnp.concatenate([right_high, right_high, right_low], axis=dims[0][1][0]),
        dims,
    )


def summed(mask, value):
    high, rest = halves(value)
    low = (value - high.astype(F32) - rest.astype(F32)).astype(BF16)
    mask = mask.astype(BF16)
    return dot(jnp.concatenate([mask] * 3, axis=1), jnp.concatenate([high, rest, low], axis=0))


def sigmoid(value):
    return 0.5 * jnp.tanh(0.5 * value) + 0.5


def softplus(value):
    return jnp.maximum(value, 0.0) + jnp.log1p(jnp.exp(-jnp.abs(value)))


def taps_of(padded, lanes, masks):
    rows = masks[0].shape[0]
    shifted = [padded[8 : 8 + rows, lanes]]
    for shift in range(1, CONV):
        shifted.append(padded[8 - shift : 8 - shift + rows, lanes] * masks[shift - 1])
    return shifted


def convolve(shifted, params, lanes):
    total = params[CONV : CONV + 1, lanes]
    for shift in range(CONV):
        total = total + params[CONV - 1 - shift : CONV - shift, lanes] * shifted[shift]
    return total


def wide(column, shape):
    return jnp.broadcast_to(column, shape)


def ssd_forward_kernel(
    rest_ref, prev_ref, start_ref, par_ref, bcpar_ref, hp_ref,
    ssd_ref, states_ref, xs, ss, state, tails, keeps,
):
    width = ssd_ref.shape[1]
    pairs = width // LANES
    shape = (BLK, LANES)
    base_i = pl.program_id(1) * BLK
    base = base_i.astype(F32)

    @pl.when(pl.program_id(1) == 0)
    def _():
        state[...] = jnp.zeros_like(state)

    xs[0:8, :] = prev_ref[:, 0:width]
    xs[8 : 8 + BLK, :] = rest_ref[:, 0:width]
    ss[0:8, :] = prev_ref[:, width : width + 2 * NS]
    ss[8 : 8 + BLK, :] = rest_ref[:, width : width + 2 * NS]
    start = start_ref[...]
    row = (lax.broadcasted_iota(jnp.int32, shape, 0) + base_i).astype(F32)
    col = (lax.broadcasted_iota(jnp.int32, shape, 1) + base_i).astype(F32)
    lane = lax.broadcasted_iota(jnp.int32, shape, 1)
    low = lane < LANES // 2
    pos = row - start
    masks = [jnp.where(pos >= float(k), 1.0, 0.0) for k in range(1, CONV)]
    bias = jnp.where((col >= start) & (col <= row), 0.0, FAR)
    carried = start < base
    last_start = start_ref[BLK - 1 : BLK, :]
    tail_ok = row >= last_start
    keep_ok = last_start < base

    acts = []
    for part in range(2):
        lanes = slice(part * NS, (part + 1) * NS)
        raw = convolve(taps_of(ss, lanes, masks), bcpar_ref, lanes)
        acts.append(raw * sigmoid(raw))
    b_act, c_act = acts
    first_step = width + 2 * NS
    steps = softplus(rest_ref[:, first_step : first_step + LANES] + hp_ref[0:1, :])
    lower = jnp.where(col <= row, 1.0, 0.0)
    cum = summed(lower, steps * hp_ref[1:2, :])
    cum_t = cum.T
    scores = careful(c_act, b_act, NT)
    states_ref[0] = state[...]
    from_state = product(c_act, state[...])
    for pair in range(pairs):
        lanes = slice(pair * LANES, (pair + 1) * LANES)
        raw = convolve(taps_of(xs, lanes, masks), par_ref, lanes)
        act = raw * sigmoid(raw)
        col_a = wide(cum[:, 2 * pair : 2 * pair + 1], shape)
        col_b = wide(cum[:, 2 * pair + 1 : 2 * pair + 2], shape)
        both = jnp.where(low, col_a, col_b)
        step_both = jnp.where(
            low,
            wide(steps[:, 2 * pair : 2 * pair + 1], shape),
            wide(steps[:, 2 * pair + 1 : 2 * pair + 2], shape),
        )
        scaled = act * step_both
        weight_a = scores * jnp.exp2(col_a - cum_t[2 * pair : 2 * pair + 1, :] + bias)
        weight_b = scores * jnp.exp2(col_b - cum_t[2 * pair + 1 : 2 * pair + 2, :] + bias)
        inner = by_halves(
            jnp.concatenate([weight_a, weight_b], axis=1),
            jnp.concatenate([jnp.where(low, scaled, 0.0), jnp.where(low, 0.0, scaled)], axis=0),
        )
        carry = jnp.where(carried, jnp.exp2(both), 0.0)
        ssd_ref[:, lanes] = inner + carry * from_state[:, lanes] + par_ref[5:6, lanes] * act
        last = both[BLK - 1 : BLK, :]
        tails[:, lanes] = scaled * jnp.where(tail_ok, jnp.exp2(last - both), 0.0)
        keeps[0:1, lanes] = jnp.where(keep_ok, jnp.exp2(last), 0.0)
    state[...] = keeps[0:1, :] * state[...] + product(b_act.T, tails[...])


def ssd_backward_kernel(
    *refs,
):
    held = max(len(refs) - 27, 0)
    ssd_backward_body(*refs[held:])


def ssd_backward_body(
    place_ref, rest_ref, prev_ref, dy_ref, states_ref, start_ref, end_ref, srow_ref,
    par_ref, bcpar_ref, hp_ref, pick_ref,
    drest_ref, dside_ref, gx_ref, gbc_ref, gh_ref,
    xs, ss, dxs, dbs, dstate, tails, carries, terms, rows_in, keeps,
):
    width = dy_ref.shape[1]
    pairs = width // LANES
    shape = (BLK, LANES)
    blocks = pl.num_programs(0)
    base_i = (blocks - 1 - pl.program_id(0)) * BLK
    base = base_i.astype(F32)

    @pl.when(pl.program_id(0) == 0)
    def _():
        gx_ref[...] = jnp.zeros_like(gx_ref)
        gbc_ref[...] = jnp.zeros_like(gbc_ref)
        gh_ref[...] = jnp.zeros_like(gh_ref)
        rows_in[...] = jnp.zeros_like(rows_in)
        dxs[0:8, :] = jnp.zeros((8, width), F32)
        dbs[0:8, :] = jnp.zeros((8, 2 * NS), F32)
        dstate[...] = jnp.zeros_like(dstate)

    dxs[BLK : BLK + 8, :] = dxs[0:8, :]
    dbs[BLK : BLK + 8, :] = dbs[0:8, :]
    xs[0:8, :] = prev_ref[:, 0:width]
    xs[8 : 8 + BLK, :] = rest_ref[:, 0:width]
    ss[0:8, :] = prev_ref[:, width : width + 2 * NS]
    ss[8 : 8 + BLK, :] = rest_ref[:, width : width + 2 * NS]
    start = start_ref[...]
    row_i = lax.broadcasted_iota(jnp.int32, shape, 0)
    lane = lax.broadcasted_iota(jnp.int32, shape, 1)
    row = (row_i + base_i).astype(F32)
    col = (lane + base_i).astype(F32)
    low = lane < LANES // 2
    pos = row - start
    left = end_ref[...] - row
    masks = [jnp.where(pos >= float(k), 1.0, 0.0) for k in range(1, CONV)]
    after = [jnp.where(left > float(k), 1.0, 0.0) for k in range(1, CONV)]
    bias_t = jnp.where((row >= srow_ref[...]) & (row <= col), 0.0, FAR)
    carried = start < base
    last_start = start_ref[BLK - 1 : BLK, :]
    tail_ok = row >= last_start
    keep_ok = last_start < base

    acts, slopes, bc_taps = [], [], []
    for part in range(2):
        lanes = slice(part * NS, (part + 1) * NS)
        shifted = taps_of(ss, lanes, masks)
        raw = convolve(shifted, bcpar_ref, lanes)
        sig = sigmoid(raw)
        acts.append(raw * sig)
        slopes.append(sig * (1.0 + raw * (1.0 - sig)))
        bc_taps.append(shifted)
    b_act, c_act = acts
    first_step = width + 2 * NS
    raw_steps = rest_ref[:, first_step : first_step + LANES] + hp_ref[0:1, :]
    steps = softplus(raw_steps)
    lower = jnp.where(col <= row, 1.0, 0.0)
    upper = jnp.where(col >= row, 1.0, 0.0)
    cum = summed(lower, steps * hp_ref[1:2, :])
    cum_t = cum.T
    scores_t = careful(b_act, c_act, NT)
    old = states_ref[0]
    from_state = product(c_act, old)
    from_next = product(b_act, dstate[...])
    d_scores = jnp.zeros(shape, F32)
    direct = jnp.zeros(shape, F32)

    def add_rows(ref, first, lanes, value):
        ref[first : first + 8, lanes] += jnp.sum(value.reshape(BLK // 8, 8, value.shape[1]), axis=0)

    for pair in range(pairs):
        lanes = slice(pair * LANES, (pair + 1) * LANES)
        shifted = taps_of(xs, lanes, masks)
        raw = convolve(shifted, par_ref, lanes)
        sig = sigmoid(raw)
        act = raw * sig
        dy = dy_ref[:, lanes]
        cols = [wide(cum[:, h : h + 1], shape) for h in (2 * pair, 2 * pair + 1)]
        step_cols = [wide(steps[:, h : h + 1], shape) for h in (2 * pair, 2 * pair + 1)]
        both = jnp.where(low, cols[0], cols[1])
        step_both = jnp.where(low, step_cols[0], step_cols[1])
        parts = [jnp.where(low, act, 0.0), jnp.where(low, 0.0, act)]
        dy_high, dy_low = halves(dy)
        dy_wide = jnp.concatenate([dy_high, dy_high, dy_low], axis=1)
        high, rest = halves(jnp.concatenate(parts, axis=0))
        inners = dot(jnp.concatenate([high, rest, high], axis=1), dy_wide, NT)
        weights = []
        for which in range(2):
            head = 2 * pair + which
            decay = jnp.exp2(cum_t[head : head + 1, :] - cols[which] + bias_t)
            inner = inners[which * BLK : (which + 1) * BLK, :]
            weight = decay * scores_t
            weights.append(weight)
            d_scores = d_scores + decay * inner * step_cols[which]
            pulled = weight * inner
            direct = jnp.where(lane == head, jnp.sum(pulled, axis=1, keepdims=True), direct)
            rows_in[head : head + 1, :] = jnp.sum(pulled * step_cols[which], axis=0, keepdims=True)
        d_intra = by_halves(
            jnp.concatenate(weights, axis=1),
            jnp.concatenate([jnp.where(low, dy, 0.0), jnp.where(low, 0.0, dy)], axis=0),
        )
        last = both[BLK - 1 : BLK, :]
        tail = jnp.where(tail_ok, jnp.exp2(last - both), 0.0)
        d_tail = tail * from_next[:, lanes]
        terms[0:BLK, lanes] = act * d_tail
        tails[:, lanes] = act * step_both * tail
        carry = dy * jnp.where(carried, jnp.exp2(both), 0.0)
        carries[:, lanes] = carry
        terms[BLK : 2 * BLK, lanes] = carry * from_state[:, lanes]
        keeps[0:1, lanes] = jnp.where(keep_ok, jnp.exp2(last), 0.0)
        d_act = step_both * (d_intra + d_tail) + par_ref[5:6, lanes] * dy
        d_conv = d_act * (sig * (1.0 + raw * (1.0 - sig)))
        dxs[0:BLK, lanes] = d_conv
        for shift in range(CONV):
            add_rows(gx_ref, 8 * (CONV - 1 - shift), lanes, d_conv * shifted[shift])
        add_rows(gx_ref, 8 * CONV, lanes, d_conv)
        add_rows(gx_ref, 8 * (CONV + 1), lanes, dy * act)
        d_in = par_ref[CONV - 1 : CONV, lanes] * d_conv
        for shift in range(1, CONV):
            d_in = d_in + par_ref[CONV - 1 - shift : CONV - shift, lanes] * (
                after[shift - 1] * dxs[shift : shift + BLK, lanes]
            )
        drest_ref[:, lanes] = d_in.astype(BF16)

    stay = keeps[0:1, :] * jnp.sum((old * dstate[...]).reshape(NS // 8, 8, width), axis=0)
    terms[2 * BLK : 2 * BLK + 8, :] = stay
    by_head = dot(terms[...].astype(BF16), pick_ref[...])
    at_heads = by_head[0:BLK, :]
    stay_heads = jnp.sum(by_head[2 * BLK : 2 * BLK + 8, :], axis=0, keepdims=True)
    direct = direct + at_heads
    d_cum = rows_in[...].T + by_head[BLK : 2 * BLK, :] - steps * direct
    at_last = jnp.sum(steps * at_heads, axis=0, keepdims=True) + stay_heads
    through = summed(upper, d_cum) + at_last
    decay_rate = hp_ref[2:3, :]
    d_steps = direct + decay_rate * through
    d_raw = d_steps * sigmoid(raw_steps)
    every = slice(0, LANES)
    add_rows(gh_ref, 0, every, decay_rate * steps * through)
    add_rows(gh_ref, 8, every, d_raw)
    dside_ref[:, 2 * NS :] = pltpu.roll(d_raw, place_ref[0], 1)
    drest_ref[:, first_step : first_step + LANES] = d_raw.astype(BF16)
    drest_ref[:, first_step + LANES :] = jnp.zeros(
        (BLK, drest_ref.shape[1] - first_step - LANES), BF16
    )
    d_b = careful(d_scores, c_act) + product(tails[...], dstate[...], NT)
    d_c = careful(d_scores.T, b_act) + product(carries[...], old, NT)
    for part, value in ((0, d_b), (1, d_c)):
        lanes = slice(part * NS, (part + 1) * NS)
        d_conv = value * slopes[part]
        dbs[0:BLK, lanes] = d_conv
        for shift in range(CONV):
            add_rows(gbc_ref, 8 * (CONV - 1 - shift), lanes, d_conv * bc_taps[part][shift])
        add_rows(gbc_ref, 8 * CONV, lanes, d_conv)
        d_in = bcpar_ref[CONV - 1 : CONV, lanes] * d_conv
        for shift in range(1, CONV):
            d_in = d_in + bcpar_ref[CONV - 1 - shift : CONV - shift, lanes] * (
                after[shift - 1] * dbs[shift : shift + BLK, lanes]
            )
        dside_ref[:, lanes] = d_in
        drest_ref[:, width + part * NS : width + (part + 1) * NS] = d_in.astype(BF16)
    dstate[...] = keeps[0:1, :] * dstate[...] + product(c_act.T, carries[...])


def ssd_forward(rest, starts, par, bcpar, hp, sequences):
    rows, width = rest.shape[0], par.shape[1]
    blocks = rows // sequences // BLK
    here = lambda s, b: (s * blocks + b, 0)
    before = lambda s, b: (jnp.maximum((s * blocks + b) * (BLK // 8) - 1, 0), 0)
    fixed = lambda s, b: (0, 0)
    return pl.pallas_call(
        ssd_forward_kernel,
        grid=(sequences, blocks),
        in_specs=[
            pl.BlockSpec((BLK, rest.shape[1]), here),
            pl.BlockSpec((8, rest.shape[1]), before),
            pl.BlockSpec((BLK, LANES), here),
            pl.BlockSpec(par.shape, fixed),
            pl.BlockSpec(bcpar.shape, fixed),
            pl.BlockSpec(hp.shape, fixed),
        ],
        out_specs=[
            pl.BlockSpec((BLK, width), here),
            pl.BlockSpec((1, NS, width), lambda s, b: (s * blocks + b, 0, 0)),
        ],
        out_shape=[
            jax.ShapeDtypeStruct((rows, width), F32),
            jax.ShapeDtypeStruct((sequences * blocks, NS, width), F32),
        ],
        scratch_shapes=[
            pltpu.VMEM((BLK + 8, width), F32),
            pltpu.VMEM((BLK + 8, 2 * NS), F32),
            pltpu.VMEM((NS, width), F32),
            pltpu.VMEM((BLK, width), F32),
            pltpu.VMEM((8, width), F32),
        ],
        compiler_params=pltpu.CompilerParams(vmem_limit_bytes=VMEM_LIMIT),
        cost_estimate=pl.CostEstimate(
            flops=40 * rows * BLK * width, bytes_accessed=20 * rows * width, transcendentals=0
        ),
        name="ssd_forward",
    )(rest, rest, starts, par, bcpar, hp)


def ssd_backward(
    sequence, before_it, place, rest, d_ssd, states, starts, ends, start_row, par, bcpar, hp, pick, sequences
):
    rows, width = d_ssd.shape
    rest_width = rest.shape[1]
    blocks = rows // sequences // BLK
    at = lambda b: sequence * blocks + blocks - 1 - b
    here = lambda b: (at(b), 0)
    before = lambda b: (jnp.maximum(at(b) * (BLK // 8) - 1, 0), 0)
    fixed = lambda b: (0, 0)
    return pl.pallas_call(
        ssd_backward_kernel,
        grid=(blocks,),
        in_specs=[pl.BlockSpec(memory_space=pl.ANY)] * len(before_it)
        + [
            pl.BlockSpec(memory_space=pltpu.SMEM),
            pl.BlockSpec((BLK, rest_width), here),
            pl.BlockSpec((8, rest_width), before),
            pl.BlockSpec((BLK, width), here),
            pl.BlockSpec((1, NS, width), lambda b: (at(b), 0, 0)),
            pl.BlockSpec((BLK, LANES), here),
            pl.BlockSpec((BLK, LANES), here),
            pl.BlockSpec((1, BLK), lambda b: (0, at(b))),
            pl.BlockSpec(par.shape, fixed),
            pl.BlockSpec(bcpar.shape, fixed),
            pl.BlockSpec(hp.shape, fixed),
            pl.BlockSpec(pick.shape, fixed),
        ],
        out_specs=[
            pl.BlockSpec((BLK, rest_width), here),
            pl.BlockSpec((BLK, 2 * NS + LANES), lambda b: (blocks - 1 - b, 0)),
            pl.BlockSpec((8 * (CONV + 2), width), fixed),
            pl.BlockSpec((8 * (CONV + 1), 2 * NS), fixed),
            pl.BlockSpec((16, LANES), fixed),
        ],
        out_shape=[
            jax.ShapeDtypeStruct((rows, rest_width), BF16),
            jax.ShapeDtypeStruct((rows // sequences, 2 * NS + LANES), F32),
            jax.ShapeDtypeStruct((8 * (CONV + 2), width), F32),
            jax.ShapeDtypeStruct((8 * (CONV + 1), 2 * NS), F32),
            jax.ShapeDtypeStruct((16, LANES), F32),
        ],
        scratch_shapes=[
            pltpu.VMEM((BLK + 8, width), F32),
            pltpu.VMEM((BLK + 8, 2 * NS), F32),
            pltpu.VMEM((BLK + 8, width), F32),
            pltpu.VMEM((BLK + 8, 2 * NS), F32),
            pltpu.VMEM((NS, width), F32),
            pltpu.VMEM((BLK, width), F32),
            pltpu.VMEM((BLK, width), F32),
            pltpu.VMEM((2 * BLK + 8, width), F32),
            pltpu.VMEM((LANES, BLK), F32),
            pltpu.VMEM((8, width), F32),
        ],
        input_output_aliases={i: i for i in range(len(before_it))},
        compiler_params=pltpu.CompilerParams(vmem_limit_bytes=VMEM_LIMIT),
        cost_estimate=pl.CostEstimate(
            flops=100 * rows * BLK * width // sequences,
            bytes_accessed=4 * rows * 5 * width // sequences,
            transcendentals=0,
        ),
        name="ssd_backward",
    )(*before_it, place, rest, rest, d_ssd, states, starts, ends, start_row, par, bcpar, hp, pick)


def resident(array):
    return pl.BlockSpec(
        array.shape, lambda *i: (0,) * array.ndim, pipeline_mode=pl.Buffered(buffer_count=1)
    )


def matmul_kernel(left_ref, right_ref, out_ref):
    out_ref[...] = dot(left_ref[...], right_ref[...])


def project(normed, weights):
    rows = normed.shape[0]
    step = min(MID_ROWS, rows)
    width = weights.shape[1]
    here = lambda i: (i, 0)
    return pl.pallas_call(
        matmul_kernel,
        grid=(rows // step,),
        in_specs=[pl.BlockSpec((step, D), here), resident(weights)],
        out_specs=pl.BlockSpec((step, width), here),
        out_shape=jax.ShapeDtypeStruct((rows, width), F32),
        compiler_params=pltpu.CompilerParams(vmem_limit_bytes=VMEM_LIMIT),
        cost_estimate=pl.CostEstimate(
            flops=2 * rows * D * width,
            bytes_accessed=4 * rows * width + 2 * D * (rows + width),
            transcendentals=0,
        ),
        name="project",
    )(normed, weights)


def gate_kernel(normed_ref, cot_ref, wgate_ref, wout_ref, ssd_ref, gain_ref, gate_ref, dh_ref, sums_ref):
    gate_ref[...] = dot(normed_ref[...], wgate_ref[...])
    dh_ref[...] = dot(cot_ref[...], wout_ref[...], NT)
    rows, width = ssd_ref.shape
    for first in range(0, rows, LANES):
        at = slice(first, first + LANES)
        squares = jnp.zeros((LANES, LANES), F32)
        inners = jnp.zeros((LANES, LANES), F32)
        for piece in range(width // LANES):
            lanes = slice(piece * LANES, (piece + 1) * LANES)
            gate = gate_ref[at, lanes]
            gated = ssd_ref[at, lanes] * (gate * sigmoid(gate))
            squares = squares + gated * gated
            inners = inners + dh_ref[at, lanes] * gain_ref[0:1, lanes] * gated
        sums_ref[0:1, at] = jnp.sum(squares.T, axis=0, keepdims=True)
        sums_ref[1:2, at] = jnp.sum(inners.T, axis=0, keepdims=True)
    sums_ref[2:8, :] = jnp.zeros((6, rows), F32)


def gate_project(normed, cotangent, w_gate, w_output, ssd, gain):
    rows, width = ssd.shape
    step = min(MID_ROWS, rows)
    here = lambda i: (i, 0)
    return pl.pallas_call(
        gate_kernel,
        grid=(rows // step,),
        in_specs=[
            pl.BlockSpec((step, D), here),
            pl.BlockSpec((step, D), here),
            resident(w_gate),
            resident(w_output),
            pl.BlockSpec((step, width), here),
            pl.BlockSpec((1, width), lambda i: (0, 0)),
        ],
        out_specs=[
            pl.BlockSpec((step, width), here),
            pl.BlockSpec((step, width), here),
            pl.BlockSpec((8, step), lambda i: (0, i)),
        ],
        out_shape=[
            jax.ShapeDtypeStruct((rows, width), F32),
            jax.ShapeDtypeStruct((rows, width), F32),
            jax.ShapeDtypeStruct((8, rows), F32),
        ],
        compiler_params=pltpu.CompilerParams(vmem_limit_bytes=VMEM_LIMIT),
        cost_estimate=pl.CostEstimate(
            flops=4 * rows * D * width, bytes_accessed=16 * rows * width, transcendentals=0
        ),
        name="gate_project",
    )(normed, cotangent, w_gate, w_output, ssd, gain)


def gated_kernel(
    core_ref, ssd_ref, gate_ref, dh_ref, sums_ref, gain_ref, wout_ref,
    hidden_ref, dgate_ref, dssd_ref, gain_out, sent_ref, kept_ref,
):
    @pl.when(pl.program_id(0) == 0)
    def _():
        gain_out[...] = jnp.zeros_like(gain_out)

    width = ssd_ref.shape[1]
    rows = ssd_ref.shape[0]
    scale = lax.rsqrt(sums_ref[0:1, :] / DI + EPS)
    shift = scale * scale * scale * (sums_ref[1:2, :] / DI)
    turned = jnp.concatenate([scale] * 8 + [shift] * 8 + [jnp.zeros((LANES - 16, rows), F32)], axis=0).T
    chunk = min(64, rows)
    for first in range(0, rows, chunk):
        at = slice(first, first + chunk)
        scales = wide(turned[at, 0:1], (chunk, LANES))
        shifts = wide(turned[at, 8:9], (chunk, LANES))
        for piece in range(width // LANES):
            lanes = slice(piece * LANES, (piece + 1) * LANES)
            gate = gate_ref[at, lanes]
            ssd = ssd_ref[at, lanes]
            d_hidden = dh_ref[at, lanes]
            gain = gain_ref[0:1, lanes]
            sig = sigmoid(gate)
            act = gate * sig
            gated = ssd * act
            unit = gated * scales
            hidden_ref[at, lanes] = (unit * gain).astype(BF16)
            gain_out[:, lanes] += jnp.sum((d_hidden * unit).reshape(chunk // 8, 8, LANES), axis=0)
            d_gated = scales * (d_hidden * gain) - gated * shifts
            dssd_ref[at, lanes] = d_gated * act
            dgate_ref[at, lanes] = (
                d_gated * ssd * (sig * (1.0 + gate * (1.0 - sig)))
            ).astype(BF16)
    mixed = dot(hidden_ref[...], wout_ref[...]).astype(BF16)
    steps = pl.num_programs(0) // 2

    @pl.when(pl.program_id(0) < steps)
    def _():
        sent_ref[...] = mixed

    @pl.when(pl.program_id(0) >= steps)
    def _():
        kept_ref[...] = mixed


def gated_pass(core, ssd, gate, d_hidden, sums, gain, w_output):
    rows, width = ssd.shape
    step = min(MID_ROWS, rows // 2)
    steps = rows // step // 2

    def at(i, core):
        half = jnp.where(i < steps, 1 - core[0], core[0])
        return half * steps + i % steps

    here = lambda i, core: (at(i, core), 0)
    fixed = lambda i, core: (0, 0)
    return pl.pallas_call(
        gated_kernel,
        grid_spec=pltpu.PrefetchScalarGridSpec(
            num_scalar_prefetch=1,
            grid=(2 * steps,),
            in_specs=[
                pl.BlockSpec((step, width), here),
                pl.BlockSpec((step, width), here),
                pl.BlockSpec((step, width), here),
                pl.BlockSpec((8, step), lambda i, core: (0, at(i, core))),
                pl.BlockSpec((1, width), fixed),
                resident(w_output),
            ],
            out_specs=[
                pl.BlockSpec((step, width), here),
                pl.BlockSpec((step, width), here),
                pl.BlockSpec((step, width), here),
                pl.BlockSpec((8, width), fixed),
                pl.BlockSpec((step, D), lambda i, core: (jnp.minimum(i, steps - 1), 0)),
                pl.BlockSpec((step, D), lambda i, core: (jnp.maximum(i - steps, 0), 0)),
            ],
        ),
        out_shape=[
            jax.ShapeDtypeStruct((rows, width), BF16),
            jax.ShapeDtypeStruct((rows, width), BF16),
            jax.ShapeDtypeStruct((rows, width), F32),
            jax.ShapeDtypeStruct((8, width), F32),
            jax.ShapeDtypeStruct((rows // 2, D), BF16),
            jax.ShapeDtypeStruct((rows // 2, D), BF16),
        ],
        compiler_params=pltpu.CompilerParams(vmem_limit_bytes=VMEM_LIMIT),
        cost_estimate=pl.CostEstimate(
            flops=2 * rows * width * D, bytes_accessed=20 * rows * width, transcendentals=0
        ),
        name="gated_pass",
    )(core, ssd, gate, d_hidden, sums, gain, w_output)


def unit_rows(tokens_ref):
    rows = tokens_ref[...].astype(F32)
    inverse = lax.rsqrt(jnp.mean(rows * rows, axis=1, keepdims=True) + EPS)
    return rows, inverse


def normed_grad_kernel(half_ref, dgate_ref, drest_ref, tokens_ref, wgate_ref, wrest_ref, out_ref, gain_out):
    @pl.when(pl.program_id(0) == 0)
    def _():
        gain_out[...] = jnp.zeros_like(gain_out)

    total = dot(dgate_ref[...], wgate_ref[...], NT) + dot(drest_ref[...], wrest_ref[...], NT)
    out_ref[...] = total.astype(BF16)
    rows, inverse = unit_rows(tokens_ref)
    weighted = total * (rows * inverse)
    gain_out[...] += jnp.sum(weighted.reshape(-1, 8, D), axis=0)


def normed_grad(half, weight, d_gate, d_rest, tokens, w_gate, w_rest):
    rows = tokens.shape[0]
    step = min(MID_ROWS, rows // 2)
    steps = rows // step // 2
    here = lambda i, half: (half[0] * steps + i, 0)
    return pl.pallas_call(
        normed_grad_kernel,
        grid_spec=pltpu.PrefetchScalarGridSpec(
            num_scalar_prefetch=1,
            grid=(steps,),
            in_specs=[
                pl.BlockSpec((step, d_gate.shape[1]), here),
                pl.BlockSpec((step, d_rest.shape[1]), here),
                pl.BlockSpec((step, D), here),
                resident(w_gate),
                resident(w_rest),
            ],
            out_specs=[
                pl.BlockSpec((step, D), lambda i, half: (i, 0)),
                pl.BlockSpec((8, D), lambda i, half: (0, 0)),
            ],
        ),
        out_shape=[
            jax.ShapeDtypeStruct((rows // 2, D), BF16),
            jax.ShapeDtypeStruct((8, D), F32),
        ],
        compiler_params=pltpu.CompilerParams(vmem_limit_bytes=VMEM_LIMIT),
        cost_estimate=pl.CostEstimate(
            flops=weight * rows * D * (d_gate.shape[1] + d_rest.shape[1]),
            bytes_accessed=weight * 6 * rows * D,
            transcendentals=0,
        ),
        name="normed_grad",
    )(half, d_gate, d_rest, tokens, w_gate, w_rest)


def input_grad_kernel(core_ref, own_ref, other_ref, tokens_ref, cot_ref, gain_ref, out_ref, terms):
    steps = pl.num_programs(0) // 2
    mine = pl.program_id(0) // steps == core_ref[0]

    @pl.when(mine)
    def _():
        terms[...] = own_ref[...].astype(F32)

    @pl.when(jnp.logical_not(mine))
    def _():
        terms[...] = other_ref[...].astype(F32)

    rows, inverse = unit_rows(tokens_ref)
    weighted = terms[...] * gain_ref[0:1, :]
    inner = jnp.mean(weighted * rows, axis=1, keepdims=True)
    out_ref[...] = (
        cot_ref[...].astype(F32) + inverse * weighted - rows * (inverse * inverse * inverse * inner)
    )


def input_grads(core, own, other, tokens, cotangent, gain):
    rows = tokens.shape[0]
    step = min(MID_ROWS, rows // 2)
    steps = rows // step // 2
    here = lambda i, core: (i, 0)

    def part_at(is_own):
        def index(i, core):
            wanted = (i // steps == core[0]) == is_own
            parked = jnp.where((core[0] == 0) == is_own, steps - 1, 0)
            return (jnp.where(wanted, i % steps, parked), 0)

        return index

    return pl.pallas_call(
        input_grad_kernel,
        grid_spec=pltpu.PrefetchScalarGridSpec(
            num_scalar_prefetch=1,
            grid=(2 * steps,),
            in_specs=[
                pl.BlockSpec((step, D), part_at(True)),
                pl.BlockSpec((step, D), part_at(False)),
                pl.BlockSpec((step, D), here),
                pl.BlockSpec((step, D), here),
                pl.BlockSpec((1, D), lambda i, core: (0, 0)),
            ],
            out_specs=pl.BlockSpec((step, D), here),
            scratch_shapes=[pltpu.VMEM((step, D), F32)],
        ),
        out_shape=jax.ShapeDtypeStruct((rows, D), F32),
        compiler_params=pltpu.CompilerParams(vmem_limit_bytes=VMEM_LIMIT),
        cost_estimate=pl.CostEstimate(
            flops=0, bytes_accessed=10 * rows * D, transcendentals=0
        ),
        name="input_grads",
    )(core, own, other, tokens, cotangent, gain)


def held_rows(first):
    return (pl.ds(pl.multiple_of(first, COPY_ROWS), TILE), slice(None))


def band_tiles(ref):
    columns = ref.shape[1] // TILE
    for tile in range(columns * (ref.shape[0] // TILE)):
        down, across = tile // columns, tile % columns
        yield tile, (
            slice(down * TILE, (down + 1) * TILE),
            slice(across * TILE, (across + 1) * TILE),
        )


def copied(first, helds, ref, at):
    past = 0
    for held_ref in helds:
        size = held_ref.shape[0]
        if len(helds) == 1:
            ref[at] = held_ref[held_rows(first)]
        else:

            @pl.when((first >= past) & (first < past + size))
            def _(held_ref=held_ref, past=past):
                ref[at] = held_ref[held_rows(first - past)]

        past += size


def assemble_kernel(parts, width, rows_ref, *refs):
    helds = refs[:parts]
    band = pl.program_id(0)
    outs = refs[parts:]
    if width:
        outs[1][:, width:] = outs[0][...]
        outs = (outs[1].at[:, 0:width],)
    base = 0
    for ref in outs:
        count = (ref.shape[0] // TILE) * (ref.shape[1] // TILE)
        for tile, at in band_tiles(ref):
            copied(rows_ref[base + band * count + tile], helds, ref, at)
        base += count * pl.num_programs(0)


def assemble(rows, helds, side_cols, shapes):
    bands = min(shape[0] for shape in shapes) // TILE
    bands = min(bands, 8)
    here = lambda i: (i, 0)
    width = shapes[0][1] - side_cols[0].shape[1] if side_cols else 0
    return pl.pallas_call(
        functools.partial(assemble_kernel, len(helds), width),
        grid=(bands,),
        in_specs=[pl.BlockSpec(memory_space=pltpu.SMEM)]
        + [resident(held) for held in helds]
        + [pl.BlockSpec((side.shape[0] // bands, side.shape[1]), here) for side in side_cols],
        out_specs=[pl.BlockSpec((shape[0] // bands, shape[1]), here) for shape in shapes],
        out_shape=[jax.ShapeDtypeStruct(shape, BF16) for shape in shapes],
        compiler_params=pltpu.CompilerParams(vmem_limit_bytes=VMEM_LIMIT),
        cost_estimate=pl.CostEstimate(
            flops=0, bytes_accessed=4 * sum(held.size for held in helds), transcendentals=0
        ),
        name="assemble",
    )(rows, *helds, *side_cols)


def spread_kernel(rows_ref, *refs):
    out_ref = refs[-1]
    band = pl.program_id(0)
    base = 0
    for ref in refs[:-1]:
        count = (ref.shape[0] // TILE) * (ref.shape[1] // TILE)
        for tile, place in band_tiles(ref):
            first = rows_ref[base + band * count + tile]

            @pl.when(first >= 0)
            def _(first=first, place=place, ref=ref):
                out_ref[held_rows(first)] = ref[place]

        base += count * pl.num_programs(0)


def spread(grad_rows, grads, total_rows):
    bands = min(grad.shape[0] for grad in grads) // TILE
    return pl.pallas_call(
        spread_kernel,
        grid=(bands,),
        in_specs=[pl.BlockSpec(memory_space=pltpu.SMEM)]
        + [pl.BlockSpec((grad.shape[0] // bands, grad.shape[1]), lambda i: (i, 0)) for grad in grads],
        out_specs=pl.BlockSpec((total_rows, TILE), lambda i: (0, 0)),
        out_shape=jax.ShapeDtypeStruct((total_rows, TILE), BF16),
        compiler_params=pltpu.CompilerParams(vmem_limit_bytes=VMEM_LIMIT),
        cost_estimate=pl.CostEstimate(
            flops=0,
            bytes_accessed=2 * total_rows * TILE + sum(2 * grad.size for grad in grads),
            transcendentals=0,
        ),
        name="spread",
    )(grad_rows, *grads)


def update_kernel(
    rows_ref, early_ref, late_ref, repair_ref, tiles_ref, lstat_ref, rstat_ref, lroot_ref, rroot_ref,
    grads_out, left_out, right_out, tiles_out, copy_out, grad_tile,
):
    dot = functools.partial(lax.dot_general, dimension_numbers=NN, preferred_element_type=F32)
    step = tiles_ref.shape[0]
    for tile in range(step):
        first = rows_ref[pl.program_id(0) * step + tile]
        past = 0
        for source in (early_ref, late_ref, repair_ref):
            size = source.shape[0]

            @pl.when((first >= past) & (first < past + size))
            def _(source=source, past=past, tile=tile):
                grad_tile[tile] = source[held_rows(first - past)]

            past += size
    for tile in range(step):
        exact_grad = grad_tile[tile]
        grad = exact_grad.astype(BF16)
        turned = exact_grad.T.astype(BF16)
        grads_out[tile] = exact_grad
        left_out[tile] = STAT_DECAY * lstat_ref[tile] + (1.0 - STAT_DECAY) * dot(grad, turned)
        right_out[tile] = STAT_DECAY * rstat_ref[tile] + (1.0 - STAT_DECAY) * dot(turned, grad)
        shaped = careful(careful(lroot_ref[tile], exact_grad), rroot_ref[tile])
        updated = tiles_ref[tile] - LR_MAT * shaped
        tiles_out[tile] = updated
        copy_out[tile] = updated.astype(BF16)


def update_tiles(rows, early, late, repair, tiles, left_stats, right_stats, left_roots, right_roots):
    count = tiles.shape[0]
    step = TILES_STEP if count % TILES_STEP == 0 else 1
    spec = pl.BlockSpec((step, TILE, TILE), lambda i, rows: (i, 0, 0))
    sources = [pl.BlockSpec(part.shape, lambda i, rows: (0, 0)) for part in (early, late, repair)]
    whole = jax.ShapeDtypeStruct(tiles.shape, F32)
    return pl.pallas_call(
        update_kernel,
        grid_spec=pltpu.PrefetchScalarGridSpec(
            num_scalar_prefetch=1,
            grid=(count // step,),
            in_specs=sources + [spec] * 5,
            out_specs=[spec] * 5,
            scratch_shapes=[pltpu.VMEM((step, TILE, TILE), F32)],
        ),
        out_shape=[whole] * 4 + [jax.ShapeDtypeStruct(tiles.shape, BF16)],
        compiler_params=pltpu.CompilerParams(vmem_limit_bytes=VMEM_LIMIT),
        cost_estimate=pl.CostEstimate(
            flops=18 * count * TILE**3, bytes_accessed=42 * count * TILE**2, transcendentals=0
        ),
        name="update_tiles",
    )(rows, early, late, repair, tiles, left_stats, right_stats, left_roots, right_roots)


def fetch_plan(slot_map, own_tiles, side_rows):
    count = slot_map.shape[0]
    tiles = jnp.arange(count, dtype=jnp.int32)
    waits = tiles // (count // 3) != 1
    key = tiles + waits * count
    owner = slot_map // own_tiles
    together = owner[:, None] == owner[None, :]
    place = jnp.sum(together & (key[None, :] < key[:, None]), axis=1, dtype=jnp.int32)
    first = max(1, own_tiles * 13 // 24)
    first_rows, second_rows = first * TILE + side_rows, (own_tiles - first) * TILE
    early = place < first
    owners = count // own_tiles
    rows = jnp.where(
        early,
        owner * first_rows + place * TILE,
        owners * first_rows + owner * second_rows + (place - first) * TILE,
    )
    rank = lax.axis_index("dp")
    places = jnp.arange(own_tiles, dtype=jnp.int32)
    order = jnp.sum(
        jnp.where(
            (owner == rank)[None, :] & (place[None, :] == places[:, None]),
            slot_map[None, :] - rank * own_tiles,
            0,
        ),
        axis=1,
        dtype=jnp.int32,
    )
    return rows, order, first, jnp.any(~waits & ~early)


def tile_plan(slot_map, own_tiles):
    count = slot_map.shape[0]
    tiles = jnp.arange(count, dtype=jnp.int32)
    kind = tiles // (count // 3)
    waits = kind == 1
    key = tiles + waits * count
    owner = slot_map // own_tiles
    together = owner[:, None] == owner[None, :]
    first = own_tiles // 2
    last = min(own_tiles, own_tiles - first + SLACK)
    place = jnp.sum(together & (key[None, :] < key[:, None]), axis=1, dtype=jnp.int32)
    early = (place < first) & ~waits
    behind = jnp.sum(
        together & ~early[None, :] & (key[None, :] < key[:, None]), axis=1, dtype=jnp.int32
    )
    late = ~early & (behind < last)
    repair = ~early & ~late

    def rows_where(chosen, position, rows):
        return jnp.where(chosen, owner * rows + position * TILE, -1)

    early_rows, late_rows = first * TILE, last * TILE
    plans = (
        (rows_where(early, place, early_rows), early_rows),
        (rows_where(late, behind, late_rows), late_rows),
        (rows_where(repair, behind - last, early_rows), early_rows),
    )
    in_owner = jnp.where(early, place, first + behind) * TILE
    rank = lax.axis_index("dp")
    slots = rank * own_tiles + jnp.arange(own_tiles, dtype=jnp.int32)
    own_rows = jnp.sum(
        jnp.where(slot_map[None, :] == slots[:, None], in_owner[None, :], 0), axis=1, dtype=jnp.int32
    )
    return plans, own_rows, jnp.any(repair).astype(F32)


def on_device(
    tokens,
    cotangent,
    doc_ids,
    tile_slots,
    matrix_tiles,
    left_stats,
    right_stats,
    left_roots,
    right_roots,
    side_weight,
    side_moment,
    side_second,
    vector_params,
    vector_moment,
    vector_second,
):
    n_tensor = lax.axis_size("tensor")
    n_dp = lax.axis_size("dp")
    tensor_rank = lax.axis_index("tensor")
    core = tensor_rank % 2
    di_local = DI // n_tensor
    heads_local = HEADS // n_tensor
    model_local = D // n_tensor
    bc_local = 2 * NS // n_tensor
    rows = tokens.shape[0]
    half = rows // 2
    sequences, seq_len = doc_ids.shape
    slot_map = tile_slots[0]
    own_tiles = matrix_tiles.shape[1]
    side_rows = side_weight.shape[0] * SIDE // TILE
    fetch_rows, order, first_tiles, misfetch = fetch_plan(
        slot_map, own_tiles, side_rows
    )
    plans, own_rows, misfit = tile_plan(slot_map, own_tiles)
    misfits = sum_over(jnp.full((8, LANES), misfit), "tensor")
    vector = vector_params[0]
    bounds = segment_bounds(di_local, heads_local, model_local, bc_local, CONV)

    def segment_of(index):
        return vector[bounds[index] : bounds[index + 1]]

    conv_kernel = segment_of(0).reshape(CONV, di_local)
    conv_offset = segment_of(1)
    gate_gain = segment_of(2)
    log_rate = segment_of(3)
    skip_gain = segment_of(4)
    dt_offset = segment_of(5)

    mine = matrix_tiles[0].astype(BF16)[order].reshape(own_tiles * TILE, TILE)
    cut = first_tiles * TILE
    first_share = jnp.concatenate(
        [mine[:cut], side_weight.astype(BF16).reshape(side_rows, TILE)], axis=0
    )
    first_held = lax.all_gather(first_share, "dp", axis=0, tiled=True)
    second_held = lax.all_gather(mine[cut:], "dp", axis=0, tiled=True)
    shared = lax.all_gather(vector[bounds[6] :][None, :], "tensor", axis=0, tiled=True)
    pre_gain = shared[:, :model_local].reshape(D)
    bc_kernel = (
        shared[:, model_local : model_local + CONV * bc_local]
        .reshape(n_tensor, CONV, bc_local)
        .transpose(1, 0, 2)
        .reshape(CONV, 2 * NS)
    )
    bc_offset = shared[:, model_local + CONV * bc_local :].reshape(2 * NS)
    par = jnp.concatenate(
        [
            conv_kernel,
            conv_offset[None],
            jnp.repeat(skip_gain, di_local // heads_local)[None],
            gate_gain[None],
            jnp.zeros((1, di_local), F32),
        ],
        axis=0,
    )
    bcpar = jnp.concatenate([bc_kernel, bc_offset[None], jnp.zeros((3, 2 * NS), F32)], axis=0)
    decay_rate = -jnp.exp(log_rate)
    hp = jnp.pad(
        jnp.stack([dt_offset, decay_rate * LOG2E, decay_rate]), ((0, 5), (0, LANES - heads_local))
    )
    pick = (
        jnp.arange(di_local)[:, None] // (di_local // heads_local) == jnp.arange(LANES)[None, :]
    ).astype(BF16)
    starts = jnp.sum(doc_ids[:, None, :] < doc_ids[:, :, None], axis=2).astype(F32).reshape(rows)
    ends = jnp.sum(doc_ids[:, None, :] <= doc_ids[:, :, None], axis=2).astype(F32).reshape(rows)
    start_row = starts[None, :]
    start_wide = jnp.broadcast_to(starts[:, None], (rows, LANES))
    end_wide = jnp.broadcast_to(ends[:, None], (rows, LANES))

    residual = tokens.astype(F32)
    inverse = lax.rsqrt(jnp.mean(residual * residual, axis=1, keepdims=True) + EPS)
    normed = (residual * inverse * pre_gain).astype(BF16)
    normed, misfits = tied(normed, misfits)
    misfit = misfits[0, 0] > 0.0

    side_copy = first_held.reshape(n_dp, -1, TILE)[:, cut:].reshape(D, SIDE)
    side_cols = jnp.concatenate(
        [
            side_copy[:, : 2 * NS],
            lax.dynamic_slice_in_dim(side_copy, 2 * NS + tensor_rank * heads_local, heads_local, 1),
            jnp.zeros((D, 2 * NS - heads_local), BF16),
        ],
        axis=1,
    )
    per_block = (D // TILE) * (di_local // TILE)
    rest_shape = ((D, di_local + side_cols.shape[1]),)

    rest_rows = fetch_rows[per_block : 2 * per_block]

    def forward_with(rows, helds):
        weights = assemble(rows, helds, (side_cols,), rest_shape)[0]
        projected = project(normed, weights)
        scanned = ssd_forward(projected, start_wide, par, bcpar, hp, sequences)
        return (weights, projected, *scanned)

    tried = forward_with(
        jnp.minimum(rest_rows, first_held.shape[0] - TILE), (first_held,)
    )
    tried, second_held = tied(tried, second_held)
    w_rest, rest, ssd, states = lax.while_loop(
        lambda carry: carry[0],
        lambda carry: (False, forward_with(rest_rows, (first_held, second_held))),
        (misfetch, tried),
    )[1]
    w_gate, w_output = assemble(
        jnp.concatenate([fetch_rows[:per_block], fetch_rows[2 * per_block :]]),
        (first_held, second_held),
        (),
        ((D, di_local), (di_local, D)),
    )
    gate, d_hidden, sums = gate_project(
        normed, cotangent, w_gate, w_output, ssd, gate_gain[None, :]
    )
    sums = sum_over(sums, "tensor")
    core_at = core[None].astype(jnp.int32)
    hidden, d_gate, d_ssd, gain_sums, out_sent, out_kept = gated_pass(
        core_at, ssd, gate, d_hidden, sums, gate_gain[None, :], w_output
    )

    def chip_sum(kept, sent):
        return (kept.astype(F32) + swap(sent, "tensor", 1).astype(F32)).astype(BF16)

    out_chip = chip_sum(out_kept, out_sent)
    grad_output = contract_rows(hidden, cotangent).astype(BF16)
    out_chip, normed_now = tied(out_chip, normed)
    out_others = [swap(part, "tensor", 2) for part in jnp.split(out_chip, 2)]
    grad_gate = contract_rows(normed_now, d_gate).astype(BF16)
    early_grads = spread(
        jnp.concatenate([plans[0][0][:per_block], plans[0][0][2 * per_block :]]),
        (grad_gate, grad_output),
        n_dp * plans[0][1],
    )
    d_ssd, early_grads = tied(d_ssd, early_grads)
    early = OwnerSum(early_grads, ((0, 1), (2, 3)))
    given = (states, start_wide, end_wide, start_row, par, bcpar, hp, pick, sequences)
    place = (tensor_rank * heads_local).astype(jnp.int32)[None]
    back, parts, side_parts = (), [], []
    for sequence in range(sequences):
        d_rest, d_side, *sums_here = ssd_backward(sequence, back, place, rest, d_ssd, *given)
        parts.append(sums_here)
        if sequence == 0:
            d_rest, out_others[0] = early.first((d_rest, out_others[0]))
        else:
            d_rest, side_parts[-1] = tied(d_rest, side_parts[-1])
        side_parts.append((d_side, swap(d_side, "tensor", 1)))
        back = (d_rest,)
    gx, gbc, gh = (sum(terms) for terms in zip(*parts))
    d_rest, out_others[1] = early.second((back[0], out_others[1]))

    split_side = sequences // 2
    side_chips = [
        jnp.concatenate([(own + other).astype(BF16) for own, other in part], axis=0)
        for part in (side_parts[:split_side], side_parts[split_side:])
    ]
    d_rest, side_chips[0] = tied(d_rest, side_chips[0])
    side_others = [swap(side_chips[0], "tensor", 2)]
    grad_input = contract_rows(normed, d_rest[:, :di_local]).astype(BF16)
    late_grads = spread(plans[1][0], (grad_gate, grad_input, grad_output), n_dp * plans[1][1])
    late_grads, side_chips[1], side_others[0], d_rest = early.third(
        (late_grads, side_chips[1], side_others[0], d_rest)
    )
    side_others.append(swap(side_chips[1], "tensor", 2))
    late = OwnerSum(late_grads, ((0,), (1,), (2, 3)))
    d_sent, pre_sent = normed_grad(1 - core_at, 16, d_gate, d_rest, tokens, w_gate, w_rest)
    early_share, (d_sent, d_rest) = early.total((d_sent, d_rest))
    d_sent, d_rest = late.first((d_sent, d_rest))
    d_kept, pre_kept = normed_grad(core_at, 0, d_gate, d_rest, tokens, w_gate, w_rest)
    d_kept, side_others[1] = late.second((d_kept, side_others[1]))
    grad_pre = jnp.sum(pre_sent + pre_kept, axis=0)
    d_chip = chip_sum(d_kept, d_sent)
    d_others = [swap(part, "tensor", 2) for part in jnp.split(d_chip, 4)]
    d_others[0], early_share = late.third((d_others[0], early_share))

    side_total = jnp.concatenate(
        [
            (own.astype(F32) + other.astype(F32)).astype(BF16)
            for own, other in zip(side_chips, side_others)
        ],
        axis=0,
    )
    side_total, d_others[0] = tied(side_total, d_others[0])
    grad_side = lax.dynamic_index_in_dim(
        contract_rows(normed, side_total).reshape(n_dp, n_tensor, -1, side_total.shape[1]),
        tensor_rank,
        1,
        keepdims=False,
    )[:, :, :SIDE]
    gx_sums = jnp.sum(gx.reshape(CONV + 2, 8, di_local), axis=1)
    gbc_sums = jnp.sum(gbc.reshape(CONV + 1, 8, 2 * NS), axis=1)
    gh_sums = jnp.sum(gh.reshape(2, 8, LANES), axis=1)[:, :heads_local]
    own_vector = jnp.concatenate(
        [
            gx_sums[: CONV + 1].reshape(-1),
            jnp.sum(gain_sums, axis=0),
            gh_sums[0],
            jnp.sum(gx_sums[CONV + 1].reshape(heads_local, -1), axis=1),
            gh_sums[1],
        ]
    )
    small_sums = SharedSums(
        grad_side.reshape(n_dp, -1), jnp.concatenate([own_vector, grad_pre, gbc_sums.reshape(-1)])
    )
    small_sums.exchange()
    late_share, (small_sums.owned, d_others[1]) = late.total((small_sums.owned, d_others[1]))
    small_sums.exchange_rest()
    late_share, misfit = tied(late_share, misfit)

    def repaired(grads):
        again = spread(plans[2][0], grads, n_dp * plans[2][1])
        return lax.psum_scatter(again, "dp", scatter_dimension=0, tiled=True).astype(F32)

    repair_share = lax.cond(
        misfit,
        repaired,
        lambda grads: jnp.zeros((plans[2][1], TILE), F32),
        (grad_gate, grad_input, grad_output),
    )

    tile_share, left_new, right_new, tiles_new, tiles_copy = update_tiles(
        own_rows,
        early_share,
        late_share,
        repair_share,
        matrix_tiles[0],
        left_stats[0],
        right_stats[0],
        left_roots[0],
        right_roots[0],
    )
    tiles_copy, d_others[2] = tied(tiles_copy, d_others[2])
    split_at = own_vector.shape[0]
    side_own, all_vector = small_sums.owned, small_sums.shared
    quarters = jnp.where(
        (jnp.arange(n_tensor) == tensor_rank)[:, None], side_own, jnp.zeros((), F32)
    )
    common = sum_over(
        jnp.concatenate([quarters.reshape(-1), all_vector[split_at:]])[None], "tensor"
    )[0]
    side_share = common[: side_weight.size].reshape(side_weight.shape)
    common = common[side_weight.size :]
    quarter = half // 2
    mixed_own = [
        (
            lax.dynamic_slice_in_dim(tokens, core * half + i * quarter, quarter, 0).astype(F32)
            + (out_chip[i * quarter : (i + 1) * quarter].astype(F32) + out_others[i].astype(F32))
        ).astype(BF16)
        for i in range(2)
    ]
    mixed_other = [swap(part, "tensor", 1) for part in mixed_own]
    lower_half = core == 0
    mixed = jnp.concatenate(
        [jnp.where(lower_half, own, other) for own, other in zip(mixed_own, mixed_other)]
        + [jnp.where(lower_half, other, own) for own, other in zip(mixed_own, mixed_other)],
        axis=0,
    )

    d_half = (d_chip.astype(F32) + jnp.concatenate(d_others).astype(F32)).astype(BF16)
    d_half_other = swap(d_half, "tensor", 1)
    input_grad = input_grads(core_at, d_half, d_half_other, tokens, cotangent, pre_gain[None, :])

    pre_share = lax.dynamic_slice_in_dim(common[:D], tensor_rank * model_local, model_local, 0)
    bc_share = lax.dynamic_slice_in_dim(
        common[D:].reshape(CONV + 1, 2 * NS), tensor_rank * bc_local, bc_local, 1
    )
    vector_total = jnp.concatenate([all_vector[:split_at], pre_share, bc_share.reshape(-1)])[None]

    side_m, side_v, side_new = adam_update(
        side_weight, side_moment, side_second, side_share, LR_SIDE
    )
    vec_m, vec_v, vec_new = adam_update(
        vector_params, vector_moment, vector_second, vector_total, LR_VEC
    )
    return (
        mixed,
        input_grad,
        tile_share[None],
        left_new[None],
        right_new[None],
        tiles_new[None],
        tiles_copy[None],
        side_m,
        side_v,
        side_new,
        vec_m,
        vec_v,
        vec_new,
    )


def solution(mesh):
    by_dp = P("dp", None)
    by_tensor = P("tensor", None)
    by_tile = P("tensor", "dp", None, None)
    return jax.shard_map(
        on_device,
        mesh=mesh,
        in_specs=(by_dp,) * 3
        + (by_tensor,)
        + (by_tile,) * 5
        + (by_dp,) * 3
        + (by_tensor,) * 3,
        out_specs=(by_dp,) * 2 + (by_tile,) * 5 + (by_dp,) * 3 + (by_tensor,) * 3,
        check_vma=False,
    )
```

time: 2820 us -> 745 us (0.26)
  waiting for transfers between devices: 899 us -> 193 us
  matrix products: 661 us -> 45.4 us
  local copies, waits for them, and re-layouts: 637 us -> 39.4 us
  other arithmetic: 461 us -> 110 us
  Pallas kernels: 0 us -> 283 us
  blocking collectives: 84.2 us -> 6.35 us
  starting transfers between devices: 0.59 us -> 45.6 us
  loops' own time: 34 us -> 1.33 us
    dot_general x124 -> x0, matrix products: 564 us -> none  [the longest x24 184 us: advance(): output = jnp.einsum('tsh,shp->thp', weights, span_x, precision=HIGH)]
    reduce_scatter x4 -> x0, waiting for transfers between devices: 448 us -> none  [the longest x1 345 us: on_device(): lax.psum_scatter(in_slots, 'dp', scatter_dimension=0, tiled=True)]
    pallas_call x0 -> x14, Pallas kernels: none -> 283 us  [the longest x2 69 us: ssd_backward(): pl.pallas_call(ssd_backward_kernel, grid=(blocks,), in_specs=[pl.BlockSpe...]
    psum x1 -> x0, waiting for transfers between devices: 273 us -> none  [on_device(): d_normed = lax.psum(local_sum, 'tensor') + contract_cols(d_side, side_copy)]
    reshape x35 -> x10, local copies, waits for them, and re-layouts: 118 us -> 3.51 us  [the longest x1 1.39 us: on_device(): side_copy = first_held.reshape(n_dp, -1, TILE)[:, cut:].reshape(D, SIDE)]
    another operation x128 -> x1, other arithmetic: 109 us -> 0.01 us  [on_device(): jnp.stack([dt_offset, decay_rate * LOG2E, decay_rate])]
    another operation x126 -> x7, local copies, waits for them, and re-layouts: 92.5 us -> 1.49 us
    psum x4 -> x0, blocking collectives: 78 us -> none  [the longest x1 38 us: on_device(): vector_total = lax.psum(packed_grad[None, :], 'dp')]
  transfers between devices with their start and end apart: 9 -> 41, of which waited for: 6 -> 12; matrix products, arithmetic and copies ran while one was open for 10% -> 21% of each run, Pallas kernels for 0% -> 26%
where the time goes in v1:
time: 745 us; the launch traced here: 740 us
  Pallas kernels  283 us (38%)
  waiting for transfers between devices  193 us (26%)
  other arithmetic  110 us (15%)
  starting transfers between devices  45.6 us (6%)
  matrix products  45.4 us (6%)
  local copies, waits for them, and re-layouts  39.4 us (5%)
  between operations  17.3 us (2%)
    all_gather x1, waiting for transfers between devices, on_device(): first_held = lax.all_gather(first_share, 'dp', axis=0, tiled=True)  90.3 us
    pallas_call x2, Pallas kernels, ssd_backward(): pl.pallas_call(ssd_backward_kernel, grid=(blocks,), in_specs=[pl.BlockSpe...  69 us
    ppermute x29, waiting for transfers between devices, swap(): return lax.ppermute(value, axis, [(i, i ^ bit) for i in range(size)])  47.3 us
    dot_general x4, matrix products, contract_rows(): lax.dot_general(left, right, (((0,), (0,)), ((), ())), preferred_element_...  45.4 us
    pallas_call x2, Pallas kernels, normed_grad(): pl.pallas_call(normed_grad_kernel, grid_spec=pltpu.PrefetchScalarGridSpec...  39.3 us
    all_gather x1, waiting for transfers between devices, on_device(): second_held = lax.all_gather(mine[cut:], 'dp', axis=0, tiled=True)  34.3 us
    pallas_call x1, Pallas kernels, ssd_forward(): pl.pallas_call(ssd_forward_kernel, grid=(sequences, blocks), in_specs=[pl...  28 us
    pallas_call x1, Pallas kernels, gate_project(): pl.pallas_call(gate_kernel, grid=(rows // step,), in_specs=[pl.BlockSpec(...  26.3 us
  transfers between devices with their start and end apart: 41, of which 12 were waited for; matrix products, arithmetic and copies ran while one was open for 21% of the time, Pallas kernels for 26%

profile of v1, /device:TPU:0, one launch (start us, length us, event | category | flops | bytes accessed | tf_op | source)
XLA Modules:
  0.0 740.2 jit_solution(16085795887766666008)
XLA Ops:
  18.9 6.3 all-gather
  28.1 5.1 fusion.2
  33.3 2.6 convert_reduce_fusion
  36.4 8.8 %fusion.4.left_ref.normed_ref = bf16[2048,2048]{1,0:T(8,128)(2,1)} fusion(bf16[2048,2048]{1,0:T(8,128)(2,1)} %tokens_ref.5, f32[2048]{0:T(1024)S(1)} %bitcast.170, f32[2048]{0:T(1024)S(1)} %add_rsqrt_fusion), kind=kLoop, calls=%fused_computation.7 | loop fusion | flops 16777216 | bytes 16793600 | tf_op jit(solution)/shard_map/convert_element_type | solution.py:1203
  49.6 90.3 %all-gather.4.cloned.1.call-done.refs_0_ = bf16[31744,128]{1,0:T(8,128)(2,1)} async-done(((bf16[3968,128]{1,0:T(8,128)(2,1)}), bf16[31744,128]{1,0:T(8,128)(2,1)}) %all-gather.4.cloned.1.call-update) | async-done | bytes 8126480 | tf_op jit(solution)/shard_map/all_gather | solution.py:1166
  143.4 7.7 %assemble.3.right_ref = bf16[2048,1536]{1,0:T(8,128)(2,1)} custom-call(s32[128]{0:T(128)} %get-tuple-element.453.rows_ref, bf16[31744,128]{1,0:T(8,128)(2,1)} %all-gather.4.cloned.1.call-done.refs_0_, bf16[2048,512]{1,0:T(8,128)(2,1)S(1)} %maximum_maximum_fusion.refs_1_), custom_call_target="tpu_custom_call" | custom-call | bytes 16252928 | tf_op jit(solution)/shard_map/assemble/pallas_call | solution.py:940
  151.1 18.8 %project.2.rest_ref.prev_ref = f32[2048,1536]{1,0:T(8,128)} custom-call(bf16[2048,2048]{1,0:T(8,128)(2,1)} %fusion.4.left_ref.normed_ref, bf16[2048,1536]{1,0:T(8,128)(2,1)} %assemble.3.right_ref), custom_call_target="tpu_custom_call" | custom-call | flops 12884901888 | bytes 27262976 | tf_op jit(solution)/shard_map/project/pallas_call | solution.py:615
  171.2 28.0 %ssd_forward.2 = (f32[2048,1024]{1,0:T(8,128)}, f32[16,128,1024]{2,1,0:T(8,128)}) custom-call(f32[2048,1536]{1,0:T(8,128)} %project.2.rest_ref.prev_ref, f32[2048,1536]{1,0:T(8,128)} %project.2.rest_ref.prev_ref, f32[2048,128]{1,0:T(8,128)} %broadcast_in_dim.141.start_ref.refs_5_.refs_6_, f32[8,1024]{1,0:T(8,128)S(1)} %concatenate.81.par_ref.refs_8_.refs_9_, ...), custom_call_target="tpu_custom_call" | custom-call | flops 10737418240 | bytes 41943040 | tf_op jit(solution)/shard_map/ssd_forward/pallas_call | solution.py:501
  199.2 34.3 %all-gather.6.cloned.1.call-done.refs_1_ = bf16[22528,128]{1,0:T(8,128)(2,1)} async-done(((bf16[2816,128]{1,0:T(8,128)(2,1)}), bf16[22528,128]{1,0:T(8,128)(2,1)}) %all-gather.6.cloned.1.call-update) | async-done | bytes 5767184 | tf_op jit(solution)/shard_map/all_gather | solution.py:1167
  234.5 12.0 %assemble.4 = (bf16[2048,1024]{1,0:T(8,128)(2,1)}, bf16[1024,2048]{1,0:T(8,128)(2,1)}) custom-call(s32[256]{0:T(256)} %pad_add_fusion.rows_ref, bf16[31744,128]{1,0:T(8,128)(2,1)} %get-tuple-element.520, bf16[22528,128]{1,0:T(8,128)(2,1)} %get-tuple-element.522), custom_call_target="tpu_custom_call" | custom-call | bytes 27787264 | tf_op jit(solution)/shard_map/assemble/pallas_call | solution.py:940
  246.6 26.3 %gate_project.1 = (f32[2048,1024]{1,0:T(8,128)}, f32[2048,1024]{1,0:T(8,128)}, f32[8,2048]{1,0:T(8,128)}) custom-call(bf16[2048,2048]{1,0:T(8,128)(2,1)} %get-tuple-element.525, bf16[2048,2048]{1,0:T(8,128)(2,1)} %cot_ref.3, bf16[2048,1024]{1,0:T(8,128)(2,1)} %get-tuple-element.215.wgate_ref, bf16[1024,2048]{1,0:T(8,128)(2,1)} %get-tuple-element.216.wout_ref, ...), custom_call_target="tpu_custom_call" | custom-call | flops 17179869184 | bytes 33554432 | tf_op jit(solution)/shard_map/gate_project/pallas_call | solution.py:654
  276.7 2.8 collective-permute-done.3
  280.2 25.8 %gated_pass.1 = (bf16[2048,1024]{1,0:T(8,128)(2,1)}, bf16[2048,1024]{1,0:T(8,128)(2,1)}, f32[2048,1024]{1,0:T(8,128)}, f32[8,1024]{1,0:T(8,128)}, bf16[1024,2048...) custom-call(s32[1]{0:T(128)} %bitcast.core_ref.half_ref, f32[2048,1024]{1,0:T(8,128)} %get-tuple-element.214.ssd_ref, ...), custom_call_target="tpu_custom_call" | custom-call | flops 8589934592 | bytes 41943040 | tf_op jit(solution)/shard_map/gated_pass/pallas_call | solution.py:741
  316.2 14.4 %convolution_convert_fusion.refs_1_.refs_2_ = bf16[1024,2048]{1,0:T(8,128)(2,1)} fusion(bf16[2048,1024]{1,0:T(8,128)(2,1)} %get-tuple-element.226, bf16[2048,2048]{1,0:T(8,128)(2,1)} %cot_ref.3), kind=kOutput, calls=%fused_computation.19 | convolution fusion | flops 8592031744 | bytes 16777216 | tf_op jit(solution)/shard_map/dot_general | solution.py:74
  330.6 6.2 add_convert_fusion.2
  336.8 13.0 %convolution_convert_fusion.1.refs_0_ = bf16[2048,1024]{1,0:T(8,128)(2,1)} fusion(bf16[2048,2048]{1,0:T(8,128)(2,1)} %get-tuple-element.525, bf16[2048,1024]{1,0:T(8,128)(2,1)S(1)} %copy-done.11), kind=kOutput, calls=%fused_computation.20 | convolution fusion | flops 8592031744 | bytes 16777216 | tf_op jit(solution)/shard_map/dot_general | solution.py:74
  349.8 9.8 %spread.4 = bf16[24576,128]{1,0:T(8,128)(2,1)} custom-call(s32[256]{0:T(256)} %pad_add_fusion.1.rows_ref, bf16[2048,1024]{1,0:T(8,128)(2,1)} %convolution_convert_fusion.1.refs_0_, bf16[1024,2048]{1,0:T(8,128)(2,1)} %convolution_convert_fusion.refs_1_.refs_2_), custom_call_target="tpu_custom_call" | custom-call | bytes 14680064 | tf_op jit(solution)/shard_map/spread/pallas_call | solution.py:974
  359.7 5.0 fusion.36
  369.5 34.4 %ssd_backward.2 = (bf16[2048,1536]{1,0:T(8,128)(2,1)}, f32[1024,384]{1,0:T(8,128)}, f32[48,1024]{1,0:T(8,128)}, f32[40,256]{1,0:T(8,128)}, f32[16,128]{1,0:T(8,128)}) custom-call(s32[1]{0:T(128)} %bitcast.13.refs_0_.refs_1_, f32[2048,1536]{1,0:T(8,128)} %get-tuple-element.228.refs_1_.refs_2_.refs_3_, ...), custom_call_target="tpu_custom_call" | custom-call | flops 13421772800 | bytes 20971520 | tf_op jit(solution)/shard_map/ssd_backward/pallas_call | solution.py:545
  407.2 6.1 collective-permute-done.6
  414.8 3.2 collective-permute-start.8
  418.0 34.6 %ssd_backward.3 = (bf16[2048,1536]{1,0:T(8,128)(2,1)}, f32[1024,384]{1,0:T(8,128)}, f32[48,1024]{1,0:T(8,128)}, f32[40,256]{1,0:T(8,128)}, f32[16,128]{1,0:T(8,128)}) custom-call(bf16[2048,1536]{1,0:T(8,128)(2,1)} %get-tuple-element.234.refs_0_, s32[1]{0:T(128)} %bitcast.13.refs_0_.refs_1_, ...), custom_call_target="tpu_custom_call", output_to_operand_aliasing={{0}: (0, {})} | custom-call | flops 13421772800 | bytes 20971520 | tf_op jit(solution)/shard_map/ssd_backward/pallas_call | solution.py:545
  459.9 3.2 fusion.16
  466.8 13.3 %fusion.7.refs_1_ = bf16[2048,1024]{1,0:T(8,128)(2,1)} fusion(bf16[2048,2048]{1,0:T(8,128)(2,1)} %get-tuple-element.525, bf16[2048,1536]{1,0:T(8,128)(2,1)S(1)} %copy-done.3), kind=kOutput, calls=%fused_computation.18 | convolution fusion | flops 8592031744 | bytes 16777216 | tf_op jit(solution)/shard_map/dot_general | solution.py:74
  481.7 11.5 %spread.5 = bf16[26624,128]{1,0:T(8,128)(2,1)} custom-call(s32[384]{0:T(512)} %get-tuple-element.448.rows_ref, bf16[2048,1024]{1,0:T(8,128)(2,1)} %convolution_convert_fusion.1.refs_0_, bf16[2048,1024]{1,0:T(8,128)(2,1)} %fusion.7.refs_1_, bf16[1024,2048]{1,0:T(8,128)(2,1)} %convolution_convert_fusion.refs_1_.refs_2_), custom_call_target="tpu_custom_call" | custom-call | bytes 19398656 | tf_op jit(solution)/shard_map/spread/pallas_call | solution.py:974
  494.3 7.5 %add_convert_fusion.4 = (bf16[512,2048]{1,0:T(8,128)(2,1)}, bf16[512,2048]{1,0:T(8,128)(2,1)}) fusion(bf16[512,2048]{1,0:T(8,128)(2,1)} %collective-permute-done.6, bf16[2048,2048]{1,0:T(8,128)(2,1)} %tokens_ref.5, s32[]{:T(128)S(6)} %select_n.295, bf16[1024,2048]{1,0:T(8,128)(2,1)} %add_convert_fusion.2, bf16[512,2048]{1,0:T(8,128)(2,1)} %collective-permute-done.10, ...), kind=kLoop, calls=%fused_computation.17 | loop fusion | flops 12582912 | bytes 16777224 | tf_op jit(solution)/shard_map/convert_element_type | solution.py:1377
  502.0 2.7 add_convert_fusion.11
  504.8 4.3 add_convert_fusion.9
  516.6 19.7 %normed_grad.2 = (bf16[1024,2048]{1,0:T(8,128)(2,1)}, f32[8,2048]{1,0:T(8,128)}) custom-call(s32[1]{0:T(128)S(6)} %sub.98.half_ref, bf16[2048,1024]{1,0:T(8,128)(2,1)} %get-tuple-element.225.dgate_ref, bf16[2048,1536]{1,0:T(8,128)(2,1)} %get-tuple-element.257.drest_ref, bf16[2048,2048]{1,0:T(8,128)(2,1)} %tokens_ref.5, ...), custom_call_target="tpu_custom_call" | custom-call | flops 171798691840 | bytes 402653184 | tf_op jit(solution)/shard_map/normed_grad/pallas_call | solution.py:802
  541.1 5.5 collective-permute-start.20
  546.5 3.4 fusion.14.early_ref
  550.0 19.6 %normed_grad.3 = (bf16[1024,2048]{1,0:T(8,128)(2,1)}, f32[8,2048]{1,0:T(8,128)}) custom-call(s32[1]{0:T(128)} %bitcast.core_ref.half_ref, bf16[2048,1024]{1,0:T(8,128)(2,1)} %get-tuple-element.225.dgate_ref, bf16[2048,1536]{1,0:T(8,128)(2,1)} %get-tuple-element.257.drest_ref, bf16[2048,2048]{1,0:T(8,128)(2,1)} %tokens_ref.5, ...), custom_call_target="tpu_custom_call" | custom-call | tf_op jit(solution)/shard_map/normed_grad/pallas_call | solution.py:802
  570.9 4.6 broadcast_select_fusion.3
  580.3 4.1 add_convert_fusion.1
  594.3 20.6 %collective-permute-done.26 = bf16[6656,128]{1,0:T(8,128)(2,1)S(1)} collective-permute-done((bf16[6656,128]{1,0:T(8,128)(2,1)S(1)}, bf16[6656,128]{1,0:T(8,128)(2,1)S(1)}, u32[]{:S(2)}, u32[]{:S(2)}) %collective-permute-start.26) | collective-permute-done | bytes 1703968 | tf_op jit(solution)/shard_map/ppermute | solution.py:83
  616.9 4.7 fusion.41
  624.3 4.1 add_convert_fusion.5
  628.4 5.1 collective-permute-start.28
  633.5 7.8 %collective-permute-done.30 = f32[1,91440]{1,0:T(1,128)S(1)} collective-permute-done((f32[1,91440]{1,0:T(1,128)S(1)}, f32[1,91440]{1,0:T(1,128)S(1)}, u32[]{:S(2)}, u32[]{:S(2)}) %collective-permute-start.30) | collective-permute-done | bytes 365792 | tf_op jit(solution)/shard_map/ppermute | solution.py:83
  643.8 5.9 collective-permute-done.28
  649.7 14.6 %collective-permute-done.29 = bf16[3328,128]{1,0:T(8,128)(2,1)} collective-permute-done((bf16[3328,128]{1,0:T(8,128)(2,1)}, bf16[3328,128]{1,0:T(8,128)(2,1)}, u32[]{:S(2)}, u32[]{:S(2)}) %collective-permute-start.29) | collective-permute-done | bytes 852000 | tf_op jit(solution)/shard_map/ppermute | solution.py:147
  665.5 3.3 fusion.10.late_ref
  669.2 2.7 collective-permute-done.35
  675.2 18.1 %update_tiles.1 = (f32[48,128,128]{2,1,0:T(8,128)}, f32[48,128,128]{2,1,0:T(8,128)}, f32[48,128,128]{2,1,0:T(8,128)}, f32[48,128,128]{2,1,0:T(8,128)}, bf16[48,128,128]{2,1,0:T(8,128)(2,1)}) custom-call(s32[48]{0:T(128)} %select_reduce_fusion.rows_ref, f32[3072,128]{1,0:T(8,128)} %fusion.14.early_ref, f32[3328,128]{1,0:T(8,128)} %fusion.10.late_ref, ...), custom_call_target="tpu_custom_call" | custom-call | flops 1811939328 | bytes 33030144 | tf_op jit(solution)/shard_map/update_tiles/pallas_call | solution.py:1027
  694.5 5.7 add_convert_fusion.own_ref
  702.3 4.0 pad_maximum_fusion
  706.3 4.8 collective-permute-done.38
  716.6 16.4 %input_grads.1 = f32[2048,2048]{1,0:T(8,128)} custom-call(s32[1]{0:T(128)} %bitcast.core_ref.half_ref, bf16[1024,2048]{1,0:T(8,128)(2,1)} %add_convert_fusion.own_ref, bf16[1024,2048]{1,0:T(8,128)(2,1)} %collective-permute-done.34.other_ref, bf16[2048,2048]{1,0:T(8,128)(2,1)} %tokens_ref.5, bf16[2048,2048]{1,0:T(8,128)(2,1)} %cot_ref.3, f32[1,2048]{1,0:T(1,128)} %bitcast.171), custom_call_target="tpu_custom_call" | custom-call | bytes 41943040 | tf_op jit(solution)/shard_map/input_grads/pallas_call | solution.py:867
  (362 shorter events, 110.5 us)
Async XLA Ops:
  7.2 132.7 %all-gather.4.cloned.1.call-start = ((), (), s32[]{:S(2)}) async-start(), calls=%async_computation.2 | async-start | bytes 9142272 | tf_op jit(solution)/shard_map/all_gather | solution.py:1166
  15.4 218.1 %all-gather.6.cloned.1.call-start = ((), (), s32[]{:S(2)}) async-start(), calls=%async_computation.3 | async-start | bytes 6488064 | tf_op jit(solution)/shard_map/all_gather | solution.py:1167
  18.3 27.0 %collective-permute-start = (f32[8,128]{1,0:T(8,128)S(1)}, f32[8,128]{1,0:T(8,128)S(1)}, u32[]{:S(2)}, u32[]{:S(2)}) collective-permute-start(f32[8,128]{1,0:T(8,128)S(1)} %broadcast_in_dim.140), channel_id=1, source_target_pairs={{0,1},{1,0},{2,3},{3,2},{4,5},{5,4},{6,7},{7,6},{8,9},{9,8},{10,11... | collective-permute-start | bytes 12296 | tf_op jit(solution)/shard_map/ppermute | solution.py:83
  45.3 3.7 collective-permute-start.1
  272.8 1.5 collective-permute-start.2
  275.2 4.3 collective-permute-start.3
  280.2 30.6 %copy-start.59 = (s32[384]{0:T(512)S(1)}, s32[384]{0:T(512)}, u32[]{:S(2)}) copy-start(s32[384]{0:T(512)} %get-tuple-element.407) | copy-start | bytes 4612
  280.2 31.2 %copy-start.48 = (s32[384]{0:T(512)S(1)}, s32[384]{0:T(512)}, u32[]{:S(2)}) copy-start(s32[384]{0:T(512)} %copy-done.47) | copy-start | bytes 4612
  280.2 31.2 %copy-start.55 = (s32[384]{0:T(512)S(1)}, s32[384]{0:T(512)}, u32[]{:S(2)}) copy-start(s32[384]{0:T(512)} %get-tuple-element.447) | copy-start | bytes 4612
  306.0 24.6 %collective-permute-start.4 = (bf16[1024,2048]{1,0:T(8,128)(2,1)}, bf16[1024,2048]{1,0:T(8,128)(2,1)}, u32[]{:S(2)}, u32[]{:S(2)}) collective-permute-start(bf16[1024,2048]{1,0:T(8,128)(2,1)} %get-tuple-element.221), channel_id=1, source_target_pairs={{0,1},{1,0},{2,3},{3,2},{4,5},{5,4},{6,7},{7,6},{8,9},{9,8},{10,11... | collective-permute-start | bytes 12582920 | tf_op jit(solution)/shard_map/ppermute | solution.py:83
  364.6 48.8 %collective-permute-start.6 = (bf16[512,2048]{1,0:T(8,128)(2,1)}, bf16[512,2048]{1,0:T(8,128)(2,1)}, u32[]{:S(2)}, u32[]{:S(2)}) collective-permute-start(bf16[512,2048]{1,0:T(8,128)(2,1)} %get-tuple-element.436), channel_id=1, source_target_pairs={{0,2},{1,3},{2,0},{3,1},{4,6},{5,7},{6,4},{7,5},{8,10},{9,11},{10,... | collective-permute-start | bytes 6291464 | tf_op jit(solution)/shard_map/ppermute | solution.py:83
  367.6 39.7 %collective-permute-start.5 = (bf16[6144,128]{1,0:T(8,128)(2,1)}, bf16[6144,128]{1,0:T(8,128)(2,1)S(1)}, u32[]{:S(2)}, u32[]{:S(2)}) collective-permute-start(bf16[6144,128]{1,0:T(8,128)(2,1)} %pad_maximum_fusion.2), channel_id=1, source_target_pairs={{0,4},{4,0},{8,12},{12,8},{16,20},{20,16},{24,28},{28,24},{1,5},{5... | collective-permute-start | bytes 4718600 | tf_op jit(solution)/shard_map/ppermute | solution.py:83
  403.8 51.2 %collective-permute-start.9 = (f32[1024,384]{1,0:T(8,128)}, f32[1024,384]{1,0:T(8,128)}, u32[]{:S(2)}, u32[]{:S(2)}) collective-permute-start(f32[1024,384]{1,0:T(8,128)} %get-tuple-element.242), channel_id=1, source_target_pairs={{0,1},{1,0},{2,3},{3,2},{4,5},{5,4},{6,7},{7,6},{8,9},{9,8},{10,11... | collective-permute-start | bytes 4718600 | tf_op jit(solution)/shard_map/ppermute | solution.py:83
  403.9 56.0 %collective-permute-start.10 = (bf16[512,2048]{1,0:T(8,128)(2,1)}, bf16[512,2048]{1,0:T(8,128)(2,1)}, u32[]{:S(2)}, u32[]{:S(2)}) collective-permute-start(bf16[512,2048]{1,0:T(8,128)(2,1)} %get-tuple-element.435), channel_id=1, source_target_pairs={{0,2},{1,3},{2,0},{3,1},{4,6},{5,7},{6,4},{7,5},{8,10},{9,11},{10,... | collective-permute-start | bytes 6291464 | tf_op jit(solution)/shard_map/ppermute | solution.py:83
  405.8 99.0 %collective-permute-start.14 = (bf16[6144,128]{1,0:T(8,128)(2,1)}, bf16[6144,128]{1,0:T(8,128)(2,1)}, u32[]{:S(2)}, u32[]{:S(2)}) collective-permute-start(bf16[6144,128]{1,0:T(8,128)(2,1)} %pad_maximum_fusion.3), channel_id=1, source_target_pairs={{0,4},{4,0},{8,12},{12,8},{16,20},{20,16},{24,28},{28,24},{1,5},{5... | collective-permute-start | bytes 4718600 | tf_op jit(solution)/shard_map/ppermute | solution.py:83
  414.7 37.9 %copy-start.33 = (f32[48,1024]{1,0:T(8,128)S(1)}, f32[48,1024]{1,0:T(8,128)}, u32[]{:S(2)}) copy-start(f32[48,1024]{1,0:T(8,128)} %get-tuple-element.274) | copy-start | bytes 589828
  414.7 38.9 %copy-start.39 = (f32[40,256]{1,0:T(8,128)S(1)}, f32[40,256]{1,0:T(8,128)}, u32[]{:S(2)}) copy-start(f32[40,256]{1,0:T(8,128)} %get-tuple-element.281) | copy-start | bytes 122884
  414.7 41.7 %copy-start.51 = (f32[16,128]{1,0:T(8,128)S(1)}, f32[16,128]{1,0:T(8,128)}, u32[]{:S(2)}) copy-start(f32[16,128]{1,0:T(8,128)} %get-tuple-element.277) | copy-start | bytes 24580
  414.8 45.1 %collective-permute-start.8 = (bf16[3072,128]{1,0:T(8,128)(2,1)S(1)}, bf16[3072,128]{1,0:T(8,128)(2,1)}, u32[]{:S(2)}, u32[]{:S(2)}) collective-permute-start(bf16[3072,128]{1,0:T(8,128)(2,1)S(1)} %fusion.13), channel_id=1, source_target_pairs={{0,8},{4,12},{24,16},{28,20},{1,9},{5,13},{25,17},{29,21},{2,10},{... | collective-permute-start | bytes 2359304 | tf_op jit(solution)/shard_map/ppermute | solution.py:147
  455.0 46.7 %collective-permute-start.15 = (f32[1024,384]{1,0:T(8,128)}, f32[1024,384]{1,0:T(8,128)}, u32[]{:S(2)}, u32[]{:S(2)}) collective-permute-start(f32[1024,384]{1,0:T(8,128)} %get-tuple-element.245), channel_id=1, source_target_pairs={{0,1},{1,0},{2,3},{3,2},{4,5},{5,4},{6,7},{7,6},{8,9},{9,8},{10,11... | collective-permute-start | bytes 4718600 | tf_op jit(solution)/shard_map/ppermute | solution.py:83
  463.1 41.7 %collective-permute-start.12 = (bf16[3072,128]{1,0:T(8,128)(2,1)}, bf16[3072,128]{1,0:T(8,128)(2,1)}, u32[]{:S(2)}, u32[]{:S(2)}) collective-permute-start(bf16[3072,128]{1,0:T(8,128)(2,1)} %fusion.16), channel_id=1, source_target_pairs={{0,8},{4,12},{8,16},{12,20},{1,9},{5,13},{9,17},{13,21},{2,10},{6,... | collective-permute-start | bytes 2359304 | tf_op jit(solution)/shard_map/ppermute | solution.py:147
  465.3 39.5 %collective-permute-start.13 = (bf16[3072,128]{1,0:T(8,128)(2,1)}, bf16[3072,128]{1,0:T(8,128)(2,1)}, u32[]{:S(2)}, u32[]{:S(2)}) collective-permute-start(bf16[3072,128]{1,0:T(8,128)(2,1)} %fusion.16), channel_id=1, source_target_pairs={{24,16},{28,20},{16,8},{20,12},{25,17},{29,21},{17,9},{21,13},{26,... | collective-permute-start | bytes 2359304 | tf_op jit(solution)/shard_map/ppermute | solution.py:147
  480.2 24.6 %collective-permute-start.16 = (bf16[1024,384]{1,0:T(8,128)(2,1)S(1)}, bf16[1024,384]{1,0:T(8,128)(2,1)S(1)}, u32[]{:S(2)}, u32[]{:S(2)}) collective-permute-start(bf16[1024,384]{1,0:T(8,128)(2,1)S(1)} %add_convert_fusion.12), channel_id=1, source_target_pairs={{0,2},{1,3},{2,0},{3,1},{4,6},{5,7},{6,4},{7,5},{8,10},{9,11},{10,... | collective-permute-start | bytes 2359304 | tf_op jit(solution)/shard_map/ppermute | solution.py:83
  501.8 68.8 %collective-permute-start.7 = (bf16[512,2048]{1,0:T(8,128)(2,1)}, bf16[512,2048]{1,0:T(8,128)(2,1)}, u32[]{:S(2)}, u32[]{:S(2)}) collective-permute-start(bf16[512,2048]{1,0:T(8,128)(2,1)} %get-tuple-element.413), channel_id=1, source_target_pairs={{0,1},{1,0},{2,3},{3,2},{4,5},{5,4},{6,7},{7,6},{8,9},{9,8},{10,11... | collective-permute-start | bytes 6291464 | tf_op jit(solution)/shard_map/ppermute | solution.py:83
  509.1 27.3 %collective-permute-start.18 = (bf16[3072,128]{1,0:T(8,128)(2,1)}, bf16[3072,128]{1,0:T(8,128)(2,1)}, u32[]{:S(2)}, u32[]{:S(2)}) collective-permute-start(bf16[3072,128]{1,0:T(8,128)(2,1)} %get-tuple-element.416), channel_id=1, source_target_pairs={{0,8},{4,12},{8,16},{12,20},{16,24},{20,28},{1,9},{5,13},{9,17},{1... | collective-permute-start | bytes 2359304 | tf_op jit(solution)/shard_map/ppermute | solution.py:147
  511.5 25.5 %collective-permute-start.19 = (bf16[3072,128]{1,0:T(8,128)(2,1)}, bf16[3072,128]{1,0:T(8,128)(2,1)}, u32[]{:S(2)}, u32[]{:S(2)}) collective-permute-start(bf16[3072,128]{1,0:T(8,128)(2,1)} %get-tuple-element.415), channel_id=1, source_target_pairs={{24,16},{28,20},{16,8},{20,12},{8,0},{12,4},{25,17},{29,21},{17,9}... | collective-permute-start | bytes 2359304 | tf_op jit(solution)/shard_map/ppermute | solution.py:147
  514.6 22.4 %collective-permute-start.17 = (bf16[3328,128]{1,0:T(8,128)(2,1)}, bf16[3328,128]{1,0:T(8,128)(2,1)}, u32[]{:S(2)}, u32[]{:S(2)}) collective-permute-start(bf16[3328,128]{1,0:T(8,128)(2,1)} %get-tuple-element.422), channel_id=1, source_target_pairs={{0,4},{4,0},{8,12},{12,8},{16,20},{20,16},{24,28},{28,24},{1,5},{5... | collective-permute-start | bytes 2555912 | tf_op jit(solution)/shard_map/ppermute | solution.py:83
  515.2 60.8 %collective-permute-start.21 = (bf16[3328,128]{1,0:T(8,128)(2,1)}, bf16[3328,128]{1,0:T(8,128)(2,1)}, u32[]{:S(2)}, u32[]{:S(2)}) collective-permute-start(bf16[3328,128]{1,0:T(8,128)(2,1)} %get-tuple-element.421), channel_id=1, source_target_pairs={{0,4},{4,0},{8,12},{12,8},{16,20},{20,16},{24,28},{28,24},{1,5},{5... | collective-permute-start | bytes 2555912 | tf_op jit(solution)/shard_map/ppermute | solution.py:83
  536.4 39.0 %collective-permute-start.22 = (bf16[1024,384]{1,0:T(8,128)(2,1)}, bf16[1024,384]{1,0:T(8,128)(2,1)}, u32[]{:S(2)}, u32[]{:S(2)}) collective-permute-start(bf16[1024,384]{1,0:T(8,128)(2,1)} %add_convert_fusion.11), channel_id=1, source_target_pairs={{0,2},{1,3},{2,0},{3,1},{4,6},{5,7},{6,4},{7,5},{8,10},{9,11},{10,... | collective-permute-start | bytes 2359304 | tf_op jit(solution)/shard_map/ppermute | solution.py:83
  537.0 43.3 %collective-permute-start.23 = (bf16[1024,2048]{1,0:T(8,128)(2,1)}, bf16[1024,2048]{1,0:T(8,128)(2,1)}, u32[]{:S(2)}, u32[]{:S(2)}) collective-permute-start(bf16[1024,2048]{1,0:T(8,128)(2,1)} %get-tuple-element.261), channel_id=1, source_target_pairs={{0,1},{1,0},{2,3},{3,2},{4,5},{5,4},{6,7},{7,6},{8,9},{9,8},{10,11... | collective-permute-start | bytes 12582920 | tf_op jit(solution)/shard_map/ppermute | solution.py:83
  541.1 34.9 %collective-permute-start.20 = (bf16[3328,128]{1,0:T(8,128)(2,1)}, bf16[3328,128]{1,0:T(8,128)(2,1)}, u32[]{:S(2)}, u32[]{:S(2)}) collective-permute-start(bf16[3328,128]{1,0:T(8,128)(2,1)} %fusion.17), channel_id=1, source_target_pairs={{0,8},{4,12},{24,16},{28,20},{1,9},{5,13},{25,17},{29,21},{2,10},{... | collective-permute-start | bytes 2555912 | tf_op jit(solution)/shard_map/ppermute | solution.py:147
  570.6 19.0 %collective-permute-start.11 = (bf16[512,2048]{1,0:T(8,128)(2,1)S(1)}, bf16[512,2048]{1,0:T(8,128)(2,1)S(1)}, u32[]{:S(2)}, u32[]{:S(2)}) collective-permute-start(bf16[512,2048]{1,0:T(8,128)(2,1)S(1)} %copy-done.4), channel_id=1, source_target_pairs={{0,1},{1,0},{2,3},{3,2},{4,5},{5,4},{6,7},{7,6},{8,9},{9,8},{10,11... | collective-permute-start | bytes 6291464 | tf_op jit(solution)/shard_map/ppermute | solution.py:83
  575.4 39.4 %collective-permute-start.26 = (bf16[6656,128]{1,0:T(8,128)(2,1)S(1)}, bf16[6656,128]{1,0:T(8,128)(2,1)S(1)}, u32[]{:S(2)}, u32[]{:S(2)}) collective-permute-start(bf16[6656,128]{1,0:T(8,128)(2,1)S(1)} %copy-done.18), channel_id=1, source_target_pairs={{0,4},{4,0},{8,12},{12,8},{16,20},{20,16},{24,28},{28,24},{1,5},{5... | collective-permute-start | bytes 5111816 | tf_op jit(solution)/shard_map/ppermute | solution.py:83
  578.0 38.4 %collective-permute-start.24 = (bf16[3328,128]{1,0:T(8,128)(2,1)S(1)}, bf16[3328,128]{1,0:T(8,128)(2,1)S(1)}, u32[]{:S(2)}, u32[]{:S(2)}) collective-permute-start(bf16[3328,128]{1,0:T(8,128)(2,1)S(1)} %fusion.12), channel_id=1, source_target_pairs={{0,8},{4,12},{8,16},{12,20},{1,9},{5,13},{9,17},{13,21},{2,10},{6,... | collective-permute-start | bytes 2555912 | tf_op jit(solution)/shard_map/ppermute | solution.py:147
  579.4 37.5 %collective-permute-start.25 = (bf16[3328,128]{1,0:T(8,128)(2,1)S(1)}, bf16[3328,128]{1,0:T(8,128)(2,1)S(1)}, u32[]{:S(2)}, u32[]{:S(2)}) collective-permute-start(bf16[3328,128]{1,0:T(8,128)(2,1)S(1)} %fusion.12), channel_id=1, source_target_pairs={{24,16},{28,20},{16,8},{20,12},{25,17},{29,21},{17,9},{21,13},{26,... | collective-permute-start | bytes 2555912 | tf_op jit(solution)/shard_map/ppermute | solution.py:147
  584.4 32.5 %slice-start = ((s8[8388608]{0:T(1024)(128)(4,1)}), s8[4194304]{0:T(1024)(128)(4,1)S(1)}, s32[]{:S(2)}) async-start(s8[8388608]{0:T(1024)(128)(4,1)} %bitcast.149), calls=%async_computation.4 | async-start | bytes 8388608
  588.1 28.8 %collective-permute-start.27 = (bf16[256,2048]{1,0:T(8,128)(2,1)S(1)}, bf16[256,2048]{1,0:T(8,128)(2,1)S(1)}, u32[]{:S(2)}, u32[]{:S(2)}) collective-permute-start(bf16[256,2048]{1,0:T(8,128)(2,1)S(1)} %get-tuple-element.430), channel_id=1, source_target_pairs={{0,2},{1,3},{2,0},{3,1},{4,6},{5,7},{6,4},{7,5},{8,10},{9,11},{10,... | collective-permute-start | bytes 3145736 | tf_op jit(solution)/shard_map/ppermute | solution.py:83
  593.7 50.1 %collective-permute-start.31 = (bf16[256,2048]{1,0:T(8,128)(2,1)}, bf16[256,2048]{1,0:T(8,128)(2,1)}, u32[]{:S(2)}, u32[]{:S(2)}) collective-permute-start(bf16[256,2048]{1,0:T(8,128)(2,1)} %get-tuple-element.429), channel_id=1, source_target_pairs={{0,2},{1,3},{2,0},{3,1},{4,6},{5,7},{6,4},{7,5},{8,10},{9,11},{10,... | collective-permute-start | bytes 3145736 | tf_op jit(solution)/shard_map/ppermute | solution.py:83
  614.9 78.5 %collective-permute-start.32 = (bf16[256,2048]{1,0:T(8,128)(2,1)}, bf16[256,2048]{1,0:T(8,128)(2,1)}, u32[]{:S(2)}, u32[]{:S(2)}) collective-permute-start(bf16[256,2048]{1,0:T(8,128)(2,1)} %get-tuple-element.427), channel_id=1, source_target_pairs={{0,2},{1,3},{2,0},{3,1},{4,6},{5,7},{6,4},{7,5},{8,10},{9,11},{10,... | collective-permute-start | bytes 3145736 | tf_op jit(solution)/shard_map/ppermute | solution.py:83
  616.4 77.8 %collective-permute-start.33 = (bf16[256,2048]{1,0:T(8,128)(2,1)}, bf16[256,2048]{1,0:T(8,128)(2,1)}, u32[]{:S(2)}, u32[]{:S(2)}) collective-permute-start(bf16[256,2048]{1,0:T(8,128)(2,1)} %get-tuple-element.428), channel_id=1, source_target_pairs={{0,2},{1,3},{2,0},{3,1},{4,6},{5,7},{6,4},{7,5},{8,10},{9,11},{10,... | collective-permute-start | bytes 3145736 | tf_op jit(solution)/shard_map/ppermute | solution.py:83
  623.2 18.1 %collective-permute-start.30 = (f32[1,91440]{1,0:T(1,128)S(1)}, f32[1,91440]{1,0:T(1,128)S(1)}, u32[]{:S(2)}, u32[]{:S(2)}) collective-permute-start(f32[1,91440]{1,0:T(1,128)S(1)} %broadcast_in_dim.147), channel_id=1, source_target_pairs={{0,16},{4,20},{8,24},{12,28},{16,0},{20,4},{24,8},{28,12},{1,17},{... | collective-permute-start | bytes 1097288 | tf_op jit(solution)/shard_map/ppermute | solution.py:83
  628.4 21.3 %collective-permute-start.28 = (bf16[3328,128]{1,0:T(8,128)(2,1)}, bf16[3328,128]{1,0:T(8,128)(2,1)}, u32[]{:S(2)}, u32[]{:S(2)}) collective-permute-start(bf16[3328,128]{1,0:T(8,128)(2,1)} %get-tuple-element.418), channel_id=1, source_target_pairs={{0,8},{4,12},{8,16},{12,20},{16,24},{20,28},{1,9},{5,13},{9,17},{1... | collective-permute-start | bytes 2555912 | tf_op jit(solution)/shard_map/ppermute | solution.py:147
  641.2 23.1 %collective-permute-start.29 = (bf16[3328,128]{1,0:T(8,128)(2,1)}, bf16[3328,128]{1,0:T(8,128)(2,1)}, u32[]{:S(2)}, u32[]{:S(2)}) collective-permute-start(bf16[3328,128]{1,0:T(8,128)(2,1)} %get-tuple-element.417), channel_id=1, source_target_pairs={{24,16},{28,20},{16,8},{20,12},{8,0},{12,4},{25,17},{29,21},{17,9}... | collective-permute-start | bytes 2555912 | tf_op jit(solution)/shard_map/ppermute | solution.py:147
  665.5 6.4 collective-permute-start.35
  674.6 18.8 %collective-permute-start.36 = (f32[1,30000]{1,0:T(1,128)S(1)}, f32[1,30000]{1,0:T(1,128)S(1)}, u32[]{:S(2)}, u32[]{:S(2)}) collective-permute-start(f32[1,30000]{1,0:T(1,128)S(1)} %broadcast_in_dim.156), channel_id=1, source_target_pairs={{0,4},{4,0},{8,12},{12,8},{16,20},{20,16},{24,28},{28,24},{1,5},{5... | collective-permute-start | bytes 360008 | tf_op jit(solution)/shard_map/ppermute | solution.py:83
  694.1 6.1 collective-permute-start.37
  700.2 16.3 %collective-permute-start.34 = (bf16[1024,2048]{1,0:T(8,128)(2,1)}, bf16[1024,2048]{1,0:T(8,128)(2,1)}, u32[]{:S(2)}, u32[]{:S(2)}) collective-permute-start(bf16[1024,2048]{1,0:T(8,128)(2,1)} %add_convert_fusion.own_ref), channel_id=1, source_target_pairs={{0,1},{1,0},{2,3},{3,2},{4,5},{5,4},{6,7},{7,6},{8,9},{9,8},{10,11... | collective-permute-start | bytes 12582920 | tf_op jit(solution)/shard_map/ppermute | solution.py:83
  700.6 10.5 %collective-permute-start.38 = (f32[1,85248]{1,0:T(1,128)S(1)}, f32[1,85248]{1,0:T(1,128)S(1)}, u32[]{:S(2)}, u32[]{:S(2)}) collective-permute-start(f32[1,85248]{1,0:T(1,128)S(1)} %reshape_add_fusion), channel_id=1, source_target_pairs={{0,2},{1,3},{2,0},{3,1},{4,6},{5,7},{6,4},{7,5},{8,10},{9,11},{10,... | collective-permute-start | bytes 1022984 | tf_op jit(solution)/shard_map/ppermute | solution.py:83
  (58 other events, 689.8 us)
Sparse Core Ops, SparseCore 0:
  15.5 124.2 all-gather.3
  142.6 90.8 all-gather.5

commit v2 on v1

--- a/solution.py
+++ b/solution.py
@@ -96,23 +96,22 @@
         self.owned, self.shared = owned, shared
         self.bit = lax.axis_size("dp") // 2
 
-    def exchange(self):
-        if self.bit == 0:
-            return
+    def send(self):
         upper = (lax.axis_index("dp") // self.bit) % 2
         pairs = self.owned.reshape(2, -1, self.owned.shape[1])
         sent = lax.dynamic_index_in_dim(pairs, 1 - upper, 0, keepdims=False)
-        kept = lax.dynamic_index_in_dim(pairs, upper, 0, keepdims=False)
-        arrived = swap(
-            jnp.concatenate([sent.reshape(-1), self.shared])[None], "dp", self.bit
-        )[0]
-        self.owned = kept + arrived[: kept.size].reshape(kept.shape)
-        self.shared = self.shared + arrived[kept.size :]
+        self.kept = lax.dynamic_index_in_dim(pairs, upper, 0, keepdims=False)
+        return swap(jnp.concatenate([sent.reshape(-1), self.shared])[None], "dp", self.bit)
+
+    def add(self, arrived):
+        size = self.kept.size
+        self.owned = self.kept + arrived[0, :size].reshape(self.kept.shape)
+        self.shared = self.shared + arrived[0, size:]
         self.bit //= 2
 
-    def exchange_rest(self):
+    def finish(self):
         while self.bit > 0:
-            self.exchange()
+            self.add(self.send())
 
 
 class OwnerSum:
@@ -164,8 +163,9 @@
 
     def third(self, other):
         if self.lined:
-            self.up, self.down, self.groups[-1], other = tied(
-                self.up, self.down, self.groups[-1], other
+            needed = self.found[2][0]
+            self.up, self.down, self.groups[needed], other = tied(
+                self.up, self.down, self.groups[needed], other
             )
             near, far = self.pair_sum(2), self.pair_sum(0)
             up = jnp.where(self.low, near, far) + self.up.astype(F32)
@@ -178,7 +178,9 @@
         if not self.lined:
             flat = self.grads.reshape(-1, TILE)
             return lax.psum_scatter(flat, "dp", scatter_dimension=0, tiled=True).astype(F32), other
-        self.up, self.down, other = tied(self.up, self.down, other)
+        self.up, self.down, self.groups[-1], other = tied(
+            self.up, self.down, self.groups[-1], other
+        )
         return self.pair_sum(3) + (self.up.astype(F32) + self.down.astype(F32)), other
 
 
@@ -1285,22 +1287,20 @@
     ]
     d_rest, side_chips[0] = tied(d_rest, side_chips[0])
     side_others = [swap(side_chips[0], "tensor", 2)]
+    d_sent, pre_sent = normed_grad(1 - core_at, 16, d_gate, d_rest, tokens, w_gate, w_rest)
+    d_sent, side_chips[1], side_others[0], d_rest = early.third(
+        (d_sent, side_chips[1], side_others[0], d_rest)
+    )
+    side_others.append(swap(side_chips[1], "tensor", 2))
+    d_kept, pre_kept = normed_grad(core_at, 0, d_gate, d_rest, tokens, w_gate, w_rest)
+    early_share, (d_kept, side_others[1]) = early.total((d_kept, side_others[1]))
+    grad_pre = jnp.sum(pre_sent + pre_kept, axis=0)
+    d_chip, d_rest = tied(chip_sum(d_kept, d_sent), d_rest)
+    d_others = [swap(part, "tensor", 2) for part in jnp.split(d_chip, 4)]
     grad_input = contract_rows(normed, d_rest[:, :di_local]).astype(BF16)
     late_grads = spread(plans[1][0], (grad_gate, grad_input, grad_output), n_dp * plans[1][1])
-    late_grads, side_chips[1], side_others[0], d_rest = early.third(
-        (late_grads, side_chips[1], side_others[0], d_rest)
-    )
-    side_others.append(swap(side_chips[1], "tensor", 2))
-    late = OwnerSum(late_grads, ((0,), (1,), (2, 3)))
-    d_sent, pre_sent = normed_grad(1 - core_at, 16, d_gate, d_rest, tokens, w_gate, w_rest)
-    early_share, (d_sent, d_rest) = early.total((d_sent, d_rest))
-    d_sent, d_rest = late.first((d_sent, d_rest))
-    d_kept, pre_kept = normed_grad(core_at, 0, d_gate, d_rest, tokens, w_gate, w_rest)
-    d_kept, side_others[1] = late.second((d_kept, side_others[1]))
-    grad_pre = jnp.sum(pre_sent + pre_kept, axis=0)
-    d_chip = chip_sum(d_kept, d_sent)
-    d_others = [swap(part, "tensor", 2) for part in jnp.split(d_chip, 4)]
-    d_others[0], early_share = late.third((d_others[0], early_share))
+    late_grads, d_others[0] = tied(late_grads, d_others[0])
+    late = OwnerSum(late_grads, ((0,), (1,), (2,), (3,)))
 
     side_total = jnp.concatenate(
         [
@@ -1309,7 +1309,9 @@
         ],
         axis=0,
     )
-    side_total, d_others[0] = tied(side_total, d_others[0])
+    side_total, d_others[1], out_chip, out_others, early_share, grad_pre = late.first(
+        (side_total, d_others[1], out_chip, out_others, early_share, grad_pre)
+    )
     grad_side = lax.dynamic_index_in_dim(
         contract_rows(normed, side_total).reshape(n_dp, n_tensor, -1, side_total.shape[1]),
         tensor_rank,
@@ -1331,10 +1333,19 @@
     small_sums = SharedSums(
         grad_side.reshape(n_dp, -1), jnp.concatenate([own_vector, grad_pre, gbc_sums.reshape(-1)])
     )
-    small_sums.exchange()
-    late_share, (small_sums.owned, d_others[1]) = late.total((small_sums.owned, d_others[1]))
-    small_sums.exchange_rest()
-    late_share, misfit = tied(late_share, misfit)
+    arrived, d_others[2] = late.second((small_sums.send(), d_others[2]))
+    small_sums.add(arrived)
+    arrived, d_others[3] = late.third((small_sums.send(), d_others[3]))
+    small_sums.add(arrived)
+    d_half = (d_chip.astype(F32) + jnp.concatenate(d_others).astype(F32)).astype(BF16)
+    input_grad = input_grads(
+        core_at, d_half, swap(d_half, "tensor", 1), tokens, cotangent, pre_gain[None, :]
+    )
+    late_share, (arrived, input_grad, misfit) = late.total(
+        (small_sums.send(), input_grad, misfit)
+    )
+    small_sums.add(arrived)
+    small_sums.finish()
 
     def repaired(grads):
         again = spread(plans[2][0], grads, n_dp * plans[2][1])
@@ -1358,7 +1369,6 @@
         left_roots[0],
         right_roots[0],
     )
-    tiles_copy, d_others[2] = tied(tiles_copy, d_others[2])
     split_at = own_vector.shape[0]
     side_own, all_vector = small_sums.owned, small_sums.shared
     quarters = jnp.where(
@@ -1385,10 +1395,6 @@
         axis=0,
     )
 
-    d_half = (d_chip.astype(F32) + jnp.concatenate(d_others).astype(F32)).astype(BF16)
-    d_half_other = swap(d_half, "tensor", 1)
-    input_grad = input_grads(core_at, d_half, d_half_other, tokens, cotangent, pre_gain[None, :])
-
     pre_share = lax.dynamic_slice_in_dim(common[:D], tensor_rank * model_local, model_local, 0)
     bc_share = lax.dynamic_slice_in_dim(
         common[D:].reshape(CONV + 1, 2 * NS), tensor_rank * bc_local, bc_local, 1

time: 745 us -> 733 us (0.984)
  waiting for transfers between devices: 193 us -> 168 us
    ppermute x10, waiting for transfers between devices: 20.6 us -> 0.03 us  [hop(): return lax.ppermute(value.astype(BF16), 'dp', pairs)]
    ppermute x29 -> x30, waiting for transfers between devices: 47.3 us -> 43.1 us  [swap(): return lax.ppermute(value, axis, [(i, i ^ bit) for i in range(size)])]
    ppermute x29 -> x30, starting transfers between devices: 20.8 us -> 20.7 us  [swap(): return lax.ppermute(value, axis, [(i, i ^ bit) for i in range(size)])]
  transfers between devices with their start and end apart: 41 -> 42, of which waited for: 12 -> 12; matrix products, arithmetic and copies ran while one was open for 21% -> 20% of each run, Pallas kernels for 26% -> 29%
where the time goes in v2:
time: 733 us; the launch traced here: 727 us
  Pallas kernels  283 us (39%)
  waiting for transfers between devices  168 us (23%)
  other arithmetic  112 us (15%)
  starting transfers between devices  52.1 us (7%)
  matrix products  45.5 us (6%)
  local copies, waits for them, and re-layouts  42.7 us (6%)
  between operations  17.4 us (2%)
    all_gather x1, waiting for transfers between devices, on_device(): first_held = lax.all_gather(first_share, 'dp', axis=0, tiled=True)  90.3 us
    pallas_call x2, Pallas kernels, ssd_backward(): pl.pallas_call(ssd_backward_kernel, grid=(blocks,), in_specs=[pl.BlockSpe...  69.2 us
    dot_general x4, matrix products, contract_rows(): lax.dot_general(left, right, (((0,), (0,)), ((), ())), preferred_element_...  45.5 us
    ppermute x30, waiting for transfers between devices, swap(): return lax.ppermute(value, axis, [(i, i ^ bit) for i in range(size)])  43.1 us
    pallas_call x2, Pallas kernels, normed_grad(): pl.pallas_call(normed_grad_kernel, grid_spec=pltpu.PrefetchScalarGridSpec...  38.9 us
    all_gather x1, waiting for transfers between devices, on_device(): second_held = lax.all_gather(mine[cut:], 'dp', axis=0, tiled=True)  34.3 us
    ppermute x10, starting transfers between devices, hop(): return lax.ppermute(value.astype(BF16), 'dp', pairs)  31.4 us
    pallas_call x1, Pallas kernels, ssd_forward(): pl.pallas_call(ssd_forward_kernel, grid=(sequences, blocks), in_specs=[pl...  28 us
  transfers between devices with their start and end apart: 42, of which 12 were waited for; matrix products, arithmetic and copies ran while one was open for 20% of the time, Pallas kernels for 29%

profile of v2, /device:TPU:0, one launch (start us, length us, event | category | flops | bytes accessed | tf_op | source)
XLA Modules:
  0.0 727.4 jit_solution(11990393853431121938)
XLA Ops:
  18.9 6.3 all-gather
  28.1 5.1 fusion.2
  36.4 8.8 %fusion.4.left_ref.normed_ref = bf16[2048,2048]{1,0:T(8,128)(2,1)} fusion(bf16[2048,2048]{1,0:T(8,128)(2,1)} %tokens_ref.5, f32[2048]{0:T(1024)S(1)} %bitcast.170, f32[2048]{0:T(1024)S(1)} %add_rsqrt_fusion), kind=kLoop, calls=%fused_computation.7 | loop fusion | flops 16777216 | bytes 16793600 | tf_op jit(solution)/shard_map/convert_element_type | solution.py:1205
  49.6 90.3 %all-gather.4.cloned.1.call-done.refs_0_ = bf16[31744,128]{1,0:T(8,128)(2,1)} async-done(((bf16[3968,128]{1,0:T(8,128)(2,1)}), bf16[31744,128]{1,0:T(8,128)(2,1)}) %all-gather.4.cloned.1.call-update) | async-done | bytes 8126480 | tf_op jit(solution)/shard_map/all_gather | solution.py:1168
  143.4 7.7 %assemble.3.right_ref = bf16[2048,1536]{1,0:T(8,128)(2,1)} custom-call(s32[128]{0:T(128)} %get-tuple-element.467.rows_ref, bf16[31744,128]{1,0:T(8,128)(2,1)} %all-gather.4.cloned.1.call-done.refs_0_, bf16[2048,512]{1,0:T(8,128)(2,1)S(1)} %maximum_maximum_fusion.refs_1_), custom_call_target="tpu_custom_call" | custom-call | bytes 16252928 | tf_op jit(solution)/shard_map/assemble/pallas_call | solution.py:942
  151.1 18.8 %project.2.rest_ref.prev_ref = f32[2048,1536]{1,0:T(8,128)} custom-call(bf16[2048,2048]{1,0:T(8,128)(2,1)} %fusion.4.left_ref.normed_ref, bf16[2048,1536]{1,0:T(8,128)(2,1)} %assemble.3.right_ref), custom_call_target="tpu_custom_call" | custom-call | flops 12884901888 | bytes 27262976 | tf_op jit(solution)/shard_map/project/pallas_call | solution.py:617
  171.2 28.0 %ssd_forward.2 = (f32[2048,1024]{1,0:T(8,128)}, f32[16,128,1024]{2,1,0:T(8,128)}) custom-call(f32[2048,1536]{1,0:T(8,128)} %project.2.rest_ref.prev_ref, f32[2048,1536]{1,0:T(8,128)} %project.2.rest_ref.prev_ref, f32[2048,128]{1,0:T(8,128)} %broadcast_in_dim.141.start_ref.refs_5_.refs_6_, f32[8,1024]{1,0:T(8,128)S(1)} %concatenate.78.par_ref.refs_8_.refs_9_, ...), custom_call_target="tpu_custom_call" | custom-call | flops 10737418240 | bytes 41943040 | tf_op jit(solution)/shard_map/ssd_forward/pallas_call | solution.py:503
  199.1 34.3 %all-gather.6.cloned.1.call-done.refs_1_ = bf16[22528,128]{1,0:T(8,128)(2,1)} async-done(((bf16[2816,128]{1,0:T(8,128)(2,1)}), bf16[22528,128]{1,0:T(8,128)(2,1)}) %all-gather.6.cloned.1.call-update) | async-done | bytes 5767184 | tf_op jit(solution)/shard_map/all_gather | solution.py:1169
  234.5 12.0 %assemble.4 = (bf16[2048,1024]{1,0:T(8,128)(2,1)}, bf16[1024,2048]{1,0:T(8,128)(2,1)}) custom-call(s32[256]{0:T(256)} %pad_add_fusion.rows_ref, bf16[31744,128]{1,0:T(8,128)(2,1)} %get-tuple-element.535, bf16[22528,128]{1,0:T(8,128)(2,1)} %get-tuple-element.537), custom_call_target="tpu_custom_call" | custom-call | bytes 27787264 | tf_op jit(solution)/shard_map/assemble/pallas_call | solution.py:942
  246.5 26.3 %gate_project.1 = (f32[2048,1024]{1,0:T(8,128)}, f32[2048,1024]{1,0:T(8,128)}, f32[8,2048]{1,0:T(8,128)}) custom-call(bf16[2048,2048]{1,0:T(8,128)(2,1)} %get-tuple-element.540, bf16[2048,2048]{1,0:T(8,128)(2,1)} %cot_ref.3, bf16[2048,1024]{1,0:T(8,128)(2,1)} %get-tuple-element.221.wgate_ref, bf16[1024,2048]{1,0:T(8,128)(2,1)} %get-tuple-element.222.wout_ref, ...), custom_call_target="tpu_custom_call" | custom-call | flops 17179869184 | bytes 33554432 | tf_op jit(solution)/shard_map/gate_project/pallas_call | solution.py:656
  276.6 2.8 collective-permute-done.3
  280.0 25.6 %gated_pass.1 = (bf16[2048,1024]{1,0:T(8,128)(2,1)}, bf16[2048,1024]{1,0:T(8,128)(2,1)}, f32[2048,1024]{1,0:T(8,128)}, f32[8,1024]{1,0:T(8,128)}, bf16[1024,2048...) custom-call(s32[1]{0:T(128)} %bitcast.core_ref.half_ref, f32[2048,1024]{1,0:T(8,128)} %get-tuple-element.220.ssd_ref, ...), custom_call_target="tpu_custom_call" | custom-call | flops 8589934592 | bytes 41943040 | tf_op jit(solution)/shard_map/gated_pass/pallas_call | solution.py:743
  308.0 14.4 %convolution_convert_fusion.refs_1_.refs_2_ = bf16[1024,2048]{1,0:T(8,128)(2,1)} fusion(bf16[2048,1024]{1,0:T(8,128)(2,1)} %get-tuple-element.231, bf16[2048,2048]{1,0:T(8,128)(2,1)} %cot_ref.3), kind=kOutput, calls=%fused_computation.19 | convolution fusion | flops 8592031744 | bytes 16777216 | tf_op jit(solution)/shard_map/dot_general | solution.py:74
  322.4 6.2 add_convert_fusion.2
  328.6 13.0 %convolution_convert_fusion.1.refs_0_ = bf16[2048,1024]{1,0:T(8,128)(2,1)} fusion(bf16[2048,2048]{1,0:T(8,128)(2,1)} %get-tuple-element.540, bf16[2048,1024]{1,0:T(8,128)(2,1)S(1)} %copy-done.6), kind=kOutput, calls=%fused_computation.20 | convolution fusion | flops 8592031744 | bytes 16777216 | tf_op jit(solution)/shard_map/dot_general | solution.py:74
  341.6 9.8 %spread.4 = bf16[24576,128]{1,0:T(8,128)(2,1)} custom-call(s32[256]{0:T(256)} %pad_add_fusion.1.rows_ref, bf16[2048,1024]{1,0:T(8,128)(2,1)} %convolution_convert_fusion.1.refs_0_, bf16[1024,2048]{1,0:T(8,128)(2,1)} %convolution_convert_fusion.refs_1_.refs_2_), custom_call_target="tpu_custom_call" | custom-call | bytes 14680064 | tf_op jit(solution)/shard_map/spread/pallas_call | solution.py:976
  351.5 5.0 fusion.36
  361.3 34.6 %ssd_backward.2 = (bf16[2048,1536]{1,0:T(8,128)(2,1)}, f32[1024,384]{1,0:T(8,128)}, f32[48,1024]{1,0:T(8,128)}, f32[40,256]{1,0:T(8,128)}, f32[16,128]{1,0:T(8,128)}) custom-call(s32[1]{0:T(128)} %bitcast.16.refs_0_.refs_1_, f32[2048,1536]{1,0:T(8,128)} %get-tuple-element.233.refs_1_.refs_2_.refs_3_, ...), custom_call_target="tpu_custom_call" | custom-call | flops 13421772800 | bytes 20971520 | tf_op jit(solution)/shard_map/ssd_backward/pallas_call | solution.py:547
  399.2 6.0 collective-permute-done.6
  406.6 3.2 collective-permute-start.7
  409.8 34.6 %ssd_backward.3 = (bf16[2048,1536]{1,0:T(8,128)(2,1)}, f32[1024,384]{1,0:T(8,128)}, f32[48,1024]{1,0:T(8,128)}, f32[40,256]{1,0:T(8,128)}, f32[16,128]{1,0:T(8,128)}) custom-call(bf16[2048,1536]{1,0:T(8,128)(2,1)} %get-tuple-element.239.refs_0_, s32[1]{0:T(128)} %bitcast.16.refs_0_.refs_1_, ...), custom_call_target="tpu_custom_call", output_to_operand_aliasing={{0}: (0, {})} | custom-call | flops 13421772800 | bytes 20971520 | tf_op jit(solution)/shard_map/ssd_backward/pallas_call | solution.py:547
  452.1 3.0 collective-permute-start.10
  458.2 19.3 %normed_grad.2 = (bf16[1024,2048]{1,0:T(8,128)(2,1)}, f32[8,2048]{1,0:T(8,128)}) custom-call(s32[1]{0:T(128)S(6)} %sub.101.half_ref, bf16[2048,1024]{1,0:T(8,128)(2,1)} %get-tuple-element.229.dgate_ref, bf16[2048,1536]{1,0:T(8,128)(2,1)} %get-tuple-element.261.drest_ref, bf16[2048,2048]{1,0:T(8,128)(2,1)} %tokens_ref.5, ...), custom_call_target="tpu_custom_call" | custom-call | flops 171798691840 | bytes 402653184 | tf_op jit(solution)/shard_map/normed_grad/pallas_call | solution.py:804
  480.2 4.0 add_convert_fusion.9
  489.0 19.6 %normed_grad.3 = (bf16[1024,2048]{1,0:T(8,128)(2,1)}, f32[8,2048]{1,0:T(8,128)}) custom-call(s32[1]{0:T(128)} %bitcast.core_ref.half_ref, bf16[2048,1024]{1,0:T(8,128)(2,1)} %get-tuple-element.229.dgate_ref, bf16[2048,1536]{1,0:T(8,128)(2,1)} %get-tuple-element.261.drest_ref, bf16[2048,2048]{1,0:T(8,128)(2,1)} %tokens_ref.5, ...), custom_call_target="tpu_custom_call" | custom-call | tf_op jit(solution)/shard_map/normed_grad/pallas_call | solution.py:804
  513.5 6.1 add_convert_fusion.1
  524.7 11.1 %fusion.7.refs_1_ = bf16[2048,1024]{1,0:T(8,128)(2,1)} fusion(bf16[2048,2048]{1,0:T(8,128)(2,1)S(1)} %bitcast.150, bf16[2048,1536]{1,0:T(8,128)(2,1)S(1)} %bitcast.147), kind=kOutput, calls=%fused_computation.18 | convolution fusion | flops 8592031744 | bytes 16777216 | tf_op jit(solution)/shard_map/dot_general | solution.py:74
  535.8 11.5 %spread.5 = bf16[26624,128]{1,0:T(8,128)(2,1)} custom-call(s32[384]{0:T(512)} %get-tuple-element.462.rows_ref, bf16[2048,1024]{1,0:T(8,128)(2,1)} %convolution_convert_fusion.1.refs_0_, bf16[2048,1024]{1,0:T(8,128)(2,1)} %fusion.7.refs_1_, bf16[1024,2048]{1,0:T(8,128)(2,1)} %convolution_convert_fusion.refs_1_.refs_2_), custom_call_target="tpu_custom_call" | custom-call | bytes 19398656 | tf_op jit(solution)/shard_map/spread/pallas_call | solution.py:976
  548.7 3.8 dynamic-slice_bitcast_fusion
  553.8 2.9 fusion.14.early_ref
  559.1 12.1 %collective-permute-done.21 = bf16[256,2048]{1,0:T(8,128)(2,1)} collective-permute-done((bf16[256,2048]{1,0:T(8,128)(2,1)}, bf16[256,2048]{1,0:T(8,128)(2,1)}, u32[]{:S(2)}, u32[]{:S(2)}) %collective-permute-start.21) | collective-permute-done | bytes 1048608 | tf_op jit(solution)/shard_map/ppermute | solution.py:83
  571.2 3.2 collective-permute-done.20
  574.4 7.0 fusion.41
  584.3 6.2 collective-permute-start.24
  602.5 8.2 %collective-permute-done.26 = f32[1,91440]{1,0:T(1,128)S(1)} collective-permute-done((f32[1,91440]{1,0:T(1,128)S(1)}, f32[1,91440]{1,0:T(1,128)S(1)}, u32[]{:S(2)}, u32[]{:S(2)}) %collective-permute-start.26) | collective-permute-done | bytes 365792 | tf_op jit(solution)/shard_map/ppermute | solution.py:83
  611.7 2.9 fusion.12
  614.6 6.1 collective-permute-start.28
  623.4 7.3 %add_convert_fusion.4 = (bf16[512,2048]{1,0:T(8,128)(2,1)}, bf16[512,2048]{1,0:T(8,128)(2,1)S(1)}) fusion(bf16[512,2048]{1,0:T(8,128)(2,1)} %collective-permute-done.6, bf16[1024,2048]{1,0:T(8,128)(2,1)} %add_convert_fusion.2, bf16[2048,2048]{1,0:T(8,128)(2,1)} %tokens_ref.5, s32[]{:T(128)S(6)} %select_n.295, bf16[512,2048]{1,0:T(8,128)(2,1)} %collective-permute-done.9, ...), kind=kLoop, calls=%fused_computation.15 | loop fusion | flops 12582912 | bytes 16777224 | tf_op jit(solution)/shard_map/convert_element_type | solution.py:1387
  631.3 4.2 collective-permute-done.31
  635.6 4.8 add_convert_fusion.own_ref
  645.4 4.2 add_convert_fusion.5
  649.6 4.4 collective-permute-start.33
  655.3 4.5 broadcast_select_fusion.3
  660.4 3.9 broadcast_select_fusion.2
  664.3 16.5 %input_grads.1 = f32[2048,2048]{1,0:T(8,128)} custom-call(s32[1]{0:T(128)} %bitcast.core_ref.half_ref, bf16[1024,2048]{1,0:T(8,128)(2,1)} %add_convert_fusion.own_ref, bf16[1024,2048]{1,0:T(8,128)(2,1)} %collective-permute-done.37.other_ref, bf16[2048,2048]{1,0:T(8,128)(2,1)} %tokens_ref.5, bf16[2048,2048]{1,0:T(8,128)(2,1)} %cot_ref.3, f32[1,2048]{1,0:T(1,128)} %bitcast.171), custom_call_target="tpu_custom_call" | custom-call | bytes 41943040 | tf_op jit(solution)/shard_map/input_grads/pallas_call | solution.py:869
  683.6 6.2 pad_maximum_fusion
  691.7 3.3 fusion.10.late_ref
  695.1 18.4 %update_tiles.1 = (f32[48,128,128]{2,1,0:T(8,128)}, f32[48,128,128]{2,1,0:T(8,128)}, f32[48,128,128]{2,1,0:T(8,128)}, f32[48,128,128]{2,1,0:T(8,128)}, bf16[48,128,128]{2,1,0:T(8,128)(2,1)}) custom-call(s32[48]{0:T(128)} %select_reduce_fusion.rows_ref, f32[3072,128]{1,0:T(8,128)} %fusion.14.early_ref, f32[3328,128]{1,0:T(8,128)} %fusion.10.late_ref, ...), custom_call_target="tpu_custom_call" | custom-call | flops 1811939328 | bytes 33030144 | tf_op jit(solution)/shard_map/update_tiles/pallas_call | solution.py:1029
  (350 shorter events, 112.5 us)
Async XLA Ops:
  7.2 132.7 %all-gather.4.cloned.1.call-start = ((), (), s32[]{:S(2)}) async-start(), calls=%async_computation.2 | async-start | bytes 9142272 | tf_op jit(solution)/shard_map/all_gather | solution.py:1168
  15.4 218.0 %all-gather.6.cloned.1.call-start = ((), (), s32[]{:S(2)}) async-start(), calls=%async_computation.3 | async-start | bytes 6488064 | tf_op jit(solution)/shard_map/all_gather | solution.py:1169
  18.3 27.0 %collective-permute-start = (f32[8,128]{1,0:T(8,128)S(1)}, f32[8,128]{1,0:T(8,128)S(1)}, u32[]{:S(2)}, u32[]{:S(2)}) collective-permute-start(f32[8,128]{1,0:T(8,128)S(1)} %broadcast_in_dim.140), channel_id=1, source_target_pairs={{0,1},{1,0},{2,3},{3,2},{4,5},{5,4},{6,7},{7,6},{8,9},{9,8},{10,11... | collective-permute-start | bytes 12296 | tf_op jit(solution)/shard_map/ppermute | solution.py:83
  45.3 3.7 collective-permute-start.1
  272.8 1.5 collective-permute-start.2
  275.1 4.3 collective-permute-start.3
  280.0 26.4 %copy-start.43 = (s32[2,1024]{1,0:T(2,128)S(1)}, s32[2,1024]{1,0:T(2,128)}, u32[]{:S(2)}) copy-start(s32[2,1024]{1,0:T(2,128)} %get-tuple-element.377) | copy-start | bytes 24580
  280.0 26.4 %copy-start.50 = (s32[384]{0:T(512)S(1)}, s32[384]{0:T(512)}, u32[]{:S(2)}) copy-start(s32[384]{0:T(512)} %get-tuple-element.419) | copy-start | bytes 4612
  305.7 16.7 %collective-permute-start.4 = (bf16[1024,2048]{1,0:T(8,128)(2,1)}, bf16[1024,2048]{1,0:T(8,128)(2,1)}, u32[]{:S(2)}, u32[]{:S(2)}) collective-permute-start(bf16[1024,2048]{1,0:T(8,128)(2,1)} %get-tuple-element.227), channel_id=1, source_target_pairs={{0,1},{1,0},{2,3},{3,2},{4,5},{5,4},{6,7},{7,6},{8,9},{9,8},{10,11... | collective-permute-start | bytes 12582920 | tf_op jit(solution)/shard_map/ppermute | solution.py:83
  356.4 48.8 %collective-permute-start.6 = (bf16[512,2048]{1,0:T(8,128)(2,1)}, bf16[512,2048]{1,0:T(8,128)(2,1)}, u32[]{:S(2)}, u32[]{:S(2)}) collective-permute-start(bf16[512,2048]{1,0:T(8,128)(2,1)} %get-tuple-element.448), channel_id=1, source_target_pairs={{0,2},{1,3},{2,0},{3,1},{4,6},{5,7},{6,4},{7,5},{8,10},{9,11},{10,... | collective-permute-start | bytes 6291464 | tf_op jit(solution)/shard_map/ppermute | solution.py:83
  359.4 39.9 %collective-permute-start.5 = (bf16[6144,128]{1,0:T(8,128)(2,1)}, bf16[6144,128]{1,0:T(8,128)(2,1)S(1)}, u32[]{:S(2)}, u32[]{:S(2)}) collective-permute-start(bf16[6144,128]{1,0:T(8,128)(2,1)} %pad_maximum_fusion.1), channel_id=1, source_target_pairs={{0,4},{4,0},{8,12},{12,8},{16,20},{20,16},{24,28},{28,24},{1,5},{5... | collective-permute-start | bytes 4718600 | tf_op jit(solution)/shard_map/ppermute | solution.py:83
  395.9 48.6 %collective-permute-start.8 = (f32[1024,384]{1,0:T(8,128)}, f32[1024,384]{1,0:T(8,128)}, u32[]{:S(2)}, u32[]{:S(2)}) collective-permute-start(f32[1024,384]{1,0:T(8,128)} %get-tuple-element.246), channel_id=1, source_target_pairs={{0,1},{1,0},{2,3},{3,2},{4,5},{5,4},{6,7},{7,6},{8,9},{9,8},{10,11... | collective-permute-start | bytes 4718600 | tf_op jit(solution)/shard_map/ppermute | solution.py:83
  396.0 53.6 %collective-permute-start.9 = (bf16[512,2048]{1,0:T(8,128)(2,1)}, bf16[512,2048]{1,0:T(8,128)(2,1)}, u32[]{:S(2)}, u32[]{:S(2)}) collective-permute-start(bf16[512,2048]{1,0:T(8,128)(2,1)} %get-tuple-element.447), channel_id=1, source_target_pairs={{0,2},{1,3},{2,0},{3,1},{4,6},{5,7},{6,4},{7,5},{8,10},{9,11},{10,... | collective-permute-start | bytes 6291464 | tf_op jit(solution)/shard_map/ppermute | solution.py:83
  397.8 82.0 %collective-permute-start.12 = (bf16[6144,128]{1,0:T(8,128)(2,1)}, bf16[6144,128]{1,0:T(8,128)(2,1)}, u32[]{:S(2)}, u32[]{:S(2)}) collective-permute-start(bf16[6144,128]{1,0:T(8,128)(2,1)} %pad_maximum_fusion.2), channel_id=1, source_target_pairs={{0,4},{4,0},{8,12},{12,8},{16,20},{20,16},{24,28},{28,24},{1,5},{5... | collective-permute-start | bytes 4718600 | tf_op jit(solution)/shard_map/ppermute | solution.py:83
  399.2 50.4 %copy-start.7 = (bf16[6144,128]{1,0:T(8,128)(2,1)}, bf16[6144,128]{1,0:T(8,128)(2,1)S(1)}, u32[]{:S(2)}) copy-start(bf16[6144,128]{1,0:T(8,128)(2,1)S(1)} %collective-permute-done.5) | copy-start | bytes 4718596
  406.5 38.0 %copy-start.9 = (f32[1024,384]{1,0:T(8,128)S(1)}, f32[1024,384]{1,0:T(8,128)}, u32[]{:S(2)}) copy-start(f32[1024,384]{1,0:T(8,128)} %get-tuple-element.246) | copy-start | bytes 4718596
  406.6 43.0 %collective-permute-start.7 = (bf16[3072,128]{1,0:T(8,128)(2,1)S(1)}, bf16[3072,128]{1,0:T(8,128)(2,1)}, u32[]{:S(2)}, u32[]{:S(2)}) collective-permute-start(bf16[3072,128]{1,0:T(8,128)(2,1)S(1)} %fusion.13), channel_id=1, source_target_pairs={{0,8},{4,12},{24,16},{28,20},{1,9},{5,13},{25,17},{29,21},{2,10},{... | collective-permute-start | bytes 2359304 | tf_op jit(solution)/shard_map/ppermute | solution.py:146
  444.4 33.2 %collective-permute-start.13 = (f32[1024,384]{1,0:T(8,128)}, f32[1024,384]{1,0:T(8,128)}, u32[]{:S(2)}, u32[]{:S(2)}) collective-permute-start(f32[1024,384]{1,0:T(8,128)} %get-tuple-element.251), channel_id=1, source_target_pairs={{0,1},{1,0},{2,3},{3,2},{4,5},{5,4},{6,7},{7,6},{8,9},{9,8},{10,11... | collective-permute-start | bytes 4718600 | tf_op jit(solution)/shard_map/ppermute | solution.py:83
  452.1 27.6 %collective-permute-start.10 = (bf16[3072,128]{1,0:T(8,128)(2,1)}, bf16[3072,128]{1,0:T(8,128)(2,1)}, u32[]{:S(2)}, u32[]{:S(2)}) collective-permute-start(bf16[3072,128]{1,0:T(8,128)(2,1)} %fusion.16), channel_id=1, source_target_pairs={{0,8},{4,12},{8,16},{12,20},{1,9},{5,13},{9,17},{13,21},{2,10},{6,... | collective-permute-start | bytes 2359304 | tf_op jit(solution)/shard_map/ppermute | solution.py:146
  455.2 24.6 %collective-permute-start.11 = (bf16[3072,128]{1,0:T(8,128)(2,1)}, bf16[3072,128]{1,0:T(8,128)(2,1)}, u32[]{:S(2)}, u32[]{:S(2)}) collective-permute-start(bf16[3072,128]{1,0:T(8,128)(2,1)} %fusion.16), channel_id=1, source_target_pairs={{24,16},{28,20},{16,8},{20,12},{25,17},{29,21},{17,9},{21,13},{26,... | collective-permute-start | bytes 2359304 | tf_op jit(solution)/shard_map/ppermute | solution.py:146
  456.7 23.0 %collective-permute-start.14 = (bf16[1024,384]{1,0:T(8,128)(2,1)}, bf16[1024,384]{1,0:T(8,128)(2,1)}, u32[]{:S(2)}, u32[]{:S(2)}) collective-permute-start(bf16[1024,384]{1,0:T(8,128)(2,1)} %add_convert_fusion.12), channel_id=1, source_target_pairs={{0,2},{1,3},{2,0},{3,1},{4,6},{5,7},{6,4},{7,5},{8,10},{9,11},{10,... | collective-permute-start | bytes 2359304 | tf_op jit(solution)/shard_map/ppermute | solution.py:83
  479.8 33.7 %collective-permute-start.18 = (bf16[1024,2048]{1,0:T(8,128)(2,1)}, bf16[1024,2048]{1,0:T(8,128)(2,1)}, u32[]{:S(2)}, u32[]{:S(2)}) collective-permute-start(bf16[1024,2048]{1,0:T(8,128)(2,1)} %get-tuple-element.260), channel_id=1, source_target_pairs={{0,1},{1,0},{2,3},{3,2},{4,5},{5,4},{6,7},{7,6},{8,9},{9,8},{10,11... | collective-permute-start | bytes 12582920 | tf_op jit(solution)/shard_map/ppermute | solution.py:83
  484.1 27.0 %collective-permute-start.15 = (bf16[3072,128]{1,0:T(8,128)(2,1)}, bf16[3072,128]{1,0:T(8,128)(2,1)S(1)}, u32[]{:S(2)}, u32[]{:S(2)}) collective-permute-start(bf16[3072,128]{1,0:T(8,128)(2,1)} %get-tuple-element.428), channel_id=1, source_target_pairs={{0,8},{4,12},{8,16},{12,20},{16,24},{20,28},{1,9},{5,13},{9,17},{1... | collective-permute-start | bytes 2359304 | tf_op jit(solution)/shard_map/ppermute | solution.py:146
  486.8 24.3 %collective-permute-start.16 = (bf16[3072,128]{1,0:T(8,128)(2,1)}, bf16[3072,128]{1,0:T(8,128)(2,1)S(1)}, u32[]{:S(2)}, u32[]{:S(2)}) collective-permute-start(bf16[3072,128]{1,0:T(8,128)(2,1)} %get-tuple-element.427), channel_id=1, source_target_pairs={{24,16},{28,20},{16,8},{20,12},{8,0},{12,4},{25,17},{29,21},{17,9}... | collective-permute-start | bytes 2359304 | tf_op jit(solution)/shard_map/ppermute | solution.py:146
  488.1 23.0 %collective-permute-start.17 = (bf16[1024,384]{1,0:T(8,128)(2,1)S(1)}, bf16[1024,384]{1,0:T(8,128)(2,1)}, u32[]{:S(2)}, u32[]{:S(2)}) collective-permute-start(bf16[1024,384]{1,0:T(8,128)(2,1)S(1)} %add_convert_fusion.11), channel_id=1, source_target_pairs={{0,2},{1,3},{2,0},{3,1},{4,6},{5,7},{6,4},{7,5},{8,10},{9,11},{10,... | collective-permute-start | bytes 2359304 | tf_op jit(solution)/shard_map/ppermute | solution.py:83
  489.0 101.6 %copy-start.48 = (f32[16]{0:T(128)}, f32[16]{0:T(128)S(1)}, u32[]{:S(2)}) copy-start(f32[16]{0:T(128)S(1)} %get-tuple-element.470) | copy-start | bytes 196
  489.0 101.6 %copy-start.49 = (f32[16]{0:T(128)}, f32[16]{0:T(128)S(1)}, u32[]{:S(2)}) copy-start(f32[16]{0:T(128)S(1)} %get-tuple-element.471) | copy-start | bytes 196
  522.6 26.0 %collective-permute-start.19 = (bf16[256,2048]{1,0:T(8,128)(2,1)S(1)}, bf16[256,2048]{1,0:T(8,128)(2,1)S(1)}, u32[]{:S(2)}, u32[]{:S(2)}) collective-permute-start(bf16[256,2048]{1,0:T(8,128)(2,1)S(1)} %get-tuple-element.442), channel_id=1, source_target_pairs={{0,2},{1,3},{2,0},{3,1},{4,6},{5,7},{6,4},{7,5},{8,10},{9,11},{10,... | collective-permute-start | bytes 3145736 | tf_op jit(solution)/shard_map/ppermute | solution.py:83
  524.1 47.1 %collective-permute-start.21 = (bf16[256,2048]{1,0:T(8,128)(2,1)}, bf16[256,2048]{1,0:T(8,128)(2,1)}, u32[]{:S(2)}, u32[]{:S(2)}) collective-permute-start(bf16[256,2048]{1,0:T(8,128)(2,1)} %get-tuple-element.441), channel_id=1, source_target_pairs={{0,2},{1,3},{2,0},{3,1},{4,6},{5,7},{6,4},{7,5},{8,10},{9,11},{10,... | collective-permute-start | bytes 3145736 | tf_op jit(solution)/shard_map/ppermute | solution.py:83
  552.5 21.9 %collective-permute-start.20 = (bf16[3328,128]{1,0:T(8,128)(2,1)S(1)}, bf16[3328,128]{1,0:T(8,128)(2,1)S(1)}, u32[]{:S(2)}, u32[]{:S(2)}) collective-permute-start(bf16[3328,128]{1,0:T(8,128)(2,1)S(1)} %get-tuple-element.434), channel_id=1, source_target_pairs={{0,4},{4,0},{8,12},{12,8},{16,20},{20,16},{24,28},{28,24},{1,5},{5... | collective-permute-start | bytes 2555912 | tf_op jit(solution)/shard_map/ppermute | solution.py:83
  556.7 45.1 %collective-permute-start.27 = (bf16[256,2048]{1,0:T(8,128)(2,1)}, bf16[256,2048]{1,0:T(8,128)(2,1)}, u32[]{:S(2)}, u32[]{:S(2)}) collective-permute-start(bf16[256,2048]{1,0:T(8,128)(2,1)} %get-tuple-element.440), channel_id=1, source_target_pairs={{0,2},{1,3},{2,0},{3,1},{4,6},{5,7},{6,4},{7,5},{8,10},{9,11},{10,... | collective-permute-start | bytes 3145736 | tf_op jit(solution)/shard_map/ppermute | solution.py:83
  558.2 44.3 %collective-permute-start.25 = (bf16[3328,128]{1,0:T(8,128)(2,1)}, bf16[3328,128]{1,0:T(8,128)(2,1)}, u32[]{:S(2)}, u32[]{:S(2)}) collective-permute-start(bf16[3328,128]{1,0:T(8,128)(2,1)} %get-tuple-element.433), channel_id=1, source_target_pairs={{0,4},{4,0},{8,12},{12,8},{16,20},{20,16},{24,28},{28,24},{1,5},{5... | collective-permute-start | bytes 2555912 | tf_op jit(solution)/shard_map/ppermute | solution.py:83
  584.3 26.4 %collective-permute-start.24 = (bf16[3328,128]{1,0:T(8,128)(2,1)}, bf16[3328,128]{1,0:T(8,128)(2,1)}, u32[]{:S(2)}, u32[]{:S(2)}) collective-permute-start(bf16[3328,128]{1,0:T(8,128)(2,1)} %fusion.17), channel_id=1, source_target_pairs={{0,8},{4,12},{24,16},{28,20},{1,9},{5,13},{25,17},{29,21},{2,10},{... | collective-permute-start | bytes 2555912 | tf_op jit(solution)/shard_map/ppermute | solution.py:146
  591.4 19.3 %collective-permute-start.26 = (f32[1,91440]{1,0:T(1,128)S(1)}, f32[1,91440]{1,0:T(1,128)S(1)}, u32[]{:S(2)}, u32[]{:S(2)}) collective-permute-start(f32[1,91440]{1,0:T(1,128)S(1)} %broadcast_in_dim.147), channel_id=1, source_target_pairs={{0,16},{4,20},{8,24},{12,28},{16,0},{20,4},{24,8},{28,12},{1,17},{... | collective-permute-start | bytes 1097288 | tf_op jit(solution)/shard_map/ppermute | solution.py:83
  599.3 31.4 %collective-permute-start.32 = (bf16[256,2048]{1,0:T(8,128)(2,1)}, bf16[256,2048]{1,0:T(8,128)(2,1)}, u32[]{:S(2)}, u32[]{:S(2)}) collective-permute-start(bf16[256,2048]{1,0:T(8,128)(2,1)} %get-tuple-element.439), channel_id=1, source_target_pairs={{0,2},{1,3},{2,0},{3,1},{4,6},{5,7},{6,4},{7,5},{8,10},{9,11},{10,... | collective-permute-start | bytes 3145736 | tf_op jit(solution)/shard_map/ppermute | solution.py:83
  601.9 29.4 %collective-permute-start.30 = (bf16[3328,128]{1,0:T(8,128)(2,1)}, bf16[3328,128]{1,0:T(8,128)(2,1)}, u32[]{:S(2)}, u32[]{:S(2)}) collective-permute-start(bf16[3328,128]{1,0:T(8,128)(2,1)} %get-tuple-element.432), channel_id=1, source_target_pairs={{0,4},{4,0},{8,12},{12,8},{16,20},{20,16},{24,28},{28,24},{1,5},{5... | collective-permute-start | bytes 2555912 | tf_op jit(solution)/shard_map/ppermute | solution.py:83
  614.6 21.0 %collective-permute-start.28 = (bf16[3328,128]{1,0:T(8,128)(2,1)}, bf16[3328,128]{1,0:T(8,128)(2,1)}, u32[]{:S(2)}, u32[]{:S(2)}) collective-permute-start(bf16[3328,128]{1,0:T(8,128)(2,1)} %fusion.12), channel_id=1, source_target_pairs={{0,8},{4,12},{8,16},{12,20},{1,9},{5,13},{9,17},{13,21},{2,10},{6,... | collective-permute-start | bytes 2555912 | tf_op jit(solution)/shard_map/ppermute | solution.py:146
  620.7 14.8 %collective-permute-start.29 = (bf16[3328,128]{1,0:T(8,128)(2,1)}, bf16[3328,128]{1,0:T(8,128)(2,1)}, u32[]{:S(2)}, u32[]{:S(2)}) collective-permute-start(bf16[3328,128]{1,0:T(8,128)(2,1)} %fusion.12), channel_id=1, source_target_pairs={{24,16},{28,20},{16,8},{20,12},{25,17},{29,21},{17,9},{21,13},{26,... | collective-permute-start | bytes 2555912 | tf_op jit(solution)/shard_map/ppermute | solution.py:146
  623.4 12.2 %collective-permute-start.31 = (f32[1,50480]{1,0:T(1,128)S(1)}, f32[1,50480]{1,0:T(1,128)S(1)}, u32[]{:S(2)}, u32[]{:S(2)}) collective-permute-start(f32[1,50480]{1,0:T(1,128)S(1)} %broadcast_in_dim.148), channel_id=1, source_target_pairs={{0,8},{4,12},{8,0},{12,4},{16,24},{20,28},{24,16},{28,20},{1,9},{5... | collective-permute-start | bytes 605768 | tf_op jit(solution)/shard_map/ppermute | solution.py:83
  630.7 50.2 %collective-permute-start.35 = (bf16[3328,128]{1,0:T(8,128)(2,1)}, bf16[3328,128]{1,0:T(8,128)(2,1)}, u32[]{:S(2)}, u32[]{:S(2)}) collective-permute-start(bf16[3328,128]{1,0:T(8,128)(2,1)} %get-tuple-element.431), channel_id=1, source_target_pairs={{0,4},{4,0},{8,12},{12,8},{16,20},{20,16},{24,28},{28,24},{1,5},{5... | collective-permute-start | bytes 2555912 | tf_op jit(solution)/shard_map/ppermute | solution.py:83
  631.3 22.7 %collective-permute-start.22 = (bf16[512,2048]{1,0:T(8,128)(2,1)}, bf16[512,2048]{1,0:T(8,128)(2,1)}, u32[]{:S(2)}, u32[]{:S(2)}) collective-permute-start(bf16[512,2048]{1,0:T(8,128)(2,1)} %get-tuple-element.425), channel_id=1, source_target_pairs={{0,1},{1,0},{2,3},{3,2},{4,5},{5,4},{6,7},{7,6},{8,9},{9,8},{10,11... | collective-permute-start | bytes 6291464 | tf_op jit(solution)/shard_map/ppermute | solution.py:83
  635.5 24.3 %collective-permute-start.23 = (bf16[512,2048]{1,0:T(8,128)(2,1)S(1)}, bf16[512,2048]{1,0:T(8,128)(2,1)}, u32[]{:S(2)}, u32[]{:S(2)}) collective-permute-start(bf16[512,2048]{1,0:T(8,128)(2,1)S(1)} %get-tuple-element.426), channel_id=1, source_target_pairs={{0,1},{1,0},{2,3},{3,2},{4,5},{5,4},{6,7},{7,6},{8,9},{9,8},{10,11... | collective-permute-start | bytes 6291464 | tf_op jit(solution)/shard_map/ppermute | solution.py:83
  640.4 23.9 %collective-permute-start.37 = (bf16[1024,2048]{1,0:T(8,128)(2,1)}, bf16[1024,2048]{1,0:T(8,128)(2,1)}, u32[]{:S(2)}, u32[]{:S(2)}) collective-permute-start(bf16[1024,2048]{1,0:T(8,128)(2,1)} %add_convert_fusion.own_ref), channel_id=1, source_target_pairs={{0,1},{1,0},{2,3},{3,2},{4,5},{5,4},{6,7},{7,6},{8,9},{9,8},{10,11... | collective-permute-start | bytes 12582920 | tf_op jit(solution)/shard_map/ppermute | solution.py:83
  649.6 31.3 %collective-permute-start.33 = (bf16[3328,128]{1,0:T(8,128)(2,1)}, bf16[3328,128]{1,0:T(8,128)(2,1)S(1)}, u32[]{:S(2)}, u32[]{:S(2)}) collective-permute-start(bf16[3328,128]{1,0:T(8,128)(2,1)} %get-tuple-element.430), channel_id=1, source_target_pairs={{0,8},{4,12},{8,16},{12,20},{16,24},{20,28},{1,9},{5,13},{9,17},{1... | collective-permute-start | bytes 2555912 | tf_op jit(solution)/shard_map/ppermute | solution.py:146
  654.0 26.8 %collective-permute-start.34 = (bf16[3328,128]{1,0:T(8,128)(2,1)}, bf16[3328,128]{1,0:T(8,128)(2,1)}, u32[]{:S(2)}, u32[]{:S(2)}) collective-permute-start(bf16[3328,128]{1,0:T(8,128)(2,1)} %get-tuple-element.429), channel_id=1, source_target_pairs={{24,16},{28,20},{16,8},{20,12},{8,0},{12,4},{25,17},{29,21},{17,9}... | collective-permute-start | bytes 2555912 | tf_op jit(solution)/shard_map/ppermute | solution.py:146
  659.9 21.0 %collective-permute-start.36 = (f32[1,30000]{1,0:T(1,128)}, f32[1,30000]{1,0:T(1,128)}, u32[]{:S(2)}, u32[]{:S(2)}) collective-permute-start(f32[1,30000]{1,0:T(1,128)} %broadcast_in_dim.149), channel_id=1, source_target_pairs={{0,4},{4,0},{8,12},{12,8},{16,20},{20,16},{24,28},{28,24},{1,5},{5... | collective-permute-start | bytes 360008 | tf_op jit(solution)/shard_map/ppermute | solution.py:83
  683.5 6.3 collective-permute-start.38
  690.2 23.4 %collective-permute-start.39 = (f32[1,85248]{1,0:T(1,128)S(1)}, f32[1,85248]{1,0:T(1,128)}, u32[]{:S(2)}, u32[]{:S(2)}) collective-permute-start(f32[1,85248]{1,0:T(1,128)S(1)} %reshape_add_fusion), channel_id=1, source_target_pairs={{0,2},{1,3},{2,0},{3,1},{4,6},{5,7},{6,4},{7,5},{8,10},{9,11},{10,... | collective-permute-start | bytes 1022984 | tf_op jit(solution)/shard_map/ppermute | solution.py:83
  (52 other events, 429.7 us)
Sparse Core Ops, SparseCore 0:
  15.5 124.2 all-gather.3
  142.6 90.8 all-gather.5

commit v3 on v2

--- a/solution.py
+++ b/solution.py
@@ -18,6 +18,7 @@
 BLK = 128
 LANES = 128
 MID_ROWS = 512
+PART_ROWS = 256
 TILES_STEP = 6
 COPY_ROWS = 16
 SLACK = 2
@@ -322,6 +323,26 @@
     state[...] = keeps[0:1, :] * state[...] + product(b_act.T, tails[...])
 
 
+def both_halves(left_high, left_low, right_high, right_low, low, which):
+    mine = low if which == 0 else jnp.logical_not(low)
+
+    def turned(value):
+        return pltpu.roll(value.astype(F32), LANES // 2, 1)
+
+    left_high, right_high = left_high.astype(F32), right_high.astype(F32)
+    left = jnp.concatenate(
+        [jnp.where(mine, left_high, turned(left_low)), jnp.where(mine, left_high, 0.0)], axis=1
+    )
+    right = jnp.concatenate(
+        [
+            jnp.where(mine, right_high, turned(right_high)),
+            jnp.where(mine, right_low.astype(F32), 0.0),
+        ],
+        axis=1,
+    )
+    return dot(left.astype(BF16), right.astype(BF16), NT)
+
+
 def ssd_backward_kernel(
     *refs,
 ):
@@ -412,16 +433,16 @@
         step_cols = [wide(steps[:, h : h + 1], shape) for h in (2 * pair, 2 * pair + 1)]
         both = jnp.where(low, cols[0], cols[1])
         step_both = jnp.where(low, step_cols[0], step_cols[1])
-        parts = [jnp.where(low, act, 0.0), jnp.where(low, 0.0, act)]
+        act_high, act_low = halves(act)
         dy_high, dy_low = halves(dy)
-        dy_wide = jnp.concatenate([dy_high, dy_high, dy_low], axis=1)
-        high, rest = halves(jnp.concatenate(parts, axis=0))
-        inners = dot(jnp.concatenate([high, rest, high], axis=1), dy_wide, NT)
+        inners = [
+            both_halves(act_high, act_low, dy_high, dy_low, low, which) for which in range(2)
+        ]
         weights = []
         for which in range(2):
             head = 2 * pair + which
             decay = jnp.exp2(cum_t[head : head + 1, :] - cols[which] + bias_t)
-            inner = inners[which * BLK : (which + 1) * BLK, :]
+            inner = inners[which]
             weight = decay * scores_t
             weights.append(weight)
             d_scores = d_scores + decay * inner * step_cols[which]
@@ -631,10 +652,13 @@
 
 
 def gate_kernel(normed_ref, cot_ref, wgate_ref, wout_ref, ssd_ref, gain_ref, gate_ref, dh_ref, sums_ref):
-    gate_ref[...] = dot(normed_ref[...], wgate_ref[...])
-    dh_ref[...] = dot(cot_ref[...], wout_ref[...], NT)
     rows, width = ssd_ref.shape
+    part = min(PART_ROWS, rows)
     for first in range(0, rows, LANES):
+        if first % part == 0:
+            now = slice(first, first + part)
+            gate_ref[now, :] = dot(normed_ref[now, :], wgate_ref[...])
+            dh_ref[now, :] = dot(cot_ref[now, :], wout_ref[...], NT)
         at = slice(first, first + LANES)
         squares = jnp.zeros((LANES, LANES), F32)
         inners = jnp.zeros((LANES, LANES), F32)
@@ -696,6 +720,8 @@
     shift = scale * scale * scale * (sums_ref[1:2, :] / DI)
     turned = jnp.concatenate([scale] * 8 + [shift] * 8 + [jnp.zeros((LANES - 16, rows), F32)], axis=0).T
     chunk = min(64, rows)
+    part = min(PART_ROWS, rows)
+    sending = pl.program_id(0) < pl.num_programs(0) // 2
     for first in range(0, rows, chunk):
         at = slice(first, first + chunk)
         scales = wide(turned[at, 0:1], (chunk, LANES))
@@ -717,16 +743,12 @@
             dgate_ref[at, lanes] = (
                 d_gated * ssd * (sig * (1.0 + gate * (1.0 - sig)))
             ).astype(BF16)
-    mixed = dot(hidden_ref[...], wout_ref[...]).astype(BF16)
-    steps = pl.num_programs(0) // 2
-
-    @pl.when(pl.program_id(0) < steps)
-    def _():
-        sent_ref[...] = mixed
-
-    @pl.when(pl.program_id(0) >= steps)
-    def _():
-        kept_ref[...] = mixed
+        done = first + chunk
+        if done % part == 0:
+            now = slice(done - part, done)
+            mixed = dot(hidden_ref[now, :], wout_ref[...]).astype(BF16)
+            sent_ref[now, :] = jnp.where(sending, mixed, sent_ref[now, :])
+            kept_ref[now, :] = jnp.where(sending, kept_ref[now, :], mixed)
 
 
 def gated_pass(core, ssd, gate, d_hidden, sums, gain, w_output):
@@ -778,8 +800,8 @@
     )(core, ssd, gate, d_hidden, sums, gain, w_output)
 
 
-def unit_rows(tokens_ref):
-    rows = tokens_ref[...].astype(F32)
+def unit_rows(tokens):
+    rows = tokens.astype(F32)
     inverse = lax.rsqrt(jnp.mean(rows * rows, axis=1, keepdims=True) + EPS)
     return rows, inverse
 
@@ -789,11 +811,15 @@
     def _():
         gain_out[...] = jnp.zeros_like(gain_out)
 
-    total = dot(dgate_ref[...], wgate_ref[...], NT) + dot(drest_ref[...], wrest_ref[...], NT)
-    out_ref[...] = total.astype(BF16)
-    rows, inverse = unit_rows(tokens_ref)
-    weighted = total * (rows * inverse)
-    gain_out[...] += jnp.sum(weighted.reshape(-1, 8, D), axis=0)
+    rows = tokens_ref.shape[0]
+    part = min(PART_ROWS, rows)
+    for first in range(0, rows, part):
+        now = slice(first, first + part)
+        total = dot(dgate_ref[now, :], wgate_ref[...], NT) + dot(drest_ref[now, :], wrest_ref[...], NT)
+        out_ref[now, :] = total.astype(BF16)
+        values, inverse = unit_rows(tokens_ref[now, :])
+        weighted = total * (values * inverse)
+        gain_out[...] += jnp.sum(weighted.reshape(-1, 8, D), axis=0)
 
 
 def normed_grad(half, weight, d_gate, d_rest, tokens, w_gate, w_rest):
@@ -844,7 +870,7 @@
     def _():
         terms[...] = other_ref[...].astype(F32)
 
-    rows, inverse = unit_rows(tokens_ref)
+    rows, inverse = unit_rows(tokens_ref[...])
     weighted = terms[...] * gain_ref[0:1, :]
     inner = jnp.mean(weighted * rows, axis=1, keepdims=True)
     out_ref[...] = (
@@ -1292,15 +1318,20 @@
         (d_sent, side_chips[1], side_others[0], d_rest)
     )
     side_others.append(swap(side_chips[1], "tensor", 2))
-    d_kept, pre_kept = normed_grad(core_at, 0, d_gate, d_rest, tokens, w_gate, w_rest)
-    early_share, (d_kept, side_others[1]) = early.total((d_kept, side_others[1]))
-    grad_pre = jnp.sum(pre_sent + pre_kept, axis=0)
-    d_chip, d_rest = tied(chip_sum(d_kept, d_sent), d_rest)
-    d_others = [swap(part, "tensor", 2) for part in jnp.split(d_chip, 4)]
     grad_input = contract_rows(normed, d_rest[:, :di_local]).astype(BF16)
     late_grads = spread(plans[1][0], (grad_gate, grad_input, grad_output), n_dp * plans[1][1])
-    late_grads, d_others[0] = tied(late_grads, d_others[0])
+    early_share, (late_grads, side_others[1], d_rest) = early.total(
+        (late_grads, side_others[1], d_rest)
+    )
     late = OwnerSum(late_grads, ((0,), (1,), (2,), (3,)))
+    d_kept, pre_kept = normed_grad(core_at, 16, d_gate, d_rest, tokens, w_gate, w_rest)
+    d_kept, pre_kept = late.first((d_kept, pre_kept))
+    grad_pre = jnp.sum(pre_sent + pre_kept, axis=0)
+    d_chip = chip_sum(d_kept, d_sent)
+    d_others = [swap(part, "tensor", 2) for part in jnp.split(d_chip, 4)]
+    d_others[0], side_chips, side_others, out_chip, out_others = late.second(
+        (d_others[0], side_chips, side_others, out_chip, out_others)
+    )
 
     side_total = jnp.concatenate(
         [
@@ -1308,9 +1339,6 @@
             for own, other in zip(side_chips, side_others)
         ],
         axis=0,
-    )
-    side_total, d_others[1], out_chip, out_others, early_share, grad_pre = late.first(
-        (side_total, d_others[1], out_chip, out_others, early_share, grad_pre)
     )
     grad_side = lax.dynamic_index_in_dim(
         contract_rows(normed, side_total).reshape(n_dp, n_tensor, -1, side_total.shape[1]),
@@ -1333,16 +1361,10 @@
     small_sums = SharedSums(
         grad_side.reshape(n_dp, -1), jnp.concatenate([own_vector, grad_pre, gbc_sums.reshape(-1)])
     )
-    arrived, d_others[2] = late.second((small_sums.send(), d_others[2]))
+    arrived, d_others[1] = late.third((small_sums.send(), d_others[1]))
     small_sums.add(arrived)
-    arrived, d_others[3] = late.third((small_sums.send(), d_others[3]))
-    small_sums.add(arrived)
-    d_half = (d_chip.astype(F32) + jnp.concatenate(d_others).astype(F32)).astype(BF16)
-    input_grad = input_grads(
-        core_at, d_half, swap(d_half, "tensor", 1), tokens, cotangent, pre_gain[None, :]
-    )
-    late_share, (arrived, input_grad, misfit) = late.total(
-        (small_sums.send(), input_grad, misfit)
+    late_share, (arrived, d_others[2], misfit) = late.total(
+        (small_sums.send(), d_others[2], misfit)
     )
     small_sums.add(arrived)
     small_sums.finish()
@@ -1395,6 +1417,11 @@
         axis=0,
     )
 
+    d_half = (d_chip.astype(F32) + jnp.concatenate(d_others).astype(F32)).astype(BF16)
+    input_grad = input_grads(
+        core_at, d_half, swap(d_half, "tensor", 1), tokens, cotangent, pre_gain[None, :]
+    )
+
     pre_share = lax.dynamic_slice_in_dim(common[:D], tensor_rank * model_local, model_local, 0)
     bc_share = lax.dynamic_slice_in_dim(
         common[D:].reshape(CONV + 1, 2 * NS), tensor_rank * bc_local, bc_local, 1

time: 733 us -> 740 us (level)
  waiting for transfers between devices: 168 us -> 188 us
  other arithmetic: 112 us -> 103 us
    ppermute x30, waiting for transfers between devices: 43.1 us -> 54 us  [swap(): return lax.ppermute(value, axis, [(i, i ^ bit) for i in range(size)])]
    ppermute x10, waiting for transfers between devices: 0.03 us -> 9.63 us  [hop(): return lax.ppermute(value.astype(BF16), 'dp', pairs)]
  transfers between devices with their start and end apart: 42 -> 42, of which waited for: 12 -> 13; matrix products, arithmetic and copies ran while one was open for 20% -> 20% of each run, Pallas kernels for 29% -> 26%
where the time goes in v3:
time: 740 us; the launch traced here: 735 us
  Pallas kernels  279 us (38%)
  waiting for transfers between devices  188 us (25%)
  other arithmetic  103 us (14%)
  starting transfers between devices  51.9 us (7%)
  matrix products  47.1 us (6%)
  local copies, waits for them, and re-layouts  42 us (6%)
  between operations  17.2 us (2%)
    all_gather x1, waiting for transfers between devices, on_device(): first_held = lax.all_gather(first_share, 'dp', axis=0, tiled=True)  90.3 us
    pallas_call x2, Pallas kernels, ssd_backward(): pl.pallas_call(ssd_backward_kernel, grid=(blocks,), in_specs=[pl.BlockSpe...  67.7 us
    ppermute x30, waiting for transfers between devices, swap(): return lax.ppermute(value, axis, [(i, i ^ bit) for i in range(size)])  54 us
    dot_general x4, matrix products, contract_rows(): lax.dot_general(left, right, (((0,), (0,)), ((), ())), preferred_element_...  47.1 us
    pallas_call x2, Pallas kernels, normed_grad(): pl.pallas_call(normed_grad_kernel, grid_spec=pltpu.PrefetchScalarGridSpec...  38.4 us
    all_gather x1, waiting for transfers between devices, on_device(): second_held = lax.all_gather(mine[cut:], 'dp', axis=0, tiled=True)  34.4 us
    pallas_call x1, Pallas kernels, ssd_forward(): pl.pallas_call(ssd_forward_kernel, grid=(sequences, blocks), in_specs=[pl...  27.9 us
    ppermute x10, starting transfers between devices, hop(): return lax.ppermute(value.astype(BF16), 'dp', pairs)  27.3 us
  transfers between devices with their start and end apart: 42, of which 13 were waited for; matrix products, arithmetic and copies ran while one was open for 20% of the time, Pallas kernels for 26%

profile of v3, /device:TPU:0, one launch (start us, length us, event | category | flops | bytes accessed | tf_op | source)
XLA Modules:
  0.0 735.4 jit_solution(7526371454373161050)
XLA Ops:
  18.9 6.3 all-gather
  28.1 5.1 fusion.2
  36.4 8.8 %fusion.4.left_ref.normed_ref = bf16[2048,2048]{1,0:T(8,128)(2,1)} fusion(bf16[2048,2048]{1,0:T(8,128)(2,1)} %tokens_ref.5, f32[2048]{0:T(1024)S(1)} %bitcast.165, f32[2048]{0:T(1024)S(1)} %add_rsqrt_fusion), kind=kLoop, calls=%fused_computation.7 | loop fusion | flops 16777216 | bytes 16793600 | tf_op jit(solution)/shard_map/convert_element_type | solution.py:1231
  49.5 90.3 %all-gather.4.cloned.1.call-done.refs_0_ = bf16[31744,128]{1,0:T(8,128)(2,1)} async-done(((bf16[3968,128]{1,0:T(8,128)(2,1)}), bf16[31744,128]{1,0:T(8,128)(2,1)}) %all-gather.4.cloned.1.call-update) | async-done | bytes 8126480 | tf_op jit(solution)/shard_map/all_gather | solution.py:1194
  143.4 7.7 %assemble.3.right_ref = bf16[2048,1536]{1,0:T(8,128)(2,1)} custom-call(s32[128]{0:T(128)} %get-tuple-element.463.rows_ref, bf16[31744,128]{1,0:T(8,128)(2,1)} %all-gather.4.cloned.1.call-done.refs_0_, bf16[2048,512]{1,0:T(8,128)(2,1)S(1)} %maximum_maximum_fusion.refs_1_), custom_call_target="tpu_custom_call" | custom-call | bytes 16252928 | tf_op jit(solution)/shard_map/assemble/pallas_call | solution.py:968
  151.1 18.8 %project.2.rest_ref.prev_ref = f32[2048,1536]{1,0:T(8,128)} custom-call(bf16[2048,2048]{1,0:T(8,128)(2,1)} %fusion.4.left_ref.normed_ref, bf16[2048,1536]{1,0:T(8,128)(2,1)} %assemble.3.right_ref), custom_call_target="tpu_custom_call" | custom-call | flops 12884901888 | bytes 27262976 | tf_op jit(solution)/shard_map/project/pallas_call | solution.py:638
  171.2 27.9 %ssd_forward.2 = (f32[2048,1024]{1,0:T(8,128)}, f32[16,128,1024]{2,1,0:T(8,128)}) custom-call(f32[2048,1536]{1,0:T(8,128)} %project.2.rest_ref.prev_ref, f32[2048,1536]{1,0:T(8,128)} %project.2.rest_ref.prev_ref, f32[2048,128]{1,0:T(8,128)} %broadcast_in_dim.141.start_ref.refs_5_.refs_6_, f32[8,1024]{1,0:T(8,128)S(1)} %concatenate.78.par_ref.refs_8_.refs_9_, ...), custom_call_target="tpu_custom_call" | custom-call | flops 10737418240 | bytes 41943040 | tf_op jit(solution)/shard_map/ssd_forward/pallas_call | solution.py:524
  199.1 34.4 %all-gather.6.cloned.1.call-done.refs_1_ = bf16[22528,128]{1,0:T(8,128)(2,1)} async-done(((bf16[2816,128]{1,0:T(8,128)(2,1)}), bf16[22528,128]{1,0:T(8,128)(2,1)}) %all-gather.6.cloned.1.call-update) | async-done | bytes 5767184 | tf_op jit(solution)/shard_map/all_gather | solution.py:1195
  234.5 12.0 %assemble.4 = (bf16[2048,1024]{1,0:T(8,128)(2,1)}, bf16[1024,2048]{1,0:T(8,128)(2,1)}) custom-call(s32[256]{0:T(256)} %pad_add_fusion.rows_ref, bf16[31744,128]{1,0:T(8,128)(2,1)} %get-tuple-element.530, bf16[22528,128]{1,0:T(8,128)(2,1)} %get-tuple-element.532), custom_call_target="tpu_custom_call" | custom-call | bytes 27787264 | tf_op jit(solution)/shard_map/assemble/pallas_call | solution.py:968
  246.5 26.4 %gate_project.1 = (f32[2048,1024]{1,0:T(8,128)}, f32[2048,1024]{1,0:T(8,128)}, f32[8,2048]{1,0:T(8,128)}) custom-call(bf16[2048,2048]{1,0:T(8,128)(2,1)} %get-tuple-element.535, bf16[2048,2048]{1,0:T(8,128)(2,1)} %cot_ref.3, bf16[2048,1024]{1,0:T(8,128)(2,1)} %get-tuple-element.219.wgate_ref, bf16[1024,2048]{1,0:T(8,128)(2,1)} %get-tuple-element.220.wout_ref, ...), custom_call_target="tpu_custom_call" | custom-call | flops 17179869184 | bytes 33554432 | tf_op jit(solution)/shard_map/gate_project/pallas_call | solution.py:680
  276.7 2.8 collective-permute-done.3
  280.2 23.6 %gated_pass.1 = (bf16[2048,1024]{1,0:T(8,128)(2,1)}, bf16[2048,1024]{1,0:T(8,128)(2,1)}, f32[2048,1024]{1,0:T(8,128)}, f32[8,1024]{1,0:T(8,128)}, bf16[1024,2048...) custom-call(s32[1]{0:T(128)} %bitcast.core_ref.half_ref, f32[2048,1024]{1,0:T(8,128)} %get-tuple-element.218.ssd_ref, ...), custom_call_target="tpu_custom_call" | custom-call | flops 8589934592 | bytes 41943040 | tf_op jit(solution)/shard_map/gated_pass/pallas_call | solution.py:765
  306.9 14.4 %convolution_convert_fusion.refs_1_.refs_2_ = bf16[1024,2048]{1,0:T(8,128)(2,1)} fusion(bf16[2048,1024]{1,0:T(8,128)(2,1)} %get-tuple-element.229, bf16[2048,2048]{1,0:T(8,128)(2,1)} %cot_ref.3), kind=kOutput, calls=%fused_computation.19 | convolution fusion | flops 8592031744 | bytes 16777216 | tf_op jit(solution)/shard_map/dot_general | solution.py:75
  321.3 6.2 add_convert_fusion.2
  327.5 13.0 %convolution_convert_fusion.1.refs_0_ = bf16[2048,1024]{1,0:T(8,128)(2,1)} fusion(bf16[2048,2048]{1,0:T(8,128)(2,1)} %get-tuple-element.535, bf16[2048,1024]{1,0:T(8,128)(2,1)S(1)} %copy-done.50), kind=kOutput, calls=%fused_computation.20 | convolution fusion | flops 8592031744 | bytes 16777216 | tf_op jit(solution)/shard_map/dot_general | solution.py:75
  340.5 9.9 %spread.4 = bf16[24576,128]{1,0:T(8,128)(2,1)} custom-call(s32[256]{0:T(256)} %pad_add_fusion.1.rows_ref, bf16[2048,1024]{1,0:T(8,128)(2,1)} %convolution_convert_fusion.1.refs_0_, bf16[1024,2048]{1,0:T(8,128)(2,1)} %convolution_convert_fusion.refs_1_.refs_2_), custom_call_target="tpu_custom_call" | custom-call | bytes 14680064 | tf_op jit(solution)/shard_map/spread/pallas_call | solution.py:1002
  350.4 5.0 fusion.41
  360.2 33.8 %ssd_backward.2 = (bf16[2048,1536]{1,0:T(8,128)(2,1)}, f32[1024,384]{1,0:T(8,128)}, f32[48,1024]{1,0:T(8,128)}, f32[40,256]{1,0:T(8,128)}, f32[16,128]{1,0:T(8,128)}) custom-call(s32[1]{0:T(128)} %bitcast.16.refs_0_.refs_1_, f32[2048,1536]{1,0:T(8,128)} %get-tuple-element.231.refs_1_.refs_2_.refs_3_, ...), custom_call_target="tpu_custom_call" | custom-call | flops 13421772800 | bytes 20971520 | tf_op jit(solution)/shard_map/ssd_backward/pallas_call | solution.py:568
  397.4 6.7 collective-permute-done.6
  405.5 3.1 collective-permute-start.7
  408.6 33.9 %ssd_backward.3 = (bf16[2048,1536]{1,0:T(8,128)(2,1)}, f32[1024,384]{1,0:T(8,128)}, f32[48,1024]{1,0:T(8,128)}, f32[40,256]{1,0:T(8,128)}, f32[16,128]{1,0:T(8,128)}) custom-call(bf16[2048,1536]{1,0:T(8,128)(2,1)} %get-tuple-element.237.refs_0_, s32[1]{0:T(128)} %bitcast.16.refs_0_.refs_1_, ...), custom_call_target="tpu_custom_call", output_to_operand_aliasing={{0}: (0, {})} | custom-call | flops 13421772800 | bytes 20971520 | tf_op jit(solution)/shard_map/ssd_backward/pallas_call | solution.py:568
  445.1 3.5 collective-permute-done.9
  451.1 3.0 collective-permute-start.10
  457.1 19.2 %normed_grad.2 = (bf16[1024,2048]{1,0:T(8,128)(2,1)}, f32[8,2048]{1,0:T(8,128)}) custom-call(s32[1]{0:T(128)S(6)} %sub.101.half_ref, bf16[2048,1024]{1,0:T(8,128)(2,1)} %get-tuple-element.228.dgate_ref, bf16[2048,1536]{1,0:T(8,128)(2,1)} %get-tuple-element.257.drest_ref, bf16[2048,2048]{1,0:T(8,128)(2,1)} %tokens_ref.5, ...), custom_call_target="tpu_custom_call" | custom-call | flops 171798691840 | bytes 402653184 | tf_op jit(solution)/shard_map/normed_grad/pallas_call | solution.py:830
  478.2 4.6 add_convert_fusion.9
  482.8 2.7 collective-permute-start.15
  487.4 12.7 %fusion.7.refs_1_ = bf16[2048,1024]{1,0:T(8,128)(2,1)} fusion(bf16[2048,2048]{1,0:T(8,128)(2,1)S(1)} %copy-done.3, bf16[2048,1536]{1,0:T(8,128)(2,1)} %get-tuple-element.257.drest_ref), kind=kOutput, calls=%fused_computation.18 | convolution fusion | flops 8592031744 | bytes 16777216 | tf_op jit(solution)/shard_map/dot_general | solution.py:75
  500.2 11.5 %spread.5 = bf16[26624,128]{1,0:T(8,128)(2,1)} custom-call(s32[384]{0:T(512)} %get-tuple-element.458.rows_ref, bf16[2048,1024]{1,0:T(8,128)(2,1)} %convolution_convert_fusion.1.refs_0_, bf16[2048,1024]{1,0:T(8,128)(2,1)} %fusion.7.refs_1_, bf16[1024,2048]{1,0:T(8,128)(2,1)} %convolution_convert_fusion.refs_1_.refs_2_), custom_call_target="tpu_custom_call" | custom-call | bytes 19398656 | tf_op jit(solution)/shard_map/spread/pallas_call | solution.py:1002
  511.7 4.6 dynamic-slice_bitcast_fusion
  516.9 19.3 %normed_grad.3 = (bf16[1024,2048]{1,0:T(8,128)(2,1)}, f32[8,2048]{1,0:T(8,128)}) custom-call(s32[1]{0:T(128)} %bitcast.core_ref.half_ref, bf16[2048,1024]{1,0:T(8,128)(2,1)} %get-tuple-element.228.dgate_ref, bf16[2048,1536]{1,0:T(8,128)(2,1)} %get-tuple-element.257.drest_ref, bf16[2048,2048]{1,0:T(8,128)(2,1)} %tokens_ref.5, ...), custom_call_target="tpu_custom_call" | custom-call | flops 171798691840 | bytes 402653184 | tf_op jit(solution)/shard_map/normed_grad/pallas_call | solution.py:830
  538.0 5.4 add_convert_fusion.1
  550.8 6.1 collective-permute-start.19
  564.5 9.6 %collective-permute-done.19 = bf16[3328,128]{1,0:T(8,128)(2,1)} collective-permute-done((bf16[3328,128]{1,0:T(8,128)(2,1)}, bf16[3328,128]{1,0:T(8,128)(2,1)}, u32[]{:S(2)}, u32[]{:S(2)}) %collective-permute-start.19) | collective-permute-done | bytes 852000 | tf_op jit(solution)/shard_map/ppermute | solution.py:147
  574.1 3.3 fusion.12
  577.4 5.3 collective-permute-start.25
  586.1 6.9 fusion.14
  594.6 3.0 collective-permute-start.28
  597.5 3.4 fusion.18.early_ref
  603.0 17.1 %collective-permute-done.28 = f32[1,91440]{1,0:T(1,128)S(1)} collective-permute-done((f32[1,91440]{1,0:T(1,128)S(1)}, f32[1,91440]{1,0:T(1,128)S(1)}, u32[]{:S(2)}, u32[]{:S(2)}) %collective-permute-start.28) | collective-permute-done | bytes 365792 | tf_op jit(solution)/shard_map/ppermute | solution.py:84
  622.2 3.4 add_convert_fusion.5
  631.1 6.1 add_convert_fusion.4
  637.7 13.6 %collective-permute-done.33 = f32[1,50480]{1,0:T(1,128)S(1)} collective-permute-done((f32[1,50480]{1,0:T(1,128)S(1)}, f32[1,50480]{1,0:T(1,128)S(1)}, u32[]{:S(2)}, u32[]{:S(2)}) %collective-permute-start.33) | collective-permute-done | bytes 201952 | tf_op jit(solution)/shard_map/ppermute | solution.py:84
  659.3 5.8 add_convert_fusion.own_ref
  666.5 3.5 fusion.10.late_ref
  670.0 18.5 %update_tiles.1 = (f32[48,128,128]{2,1,0:T(8,128)}, f32[48,128,128]{2,1,0:T(8,128)}, f32[48,128,128]{2,1,0:T(8,128)}, f32[48,128,128]{2,1,0:T(8,128)}, bf16[48,128,128]{2,1,0:T(8,128)(2,1)}) custom-call(s32[48]{0:T(128)} %select_reduce_fusion.rows_ref, f32[3072,128]{1,0:T(8,128)} %fusion.18.early_ref, f32[3328,128]{1,0:T(8,128)} %fusion.10.late_ref, ...), custom_call_target="tpu_custom_call" | custom-call | flops 1811939328 | bytes 33030144 | tf_op jit(solution)/shard_map/update_tiles/pallas_call | solution.py:1055
  696.6 3.8 pad_maximum_fusion
  700.4 5.8 collective-permute-done.39
  711.7 16.4 %input_grads.1 = f32[2048,2048]{1,0:T(8,128)} custom-call(s32[1]{0:T(128)} %bitcast.core_ref.half_ref, bf16[1024,2048]{1,0:T(8,128)(2,1)} %add_convert_fusion.own_ref, bf16[1024,2048]{1,0:T(8,128)(2,1)} %collective-permute-done.36.other_ref, bf16[2048,2048]{1,0:T(8,128)(2,1)} %tokens_ref.5, bf16[2048,2048]{1,0:T(8,128)(2,1)} %cot_ref.3, f32[1,2048]{1,0:T(1,128)} %bitcast.166), custom_call_target="tpu_custom_call" | custom-call | bytes 41943040 | tf_op jit(solution)/shard_map/input_grads/pallas_call | solution.py:895
  (333 shorter events, 111.4 us)
Async XLA Ops:
  7.2 132.7 %all-gather.4.cloned.1.call-start = ((), (), s32[]{:S(2)}) async-start(), calls=%async_computation.2 | async-start | bytes 9142272 | tf_op jit(solution)/shard_map/all_gather | solution.py:1194
  15.4 218.0 %all-gather.6.cloned.1.call-start = ((), (), s32[]{:S(2)}) async-start(), calls=%async_computation.3 | async-start | bytes 6488064 | tf_op jit(solution)/shard_map/all_gather | solution.py:1195
  18.3 27.0 %collective-permute-start = (f32[8,128]{1,0:T(8,128)S(1)}, f32[8,128]{1,0:T(8,128)S(1)}, u32[]{:S(2)}, u32[]{:S(2)}) collective-permute-start(f32[8,128]{1,0:T(8,128)S(1)} %broadcast_in_dim.140), channel_id=1, source_target_pairs={{0,1},{1,0},{2,3},{3,2},{4,5},{5,4},{6,7},{7,6},{8,9},{9,8},{10,11... | collective-permute-start | bytes 12296 | tf_op jit(solution)/shard_map/ppermute | solution.py:84
  45.3 3.7 collective-permute-start.1
  272.9 1.5 collective-permute-start.2
  275.2 4.3 collective-permute-start.3
  280.2 24.4 %copy-start.40 = (s32[2,1024]{1,0:T(2,128)S(1)}, s32[2,1024]{1,0:T(2,128)}, u32[]{:S(2)}) copy-start(s32[2,1024]{1,0:T(2,128)} %get-tuple-element.373) | copy-start | bytes 24580
  280.2 24.5 %copy-start.46 = (s32[384]{0:T(512)S(1)}, s32[384]{0:T(512)}, u32[]{:S(2)}) copy-start(s32[384]{0:T(512)} %get-tuple-element.415) | copy-start | bytes 4612
  280.2 25.1 %copy-start.38 = (s32[384]{0:T(512)S(1)}, s32[384]{0:T(512)}, u32[]{:S(2)}) copy-start(s32[384]{0:T(512)} %copy-done.37) | copy-start | bytes 4612
  280.2 25.1 %copy-start.45 = (s32[384]{0:T(512)S(1)}, s32[384]{0:T(512)}, u32[]{:S(2)}) copy-start(s32[384]{0:T(512)} %get-tuple-element.457) | copy-start | bytes 4612
  303.8 17.4 %collective-permute-start.4 = (bf16[1024,2048]{1,0:T(8,128)(2,1)}, bf16[1024,2048]{1,0:T(8,128)(2,1)}, u32[]{:S(2)}, u32[]{:S(2)}) collective-permute-start(bf16[1024,2048]{1,0:T(8,128)(2,1)} %get-tuple-element.226), channel_id=1, source_target_pairs={{0,1},{1,0},{2,3},{3,2},{4,5},{5,4},{6,7},{7,6},{8,9},{9,8},{10,11... | collective-permute-start | bytes 12582920 | tf_op jit(solution)/shard_map/ppermute | solution.py:84
  355.4 48.8 %collective-permute-start.6 = (bf16[512,2048]{1,0:T(8,128)(2,1)}, bf16[512,2048]{1,0:T(8,128)(2,1)}, u32[]{:S(2)}, u32[]{:S(2)}) collective-permute-start(bf16[512,2048]{1,0:T(8,128)(2,1)} %get-tuple-element.444), channel_id=1, source_target_pairs={{0,2},{1,3},{2,0},{3,1},{4,6},{5,7},{6,4},{7,5},{8,10},{9,11},{10,... | collective-permute-start | bytes 6291464 | tf_op jit(solution)/shard_map/ppermute | solution.py:84
  358.3 39.1 %collective-permute-start.5 = (bf16[6144,128]{1,0:T(8,128)(2,1)}, bf16[6144,128]{1,0:T(8,128)(2,1)S(1)}, u32[]{:S(2)}, u32[]{:S(2)}) collective-permute-start(bf16[6144,128]{1,0:T(8,128)(2,1)} %pad_maximum_fusion.1), channel_id=1, source_target_pairs={{0,4},{4,0},{8,12},{12,8},{16,20},{20,16},{24,28},{28,24},{1,5},{5... | collective-permute-start | bytes 4718600 | tf_op jit(solution)/shard_map/ppermute | solution.py:84
  394.0 48.6 %collective-permute-start.8 = (f32[1024,384]{1,0:T(8,128)}, f32[1024,384]{1,0:T(8,128)}, u32[]{:S(2)}, u32[]{:S(2)}) collective-permute-start(f32[1024,384]{1,0:T(8,128)} %get-tuple-element.244), channel_id=1, source_target_pairs={{0,1},{1,0},{2,3},{3,2},{4,5},{5,4},{6,7},{7,6},{8,9},{9,8},{10,11... | collective-permute-start | bytes 4718600 | tf_op jit(solution)/shard_map/ppermute | solution.py:84
  394.1 54.4 %collective-permute-start.9 = (bf16[512,2048]{1,0:T(8,128)(2,1)}, bf16[512,2048]{1,0:T(8,128)(2,1)}, u32[]{:S(2)}, u32[]{:S(2)}) collective-permute-start(bf16[512,2048]{1,0:T(8,128)(2,1)} %get-tuple-element.443), channel_id=1, source_target_pairs={{0,2},{1,3},{2,0},{3,1},{4,6},{5,7},{6,4},{7,5},{8,10},{9,11},{10,... | collective-permute-start | bytes 6291464 | tf_op jit(solution)/shard_map/ppermute | solution.py:84
  396.0 82.1 %collective-permute-start.12 = (bf16[6144,128]{1,0:T(8,128)(2,1)}, bf16[6144,128]{1,0:T(8,128)(2,1)}, u32[]{:S(2)}, u32[]{:S(2)}) collective-permute-start(bf16[6144,128]{1,0:T(8,128)(2,1)} %pad_maximum_fusion.2), channel_id=1, source_target_pairs={{0,4},{4,0},{8,12},{12,8},{16,20},{20,16},{24,28},{28,24},{1,5},{5... | collective-permute-start | bytes 4718600 | tf_op jit(solution)/shard_map/ppermute | solution.py:84
  397.4 51.1 %copy-start.5 = (bf16[6144,128]{1,0:T(8,128)(2,1)}, bf16[6144,128]{1,0:T(8,128)(2,1)S(1)}, u32[]{:S(2)}) copy-start(bf16[6144,128]{1,0:T(8,128)(2,1)S(1)} %collective-permute-done.5) | copy-start | bytes 4718596
  405.5 37.1 %copy-start.9 = (f32[1024,384]{1,0:T(8,128)S(1)}, f32[1024,384]{1,0:T(8,128)}, u32[]{:S(2)}) copy-start(f32[1024,384]{1,0:T(8,128)} %get-tuple-element.244) | copy-start | bytes 4718596
  405.5 43.0 %collective-permute-start.7 = (bf16[3072,128]{1,0:T(8,128)(2,1)S(1)}, bf16[3072,128]{1,0:T(8,128)(2,1)}, u32[]{:S(2)}, u32[]{:S(2)}) collective-permute-start(bf16[3072,128]{1,0:T(8,128)(2,1)S(1)} %fusion.13), channel_id=1, source_target_pairs={{0,8},{4,12},{24,16},{28,20},{1,9},{5,13},{25,17},{29,21},{2,10},{... | collective-permute-start | bytes 2359304 | tf_op jit(solution)/shard_map/ppermute | solution.py:147
  442.5 33.8 %collective-permute-start.13 = (f32[1024,384]{1,0:T(8,128)}, f32[1024,384]{1,0:T(8,128)}, u32[]{:S(2)}, u32[]{:S(2)}) collective-permute-start(f32[1024,384]{1,0:T(8,128)} %get-tuple-element.249), channel_id=1, source_target_pairs={{0,1},{1,0},{2,3},{3,2},{4,5},{5,4},{6,7},{7,6},{8,9},{9,8},{10,11... | collective-permute-start | bytes 4718600 | tf_op jit(solution)/shard_map/ppermute | solution.py:84
  451.1 27.0 %collective-permute-start.10 = (bf16[3072,128]{1,0:T(8,128)(2,1)}, bf16[3072,128]{1,0:T(8,128)(2,1)}, u32[]{:S(2)}, u32[]{:S(2)}) collective-permute-start(bf16[3072,128]{1,0:T(8,128)(2,1)} %fusion.20), channel_id=1, source_target_pairs={{0,8},{4,12},{8,16},{12,20},{1,9},{5,13},{9,17},{13,21},{2,10},{6,... | collective-permute-start | bytes 2359304 | tf_op jit(solution)/shard_map/ppermute | solution.py:147
  454.1 24.0 %collective-permute-start.11 = (bf16[3072,128]{1,0:T(8,128)(2,1)}, bf16[3072,128]{1,0:T(8,128)(2,1)}, u32[]{:S(2)}, u32[]{:S(2)}) collective-permute-start(bf16[3072,128]{1,0:T(8,128)(2,1)} %fusion.20), channel_id=1, source_target_pairs={{24,16},{28,20},{16,8},{20,12},{25,17},{29,21},{17,9},{21,13},{26,... | collective-permute-start | bytes 2359304 | tf_op jit(solution)/shard_map/ppermute | solution.py:147
  455.6 22.4 %collective-permute-start.14 = (bf16[1024,384]{1,0:T(8,128)(2,1)}, bf16[1024,384]{1,0:T(8,128)(2,1)}, u32[]{:S(2)}, u32[]{:S(2)}) collective-permute-start(bf16[1024,384]{1,0:T(8,128)(2,1)} %add_convert_fusion.12), channel_id=1, source_target_pairs={{0,2},{1,3},{2,0},{3,1},{4,6},{5,7},{6,4},{7,5},{8,10},{9,11},{10,... | collective-permute-start | bytes 2359304 | tf_op jit(solution)/shard_map/ppermute | solution.py:84
  482.8 28.9 %collective-permute-start.15 = (bf16[3072,128]{1,0:T(8,128)(2,1)}, bf16[3072,128]{1,0:T(8,128)(2,1)S(1)}, u32[]{:S(2)}, u32[]{:S(2)}) collective-permute-start(bf16[3072,128]{1,0:T(8,128)(2,1)} %get-tuple-element.424), channel_id=1, source_target_pairs={{0,8},{4,12},{8,16},{12,20},{16,24},{20,28},{1,9},{5,13},{9,17},{1... | collective-permute-start | bytes 2359304 | tf_op jit(solution)/shard_map/ppermute | solution.py:147
  485.5 26.1 %collective-permute-start.16 = (bf16[3072,128]{1,0:T(8,128)(2,1)S(1)}, bf16[3072,128]{1,0:T(8,128)(2,1)S(1)}, u32[]{:S(2)}, u32[]{:S(2)}) collective-permute-start(bf16[3072,128]{1,0:T(8,128)(2,1)S(1)} %get-tuple-element.423), channel_id=1, source_target_pairs={{24,16},{28,20},{16,8},{20,12},{8,0},{12,4},{25,17},{29,21},{17,9}... | collective-permute-start | bytes 2359304 | tf_op jit(solution)/shard_map/ppermute | solution.py:147
  486.8 24.8 %collective-permute-start.17 = (bf16[1024,384]{1,0:T(8,128)(2,1)S(1)}, bf16[1024,384]{1,0:T(8,128)(2,1)S(1)}, u32[]{:S(2)}, u32[]{:S(2)}) collective-permute-start(bf16[1024,384]{1,0:T(8,128)(2,1)S(1)} %add_convert_fusion.11), channel_id=1, source_target_pairs={{0,2},{1,3},{2,0},{3,1},{4,6},{5,7},{6,4},{7,5},{8,10},{9,11},{10,... | collective-permute-start | bytes 2359304 | tf_op jit(solution)/shard_map/ppermute | solution.py:84
  500.2 37.8 %collective-permute-start.21 = (bf16[1024,2048]{1,0:T(8,128)(2,1)}, bf16[1024,2048]{1,0:T(8,128)(2,1)}, u32[]{:S(2)}, u32[]{:S(2)}) collective-permute-start(bf16[1024,2048]{1,0:T(8,128)(2,1)} %get-tuple-element.262), channel_id=1, source_target_pairs={{0,1},{1,0},{2,3},{3,2},{4,5},{5,4},{6,7},{7,6},{8,9},{9,8},{10,11... | collective-permute-start | bytes 12582920 | tf_op jit(solution)/shard_map/ppermute | solution.py:84
  516.2 21.7 %collective-permute-start.18 = (bf16[3328,128]{1,0:T(8,128)(2,1)}, bf16[3328,128]{1,0:T(8,128)(2,1)}, u32[]{:S(2)}, u32[]{:S(2)}) collective-permute-start(bf16[3328,128]{1,0:T(8,128)(2,1)} %get-tuple-element.430), channel_id=1, source_target_pairs={{0,4},{4,0},{8,12},{12,8},{16,20},{20,16},{24,28},{28,24},{1,5},{5... | collective-permute-start | bytes 2555912 | tf_op jit(solution)/shard_map/ppermute | solution.py:84
  536.1 28.3 %collective-permute-start.20 = (bf16[3328,128]{1,0:T(8,128)(2,1)}, bf16[3328,128]{1,0:T(8,128)(2,1)}, u32[]{:S(2)}, u32[]{:S(2)}) collective-permute-start(bf16[3328,128]{1,0:T(8,128)(2,1)} %get-tuple-element.429), channel_id=1, source_target_pairs={{0,4},{4,0},{8,12},{12,8},{16,20},{20,16},{24,28},{28,24},{1,5},{5... | collective-permute-start | bytes 2555912 | tf_op jit(solution)/shard_map/ppermute | solution.py:84
  546.7 27.4 %collective-permute-start.22 = (bf16[256,2048]{1,0:T(8,128)(2,1)}, bf16[256,2048]{1,0:T(8,128)(2,1)S(1)}, u32[]{:S(2)}, u32[]{:S(2)}) collective-permute-start(bf16[256,2048]{1,0:T(8,128)(2,1)} %get-tuple-element.438), channel_id=1, source_target_pairs={{0,2},{1,3},{2,0},{3,1},{4,6},{5,7},{6,4},{7,5},{8,10},{9,11},{10,... | collective-permute-start | bytes 3145736 | tf_op jit(solution)/shard_map/ppermute | solution.py:84
  550.8 23.2 %collective-permute-start.19 = (bf16[3328,128]{1,0:T(8,128)(2,1)}, bf16[3328,128]{1,0:T(8,128)(2,1)}, u32[]{:S(2)}, u32[]{:S(2)}) collective-permute-start(bf16[3328,128]{1,0:T(8,128)(2,1)} %fusion.21), channel_id=1, source_target_pairs={{0,8},{4,12},{24,16},{28,20},{1,9},{5,13},{25,17},{29,21},{2,10},{... | collective-permute-start | bytes 2555912 | tf_op jit(solution)/shard_map/ppermute | solution.py:147
  562.4 38.8 %collective-permute-start.27 = (bf16[3328,128]{1,0:T(8,128)(2,1)}, bf16[3328,128]{1,0:T(8,128)(2,1)}, u32[]{:S(2)}, u32[]{:S(2)}) collective-permute-start(bf16[3328,128]{1,0:T(8,128)(2,1)} %get-tuple-element.428), channel_id=1, source_target_pairs={{0,4},{4,0},{8,12},{12,8},{16,20},{20,16},{24,28},{28,24},{1,5},{5... | collective-permute-start | bytes 2555912 | tf_op jit(solution)/shard_map/ppermute | solution.py:84
  563.9 38.0 %collective-permute-start.29 = (bf16[256,2048]{1,0:T(8,128)(2,1)}, bf16[256,2048]{1,0:T(8,128)(2,1)}, u32[]{:S(2)}, u32[]{:S(2)}) collective-permute-start(bf16[256,2048]{1,0:T(8,128)(2,1)} %get-tuple-element.437), channel_id=1, source_target_pairs={{0,2},{1,3},{2,0},{3,1},{4,6},{5,7},{6,4},{7,5},{8,10},{9,11},{10,... | collective-permute-start | bytes 3145736 | tf_op jit(solution)/shard_map/ppermute | solution.py:84
  577.4 42.7 %collective-permute-start.25 = (bf16[3328,128]{1,0:T(8,128)(2,1)}, bf16[3328,128]{1,0:T(8,128)(2,1)}, u32[]{:S(2)}, u32[]{:S(2)}) collective-permute-start(bf16[3328,128]{1,0:T(8,128)(2,1)} %fusion.12), channel_id=1, source_target_pairs={{0,8},{4,12},{8,16},{12,20},{1,9},{5,13},{9,17},{13,21},{2,10},{6,... | collective-permute-start | bytes 2555912 | tf_op jit(solution)/shard_map/ppermute | solution.py:147
  582.7 37.4 %collective-permute-start.26 = (bf16[3328,128]{1,0:T(8,128)(2,1)}, bf16[3328,128]{1,0:T(8,128)(2,1)}, u32[]{:S(2)}, u32[]{:S(2)}) collective-permute-start(bf16[3328,128]{1,0:T(8,128)(2,1)} %fusion.12), channel_id=1, source_target_pairs={{24,16},{28,20},{16,8},{20,12},{25,17},{29,21},{17,9},{21,13},{26,... | collective-permute-start | bytes 2555912 | tf_op jit(solution)/shard_map/ppermute | solution.py:147
  594.6 25.6 %collective-permute-start.28 = (f32[1,91440]{1,0:T(1,128)S(1)}, f32[1,91440]{1,0:T(1,128)S(1)}, u32[]{:S(2)}, u32[]{:S(2)}) collective-permute-start(f32[1,91440]{1,0:T(1,128)S(1)} %broadcast_in_dim.147), channel_id=1, source_target_pairs={{0,16},{4,20},{8,24},{12,28},{16,0},{20,4},{24,8},{28,12},{1,17},{... | collective-permute-start | bytes 1097288 | tf_op jit(solution)/shard_map/ppermute | solution.py:84
  601.2 36.0 %collective-permute-start.32 = (bf16[3328,128]{1,0:T(8,128)(2,1)}, bf16[3328,128]{1,0:T(8,128)(2,1)}, u32[]{:S(2)}, u32[]{:S(2)}) collective-permute-start(bf16[3328,128]{1,0:T(8,128)(2,1)} %get-tuple-element.427), channel_id=1, source_target_pairs={{0,4},{4,0},{8,12},{12,8},{16,20},{20,16},{24,28},{28,24},{1,5},{5... | collective-permute-start | bytes 2555912 | tf_op jit(solution)/shard_map/ppermute | solution.py:84
  601.8 35.9 %collective-permute-start.34 = (bf16[256,2048]{1,0:T(8,128)(2,1)}, bf16[256,2048]{1,0:T(8,128)(2,1)}, u32[]{:S(2)}, u32[]{:S(2)}) collective-permute-start(bf16[256,2048]{1,0:T(8,128)(2,1)} %get-tuple-element.435), channel_id=1, source_target_pairs={{0,2},{1,3},{2,0},{3,1},{4,6},{5,7},{6,4},{7,5},{8,10},{9,11},{10,... | collective-permute-start | bytes 3145736 | tf_op jit(solution)/shard_map/ppermute | solution.py:84
  625.6 25.8 %collective-permute-start.30 = (bf16[3328,128]{1,0:T(8,128)(2,1)S(1)}, bf16[3328,128]{1,0:T(8,128)(2,1)S(1)}, u32[]{:S(2)}, u32[]{:S(2)}) collective-permute-start(bf16[3328,128]{1,0:T(8,128)(2,1)S(1)} %get-tuple-element.426), channel_id=1, source_target_pairs={{0,8},{4,12},{8,16},{12,20},{16,24},{20,28},{1,9},{5,13},{9,17},{1... | collective-permute-start | bytes 2555912 | tf_op jit(solution)/shard_map/ppermute | solution.py:147
  626.9 24.4 %collective-permute-start.31 = (bf16[3328,128]{1,0:T(8,128)(2,1)S(1)}, bf16[3328,128]{1,0:T(8,128)(2,1)S(1)}, u32[]{:S(2)}, u32[]{:S(2)}) collective-permute-start(bf16[3328,128]{1,0:T(8,128)(2,1)S(1)} %get-tuple-element.425), channel_id=1, source_target_pairs={{24,16},{28,20},{16,8},{20,12},{8,0},{12,4},{25,17},{29,21},{17,9}... | collective-permute-start | bytes 2555912 | tf_op jit(solution)/shard_map/ppermute | solution.py:147
  628.4 22.9 %collective-permute-start.33 = (f32[1,50480]{1,0:T(1,128)S(1)}, f32[1,50480]{1,0:T(1,128)S(1)}, u32[]{:S(2)}, u32[]{:S(2)}) collective-permute-start(f32[1,50480]{1,0:T(1,128)S(1)} %broadcast_in_dim.148), channel_id=1, source_target_pairs={{0,8},{4,12},{8,0},{12,4},{16,24},{20,28},{24,16},{28,20},{1,9},{5... | collective-permute-start | bytes 605768 | tf_op jit(solution)/shard_map/ppermute | solution.py:84
  637.2 22.1 %collective-permute-start.35 = (bf16[256,2048]{1,0:T(8,128)(2,1)}, bf16[256,2048]{1,0:T(8,128)(2,1)}, u32[]{:S(2)}, u32[]{:S(2)}) collective-permute-start(bf16[256,2048]{1,0:T(8,128)(2,1)} %get-tuple-element.436), channel_id=1, source_target_pairs={{0,2},{1,3},{2,0},{3,1},{4,6},{5,7},{6,4},{7,5},{8,10},{9,11},{10,... | collective-permute-start | bytes 3145736 | tf_op jit(solution)/shard_map/ppermute | solution.py:84
  637.7 53.8 %collective-permute-start.23 = (bf16[512,2048]{1,0:T(8,128)(2,1)}, bf16[512,2048]{1,0:T(8,128)(2,1)}, u32[]{:S(2)}, u32[]{:S(2)}) collective-permute-start(bf16[512,2048]{1,0:T(8,128)(2,1)} %get-tuple-element.421), channel_id=1, source_target_pairs={{0,1},{1,0},{2,3},{3,2},{4,5},{5,4},{6,7},{7,6},{8,9},{9,8},{10,11... | collective-permute-start | bytes 6291464 | tf_op jit(solution)/shard_map/ppermute | solution.py:84
  651.3 42.7 %collective-permute-start.24 = (bf16[512,2048]{1,0:T(8,128)(2,1)S(1)}, bf16[512,2048]{1,0:T(8,128)(2,1)}, u32[]{:S(2)}, u32[]{:S(2)}) collective-permute-start(bf16[512,2048]{1,0:T(8,128)(2,1)S(1)} %get-tuple-element.422), channel_id=1, source_target_pairs={{0,1},{1,0},{2,3},{3,2},{4,5},{5,4},{6,7},{7,6},{8,9},{9,8},{10,11... | collective-permute-start | bytes 6291464 | tf_op jit(solution)/shard_map/ppermute | solution.py:84
  657.2 31.3 %collective-permute-start.37 = (f32[1,30000]{1,0:T(1,128)}, f32[1,30000]{1,0:T(1,128)}, u32[]{:S(2)}, u32[]{:S(2)}) collective-permute-start(f32[1,30000]{1,0:T(1,128)} %broadcast_in_dim.156), channel_id=1, source_target_pairs={{0,4},{4,0},{8,12},{12,8},{16,20},{20,16},{24,28},{28,24},{1,5},{5... | collective-permute-start | bytes 360008 | tf_op jit(solution)/shard_map/ppermute | solution.py:84
  665.2 46.5 %collective-permute-start.36 = (bf16[1024,2048]{1,0:T(8,128)(2,1)}, bf16[1024,2048]{1,0:T(8,128)(2,1)}, u32[]{:S(2)}, u32[]{:S(2)}) collective-permute-start(bf16[1024,2048]{1,0:T(8,128)(2,1)} %add_convert_fusion.own_ref), channel_id=1, source_target_pairs={{0,1},{1,0},{2,3},{3,2},{4,5},{5,4},{6,7},{7,6},{8,9},{9,8},{10,11... | collective-permute-start | bytes 12582920 | tf_op jit(solution)/shard_map/ppermute | solution.py:84
  690.9 5.0 collective-permute-start.38
  696.2 10.0 %collective-permute-start.39 = (f32[1,85248]{1,0:T(1,128)S(1)}, f32[1,85248]{1,0:T(1,128)S(1)}, u32[]{:S(2)}, u32[]{:S(2)}) collective-permute-start(f32[1,85248]{1,0:T(1,128)S(1)} %reshape_add_fusion), channel_id=1, source_target_pairs={{0,2},{1,3},{2,0},{3,1},{4,6},{5,7},{6,4},{7,5},{8,10},{9,11},{10,... | collective-permute-start | bytes 1022984 | tf_op jit(solution)/shard_map/ppermute | solution.py:84
  (45 other events, 451.1 us)
Sparse Core Ops, SparseCore 0:
  15.6 124.2 all-gather.3
  142.6 90.8 all-gather.5

commit v4 on v3

--- a/solution.py
+++ b/solution.py
@@ -1361,13 +1361,10 @@
     small_sums = SharedSums(
         grad_side.reshape(n_dp, -1), jnp.concatenate([own_vector, grad_pre, gbc_sums.reshape(-1)])
     )
-    arrived, d_others[1] = late.third((small_sums.send(), d_others[1]))
-    small_sums.add(arrived)
-    late_share, (arrived, d_others[2], misfit) = late.total(
-        (small_sums.send(), d_others[2], misfit)
-    )
-    small_sums.add(arrived)
-    small_sums.finish()
+    d_others[1] = late.third(d_others[1])
+    late_share, (d_others[2], misfit, small_sums.owned, small_sums.shared) = late.total(
+        (d_others[2], misfit, small_sums.owned, small_sums.shared)
+    )
 
     def repaired(grads):
         again = spread(plans[2][0], grads, n_dp * plans[2][1])
@@ -1391,14 +1388,23 @@
         left_roots[0],
         right_roots[0],
     )
+    arrived, tiles_copy = tied(small_sums.send(), tiles_copy)
+    small_sums.add(arrived)
+    small_sums.finish()
     split_at = own_vector.shape[0]
     side_own, all_vector = small_sums.owned, small_sums.shared
     quarters = jnp.where(
         (jnp.arange(n_tensor) == tensor_rank)[:, None], side_own, jnp.zeros((), F32)
     )
-    common = sum_over(
-        jnp.concatenate([quarters.reshape(-1), all_vector[split_at:]])[None], "tensor"
-    )[0]
+    common = jnp.concatenate([quarters.reshape(-1), all_vector[split_at:]])[None]
+    common = common + swap(common, "tensor", 1)
+    common_other = swap(common, "tensor", 2)
+    d_half = (d_chip.astype(F32) + jnp.concatenate(d_others).astype(F32)).astype(BF16)
+    input_grad = input_grads(
+        core_at, d_half, swap(d_half, "tensor", 1), tokens, cotangent, pre_gain[None, :]
+    )
+    common_other, input_grad = tied(common_other, input_grad)
+    common = (common + common_other)[0]
     side_share = common[: side_weight.size].reshape(side_weight.shape)
     common = common[side_weight.size :]
     quarter = half // 2
@@ -1417,11 +1423,6 @@
         axis=0,
     )
 
-    d_half = (d_chip.astype(F32) + jnp.concatenate(d_others).astype(F32)).astype(BF16)
-    input_grad = input_grads(
-        core_at, d_half, swap(d_half, "tensor", 1), tokens, cotangent, pre_gain[None, :]
-    )
-
     pre_share = lax.dynamic_slice_in_dim(common[:D], tensor_rank * model_local, model_local, 0)
     bc_share = lax.dynamic_slice_in_dim(
         common[D:].reshape(CONV + 1, 2 * NS), tensor_rank * bc_local, bc_local, 1

time: 740 us -> 717 us (0.969)
  waiting for transfers between devices: 188 us -> 156 us
    ppermute x30, waiting for transfers between devices: 54 us -> 25.6 us  [swap(): return lax.ppermute(value, axis, [(i, i ^ bit) for i in range(size)])]
    ppermute x10, starting transfers between devices: 27.3 us -> 35 us  [hop(): return lax.ppermute(value.astype(BF16), 'dp', pairs)]
  transfers between devices with their start and end apart: 42 -> 42, of which waited for: 13 -> 14; matrix products, arithmetic and copies ran while one was open for 20% -> 21% of each run, Pallas kernels for 26% -> 29%
where the time goes in v4:
time: 717 us; the launch traced here: 712 us
  Pallas kernels  279 us (39%)
  waiting for transfers between devices  156 us (22%)
  other arithmetic  109 us (15%)
  starting transfers between devices  54 us (8%)
  matrix products  47.1 us (7%)
  local copies, waits for them, and re-layouts  42.5 us (6%)
  between operations  16.9 us (2%)
    all_gather x1, waiting for transfers between devices, on_device(): first_held = lax.all_gather(first_share, 'dp', axis=0, tiled=True)  90.3 us
    pallas_call x2, Pallas kernels, ssd_backward(): pl.pallas_call(ssd_backward_kernel, grid=(blocks,), in_specs=[pl.BlockSpe...  67.7 us
    dot_general x4, matrix products, contract_rows(): lax.dot_general(left, right, (((0,), (0,)), ((), ())), preferred_element_...  47.1 us
    pallas_call x2, Pallas kernels, normed_grad(): pl.pallas_call(normed_grad_kernel, grid_spec=pltpu.PrefetchScalarGridSpec...  38.5 us
    ppermute x10, starting transfers between devices, hop(): return lax.ppermute(value.astype(BF16), 'dp', pairs)  35 us
    all_gather x1, waiting for transfers between devices, on_device(): second_held = lax.all_gather(mine[cut:], 'dp', axis=0, tiled=True)  34.3 us
    pallas_call x1, Pallas kernels, ssd_forward(): pl.pallas_call(ssd_forward_kernel, grid=(sequences, blocks), in_specs=[pl...  28 us
    pallas_call x1, Pallas kernels, gate_project(): pl.pallas_call(gate_kernel, grid=(rows // step,), in_specs=[pl.BlockSpec(...  26.4 us
  transfers between devices with their start and end apart: 42, of which 14 were waited for; matrix products, arithmetic and copies ran while one was open for 21% of the time, Pallas kernels for 29%

profile of v4, /device:TPU:0, one launch (start us, length us, event | category | flops | bytes accessed | tf_op | source)
XLA Modules:
  0.0 712.3 jit_solution(7580195014756538919)
XLA Ops:
  18.8 6.4 all-gather
  28.2 5.1 fusion.2
  36.4 8.8 %fusion.4.left_ref.normed_ref = bf16[2048,2048]{1,0:T(8,128)(2,1)} fusion(bf16[2048,2048]{1,0:T(8,128)(2,1)} %tokens_ref.5, f32[2048]{0:T(1024)S(1)} %bitcast.165, f32[2048]{0:T(1024)S(1)} %add_rsqrt_fusion), kind=kLoop, calls=%fused_computation.7 | loop fusion | flops 16777216 | bytes 16793600 | tf_op jit(solution)/shard_map/convert_element_type | solution.py:1231
  49.6 90.3 %all-gather.4.cloned.1.call-done.refs_0_ = bf16[31744,128]{1,0:T(8,128)(2,1)} async-done(((bf16[3968,128]{1,0:T(8,128)(2,1)}), bf16[31744,128]{1,0:T(8,128)(2,1)}) %all-gather.4.cloned.1.call-update) | async-done | bytes 8126480 | tf_op jit(solution)/shard_map/all_gather | solution.py:1194
  143.4 7.7 %assemble.3.right_ref = bf16[2048,1536]{1,0:T(8,128)(2,1)} custom-call(s32[128]{0:T(128)} %get-tuple-element.471.rows_ref, bf16[31744,128]{1,0:T(8,128)(2,1)} %all-gather.4.cloned.1.call-done.refs_0_, bf16[2048,512]{1,0:T(8,128)(2,1)S(1)} %maximum_maximum_fusion.refs_1_), custom_call_target="tpu_custom_call" | custom-call | bytes 16252928 | tf_op jit(solution)/shard_map/assemble/pallas_call | solution.py:968
  151.1 18.8 %project.2.rest_ref.prev_ref = f32[2048,1536]{1,0:T(8,128)} custom-call(bf16[2048,2048]{1,0:T(8,128)(2,1)} %fusion.4.left_ref.normed_ref, bf16[2048,1536]{1,0:T(8,128)(2,1)} %assemble.3.right_ref), custom_call_target="tpu_custom_call" | custom-call | flops 12884901888 | bytes 27262976 | tf_op jit(solution)/shard_map/project/pallas_call | solution.py:638
  171.1 28.0 %ssd_forward.2 = (f32[2048,1024]{1,0:T(8,128)}, f32[16,128,1024]{2,1,0:T(8,128)}) custom-call(f32[2048,1536]{1,0:T(8,128)} %project.2.rest_ref.prev_ref, f32[2048,1536]{1,0:T(8,128)} %project.2.rest_ref.prev_ref, f32[2048,128]{1,0:T(8,128)} %broadcast_in_dim.141.start_ref.refs_5_.refs_6_, f32[8,1024]{1,0:T(8,128)S(1)} %concatenate.77.par_ref.refs_8_.refs_9_, ...), custom_call_target="tpu_custom_call" | custom-call | flops 10737418240 | bytes 41943040 | tf_op jit(solution)/shard_map/ssd_forward/pallas_call | solution.py:524
  199.1 34.3 %all-gather.6.cloned.1.call-done.refs_1_ = bf16[22528,128]{1,0:T(8,128)(2,1)} async-done(((bf16[2816,128]{1,0:T(8,128)(2,1)}), bf16[22528,128]{1,0:T(8,128)(2,1)}) %all-gather.6.cloned.1.call-update) | async-done | bytes 5767184 | tf_op jit(solution)/shard_map/all_gather | solution.py:1195
  234.6 12.0 %assemble.4 = (bf16[2048,1024]{1,0:T(8,128)(2,1)}, bf16[1024,2048]{1,0:T(8,128)(2,1)}) custom-call(s32[256]{0:T(256)} %pad_add_fusion.rows_ref, bf16[31744,128]{1,0:T(8,128)(2,1)} %get-tuple-element.538, bf16[22528,128]{1,0:T(8,128)(2,1)} %get-tuple-element.540), custom_call_target="tpu_custom_call" | custom-call | bytes 27787264 | tf_op jit(solution)/shard_map/assemble/pallas_call | solution.py:968
  246.6 26.4 %gate_project.1 = (f32[2048,1024]{1,0:T(8,128)}, f32[2048,1024]{1,0:T(8,128)}, f32[8,2048]{1,0:T(8,128)}) custom-call(bf16[2048,2048]{1,0:T(8,128)(2,1)} %get-tuple-element.543, bf16[2048,2048]{1,0:T(8,128)(2,1)} %cot_ref.3, bf16[2048,1024]{1,0:T(8,128)(2,1)} %get-tuple-element.223.wgate_ref, bf16[1024,2048]{1,0:T(8,128)(2,1)} %get-tuple-element.224.wout_ref, ...), custom_call_target="tpu_custom_call" | custom-call | flops 17179869184 | bytes 33554432 | tf_op jit(solution)/shard_map/gate_project/pallas_call | solution.py:680
  276.9 2.8 collective-permute-done.3
  280.3 23.6 %gated_pass.1 = (bf16[2048,1024]{1,0:T(8,128)(2,1)}, bf16[2048,1024]{1,0:T(8,128)(2,1)}, f32[2048,1024]{1,0:T(8,128)}, f32[8,1024]{1,0:T(8,128)}, bf16[1024,2048...) custom-call(s32[1]{0:T(128)} %bitcast.core_ref.half_ref, f32[2048,1024]{1,0:T(8,128)} %get-tuple-element.222.ssd_ref, ...), custom_call_target="tpu_custom_call" | custom-call | flops 8589934592 | bytes 41943040 | tf_op jit(solution)/shard_map/gated_pass/pallas_call | solution.py:765
  306.7 14.4 %convolution_convert_fusion.refs_1_.refs_2_ = bf16[1024,2048]{1,0:T(8,128)(2,1)} fusion(bf16[2048,1024]{1,0:T(8,128)(2,1)} %get-tuple-element.233, bf16[2048,2048]{1,0:T(8,128)(2,1)} %cot_ref.3), kind=kOutput, calls=%fused_computation.19 | convolution fusion | flops 8592031744 | bytes 16777216 | tf_op jit(solution)/shard_map/dot_general | solution.py:75
  321.1 6.2 add_convert_fusion.2
  327.3 13.0 %convolution_convert_fusion.1.refs_0_ = bf16[2048,1024]{1,0:T(8,128)(2,1)} fusion(bf16[2048,2048]{1,0:T(8,128)(2,1)} %get-tuple-element.543, bf16[2048,1024]{1,0:T(8,128)(2,1)S(1)} %copy-done.48), kind=kOutput, calls=%fused_computation.20 | convolution fusion | flops 8592031744 | bytes 16777216 | tf_op jit(solution)/shard_map/dot_general | solution.py:75
  340.3 9.9 %spread.4 = bf16[24576,128]{1,0:T(8,128)(2,1)} custom-call(s32[256]{0:T(256)} %pad_add_fusion.1.rows_ref, bf16[2048,1024]{1,0:T(8,128)(2,1)} %convolution_convert_fusion.1.refs_0_, bf16[1024,2048]{1,0:T(8,128)(2,1)} %convolution_convert_fusion.refs_1_.refs_2_), custom_call_target="tpu_custom_call" | custom-call | bytes 14680064 | tf_op jit(solution)/shard_map/spread/pallas_call | solution.py:1002
  350.2 5.0 fusion.41
  360.0 33.8 %ssd_backward.2 = (bf16[2048,1536]{1,0:T(8,128)(2,1)}, f32[1024,384]{1,0:T(8,128)}, f32[48,1024]{1,0:T(8,128)}, f32[40,256]{1,0:T(8,128)}, f32[16,128]{1,0:T(8,128)}) custom-call(s32[1]{0:T(128)} %bitcast.16.refs_0_.refs_1_, f32[2048,1536]{1,0:T(8,128)} %get-tuple-element.235.refs_1_.refs_2_.refs_3_, ...), custom_call_target="tpu_custom_call" | custom-call | flops 13421772800 | bytes 20971520 | tf_op jit(solution)/shard_map/ssd_backward/pallas_call | solution.py:568
  397.2 6.7 collective-permute-done.6
  405.3 3.1 collective-permute-start.7
  408.5 33.9 %ssd_backward.3 = (bf16[2048,1536]{1,0:T(8,128)(2,1)}, f32[1024,384]{1,0:T(8,128)}, f32[48,1024]{1,0:T(8,128)}, f32[40,256]{1,0:T(8,128)}, f32[16,128]{1,0:T(8,128)}) custom-call(bf16[2048,1536]{1,0:T(8,128)(2,1)} %get-tuple-element.241.refs_0_, s32[1]{0:T(128)} %bitcast.16.refs_0_.refs_1_, ...), custom_call_target="tpu_custom_call", output_to_operand_aliasing={{0}: (0, {})} | custom-call | flops 13421772800 | bytes 20971520 | tf_op jit(solution)/shard_map/ssd_backward/pallas_call | solution.py:568
  444.9 3.4 collective-permute-done.9
  448.3 2.6 fusion.20
  450.9 3.0 collective-permute-start.10
  456.9 19.2 %normed_grad.2 = (bf16[1024,2048]{1,0:T(8,128)(2,1)}, f32[8,2048]{1,0:T(8,128)}) custom-call(s32[1]{0:T(128)S(6)} %sub.101.half_ref, bf16[2048,1024]{1,0:T(8,128)(2,1)} %get-tuple-element.232.dgate_ref, bf16[2048,1536]{1,0:T(8,128)(2,1)} %get-tuple-element.261.drest_ref, bf16[2048,2048]{1,0:T(8,128)(2,1)} %tokens_ref.5, ...), custom_call_target="tpu_custom_call" | custom-call | flops 171798691840 | bytes 402653184 | tf_op jit(solution)/shard_map/normed_grad/pallas_call | solution.py:830
  478.0 4.6 add_convert_fusion.9
  482.6 2.7 collective-permute-start.15
  487.2 12.7 %fusion.7.refs_1_ = bf16[2048,1024]{1,0:T(8,128)(2,1)} fusion(bf16[2048,2048]{1,0:T(8,128)(2,1)S(1)} %copy-done.2, bf16[2048,1536]{1,0:T(8,128)(2,1)} %get-tuple-element.261.drest_ref), kind=kOutput, calls=%fused_computation.18 | convolution fusion | flops 8592031744 | bytes 16777216 | tf_op jit(solution)/shard_map/dot_general | solution.py:75
  500.0 11.5 %spread.5 = bf16[26624,128]{1,0:T(8,128)(2,1)} custom-call(s32[384]{0:T(512)} %get-tuple-element.466.rows_ref, bf16[2048,1024]{1,0:T(8,128)(2,1)} %convolution_convert_fusion.1.refs_0_, bf16[2048,1024]{1,0:T(8,128)(2,1)} %fusion.7.refs_1_, bf16[1024,2048]{1,0:T(8,128)(2,1)} %convolution_convert_fusion.refs_1_.refs_2_), custom_call_target="tpu_custom_call" | custom-call | bytes 19398656 | tf_op jit(solution)/shard_map/spread/pallas_call | solution.py:1002
  511.5 4.6 dynamic-slice_bitcast_fusion
  516.7 19.3 %normed_grad.3 = (bf16[1024,2048]{1,0:T(8,128)(2,1)}, f32[8,2048]{1,0:T(8,128)}) custom-call(s32[1]{0:T(128)} %bitcast.core_ref.half_ref, bf16[2048,1024]{1,0:T(8,128)(2,1)} %get-tuple-element.232.dgate_ref, bf16[2048,1536]{1,0:T(8,128)(2,1)} %get-tuple-element.261.drest_ref, bf16[2048,2048]{1,0:T(8,128)(2,1)} %tokens_ref.5, ...), custom_call_target="tpu_custom_call" | custom-call | flops 171798691840 | bytes 402653184 | tf_op jit(solution)/shard_map/normed_grad/pallas_call | solution.py:830
  537.8 5.4 add_convert_fusion.1
  550.2 6.0 collective-permute-start.19
  574.4 2.9 fusion.12
  577.3 5.4 collective-permute-start.25
  584.3 2.9 fusion.18.early_ref
  592.7 5.4 collective-permute-done.28
  599.0 4.4 add_convert_fusion.5
  603.4 9.0 %collective-permute-start.29 = (bf16[3328,128]{1,0:T(8,128)(2,1)}, bf16[3328,128]{1,0:T(8,128)(2,1)}, u32[]{:S(2)}, u32[]{:S(2)}) collective-permute-start(bf16[3328,128]{1,0:T(8,128)(2,1)} %get-tuple-element.434), channel_id=1, source_target_pairs={{0,8},{4,12},{8,16},{12,20},{16,24},{20,28},{1,9},{5,13},{9,17},{1... | collective-permute-start | bytes 2555912 | tf_op jit(solution)/shard_map/ppermute | solution.py:147
  613.7 6.9 fusion.14
  621.0 6.9 add_convert_fusion.4
  628.5 4.0 collective-permute-done.30
  633.2 3.5 fusion.10.late_ref
  638.6 18.4 %update_tiles.1 = (f32[48,128,128]{2,1,0:T(8,128)}, f32[48,128,128]{2,1,0:T(8,128)}, f32[48,128,128]{2,1,0:T(8,128)}, f32[48,128,128]{2,1,0:T(8,128)}, bf16[48,128,128]{2,1,0:T(8,128)(2,1)}) custom-call(s32[48]{0:T(128)} %select_reduce_fusion.rows_ref, f32[3072,128]{1,0:T(8,128)} %fusion.18.early_ref, f32[3328,128]{1,0:T(8,128)} %fusion.10.late_ref, ...), custom_call_target="tpu_custom_call" | custom-call | flops 1811939328 | bytes 33030144 | tf_op jit(solution)/shard_map/update_tiles/pallas_call | solution.py:1055
  660.6 8.8 %add_convert_fusion.own_ref = bf16[1024,2048]{1,0:T(8,128)(2,1)} fusion(bf16[1024,2048]{1,0:T(8,128)(2,1)} %copy-done, bf16[256,2048]{1,0:T(8,128)(2,1)} %collective-permute-done.38, bf16[256,2048]{1,0:T(8,128)(2,1)} %collective-permute-done.32, bf16[256,2048]{1,0:T(8,128)(2,1)S(1)} %copy-done.18, bf16[256,2048]{1,0:T(8,128)(2,1)S(1)} %copy-done.16), kind=kLoop, calls=%fused_computation.9 | loop fusion | flops 23068672 | bytes 12582912 | tf_op jit(solution)/shard_map/convert_element_type | solution.py:1402
  673.4 2.6 collective-permute-done.35
  679.2 3.9 pad_maximum_fusion
  683.1 16.6 %input_grads.1 = f32[2048,2048]{1,0:T(8,128)} custom-call(s32[1]{0:T(128)} %bitcast.core_ref.half_ref, bf16[1024,2048]{1,0:T(8,128)(2,1)} %add_convert_fusion.own_ref, bf16[1024,2048]{1,0:T(8,128)(2,1)} %collective-permute-done.39.other_ref, bf16[2048,2048]{1,0:T(8,128)(2,1)} %tokens_ref.5, bf16[2048,2048]{1,0:T(8,128)(2,1)} %cot_ref.3, f32[1,2048]{1,0:T(1,128)} %bitcast.166), custom_call_target="tpu_custom_call" | custom-call | bytes 41943040 | tf_op jit(solution)/shard_map/input_grads/pallas_call | solution.py:895
  (330 shorter events, 109.9 us)
Async XLA Ops:
  7.2 132.7 %all-gather.4.cloned.1.call-start = ((), (), s32[]{:S(2)}) async-start(), calls=%async_computation.2 | async-start | bytes 9142272 | tf_op jit(solution)/shard_map/all_gather | solution.py:1194
  15.4 218.0 %all-gather.6.cloned.1.call-start = ((), (), s32[]{:S(2)}) async-start(), calls=%async_computation.3 | async-start | bytes 6488064 | tf_op jit(solution)/shard_map/all_gather | solution.py:1195
  18.2 27.1 %collective-permute-start = (f32[8,128]{1,0:T(8,128)S(1)}, f32[8,128]{1,0:T(8,128)S(1)}, u32[]{:S(2)}, u32[]{:S(2)}) collective-permute-start(f32[8,128]{1,0:T(8,128)S(1)} %broadcast_in_dim.140), channel_id=1, source_target_pairs={{0,1},{1,0},{2,3},{3,2},{4,5},{5,4},{6,7},{7,6},{8,9},{9,8},{10,11... | collective-permute-start | bytes 12296 | tf_op jit(solution)/shard_map/ppermute | solution.py:84
  45.3 3.7 collective-permute-start.1
  273.0 1.5 collective-permute-start.2
  275.3 4.3 collective-permute-start.3
  280.3 23.8 %copy-start.32 = (f32[1,1,2,1024]{3,2,1,0:T(2,128)S(1)}, f32[1,1,2,1024]{3,2,1,0:T(2,128)}, u32[]{:S(2)}) copy-start(f32[1,1,2,1024]{3,2,1,0:T(2,128)} %get-tuple-element.463) | copy-start | bytes 24580
  280.3 24.4 %copy-start.40 = (s32[2,1024]{1,0:T(2,128)S(1)}, s32[2,1024]{1,0:T(2,128)}, u32[]{:S(2)}) copy-start(s32[2,1024]{1,0:T(2,128)} %get-tuple-element.381) | copy-start | bytes 24580
  280.3 24.9 %copy-start.42 = (s32[384]{0:T(512)S(1)}, s32[384]{0:T(512)}, u32[]{:S(2)}) copy-start(s32[384]{0:T(512)} %get-tuple-element.423) | copy-start | bytes 4612
  303.9 17.2 %collective-permute-start.4 = (bf16[1024,2048]{1,0:T(8,128)(2,1)}, bf16[1024,2048]{1,0:T(8,128)(2,1)}, u32[]{:S(2)}, u32[]{:S(2)}) collective-permute-start(bf16[1024,2048]{1,0:T(8,128)(2,1)} %get-tuple-element.230), channel_id=1, source_target_pairs={{0,1},{1,0},{2,3},{3,2},{4,5},{5,4},{6,7},{7,6},{8,9},{9,8},{10,11... | collective-permute-start | bytes 12582920 | tf_op jit(solution)/shard_map/ppermute | solution.py:84
  355.2 48.8 %collective-permute-start.6 = (bf16[512,2048]{1,0:T(8,128)(2,1)}, bf16[512,2048]{1,0:T(8,128)(2,1)}, u32[]{:S(2)}, u32[]{:S(2)}) collective-permute-start(bf16[512,2048]{1,0:T(8,128)(2,1)} %get-tuple-element.452), channel_id=1, source_target_pairs={{0,2},{1,3},{2,0},{3,1},{4,6},{5,7},{6,4},{7,5},{8,10},{9,11},{10,... | collective-permute-start | bytes 6291464 | tf_op jit(solution)/shard_map/ppermute | solution.py:84
  358.1 39.1 %collective-permute-start.5 = (bf16[6144,128]{1,0:T(8,128)(2,1)}, bf16[6144,128]{1,0:T(8,128)(2,1)S(1)}, u32[]{:S(2)}, u32[]{:S(2)}) collective-permute-start(bf16[6144,128]{1,0:T(8,128)(2,1)} %pad_maximum_fusion.1), channel_id=1, source_target_pairs={{0,4},{4,0},{8,12},{12,8},{16,20},{20,16},{24,28},{28,24},{1,5},{5... | collective-permute-start | bytes 4718600 | tf_op jit(solution)/shard_map/ppermute | solution.py:84
  393.8 48.6 %collective-permute-start.8 = (f32[1024,384]{1,0:T(8,128)}, f32[1024,384]{1,0:T(8,128)}, u32[]{:S(2)}, u32[]{:S(2)}) collective-permute-start(f32[1024,384]{1,0:T(8,128)} %get-tuple-element.248), channel_id=1, source_target_pairs={{0,1},{1,0},{2,3},{3,2},{4,5},{5,4},{6,7},{7,6},{8,9},{9,8},{10,11... | collective-permute-start | bytes 4718600 | tf_op jit(solution)/shard_map/ppermute | solution.py:84
  393.9 54.4 %collective-permute-start.9 = (bf16[512,2048]{1,0:T(8,128)(2,1)}, bf16[512,2048]{1,0:T(8,128)(2,1)}, u32[]{:S(2)}, u32[]{:S(2)}) collective-permute-start(bf16[512,2048]{1,0:T(8,128)(2,1)} %get-tuple-element.451), channel_id=1, source_target_pairs={{0,2},{1,3},{2,0},{3,1},{4,6},{5,7},{6,4},{7,5},{8,10},{9,11},{10,... | collective-permute-start | bytes 6291464 | tf_op jit(solution)/shard_map/ppermute | solution.py:84
  395.7 82.1 %collective-permute-start.12 = (bf16[6144,128]{1,0:T(8,128)(2,1)}, bf16[6144,128]{1,0:T(8,128)(2,1)}, u32[]{:S(2)}, u32[]{:S(2)}) collective-permute-start(bf16[6144,128]{1,0:T(8,128)(2,1)} %pad_maximum_fusion.2), channel_id=1, source_target_pairs={{0,4},{4,0},{8,12},{12,8},{16,20},{20,16},{24,28},{28,24},{1,5},{5... | collective-permute-start | bytes 4718600 | tf_op jit(solution)/shard_map/ppermute | solution.py:84
  397.2 51.1 %copy-start.4 = (bf16[6144,128]{1,0:T(8,128)(2,1)}, bf16[6144,128]{1,0:T(8,128)(2,1)S(1)}, u32[]{:S(2)}) copy-start(bf16[6144,128]{1,0:T(8,128)(2,1)S(1)} %collective-permute-done.5) | copy-start | bytes 4718596
  405.3 37.1 %copy-start.8 = (f32[1024,384]{1,0:T(8,128)S(1)}, f32[1024,384]{1,0:T(8,128)}, u32[]{:S(2)}) copy-start(f32[1024,384]{1,0:T(8,128)} %get-tuple-element.248) | copy-start | bytes 4718596
  405.3 43.0 %collective-permute-start.7 = (bf16[3072,128]{1,0:T(8,128)(2,1)S(1)}, bf16[3072,128]{1,0:T(8,128)(2,1)}, u32[]{:S(2)}, u32[]{:S(2)}) collective-permute-start(bf16[3072,128]{1,0:T(8,128)(2,1)S(1)} %fusion.13), channel_id=1, source_target_pairs={{0,8},{4,12},{24,16},{28,20},{1,9},{5,13},{25,17},{29,21},{2,10},{... | collective-permute-start | bytes 2359304 | tf_op jit(solution)/shard_map/ppermute | solution.py:147
  442.3 33.8 %collective-permute-start.13 = (f32[1024,384]{1,0:T(8,128)}, f32[1024,384]{1,0:T(8,128)}, u32[]{:S(2)}, u32[]{:S(2)}) collective-permute-start(f32[1024,384]{1,0:T(8,128)} %get-tuple-element.253), channel_id=1, source_target_pairs={{0,1},{1,0},{2,3},{3,2},{4,5},{5,4},{6,7},{7,6},{8,9},{9,8},{10,11... | collective-permute-start | bytes 4718600 | tf_op jit(solution)/shard_map/ppermute | solution.py:84
  450.9 27.0 %collective-permute-start.10 = (bf16[3072,128]{1,0:T(8,128)(2,1)}, bf16[3072,128]{1,0:T(8,128)(2,1)}, u32[]{:S(2)}, u32[]{:S(2)}) collective-permute-start(bf16[3072,128]{1,0:T(8,128)(2,1)} %fusion.20), channel_id=1, source_target_pairs={{0,8},{4,12},{8,16},{12,20},{1,9},{5,13},{9,17},{13,21},{2,10},{6,... | collective-permute-start | bytes 2359304 | tf_op jit(solution)/shard_map/ppermute | solution.py:147
  453.9 24.0 %collective-permute-start.11 = (bf16[3072,128]{1,0:T(8,128)(2,1)}, bf16[3072,128]{1,0:T(8,128)(2,1)}, u32[]{:S(2)}, u32[]{:S(2)}) collective-permute-start(bf16[3072,128]{1,0:T(8,128)(2,1)} %fusion.20), channel_id=1, source_target_pairs={{24,16},{28,20},{16,8},{20,12},{25,17},{29,21},{17,9},{21,13},{26,... | collective-permute-start | bytes 2359304 | tf_op jit(solution)/shard_map/ppermute | solution.py:147
  455.5 22.4 %collective-permute-start.14 = (bf16[1024,384]{1,0:T(8,128)(2,1)}, bf16[1024,384]{1,0:T(8,128)(2,1)}, u32[]{:S(2)}, u32[]{:S(2)}) collective-permute-start(bf16[1024,384]{1,0:T(8,128)(2,1)} %add_convert_fusion.12), channel_id=1, source_target_pairs={{0,2},{1,3},{2,0},{3,1},{4,6},{5,7},{6,4},{7,5},{8,10},{9,11},{10,... | collective-permute-start | bytes 2359304 | tf_op jit(solution)/shard_map/ppermute | solution.py:84
  482.6 28.8 %collective-permute-start.15 = (bf16[3072,128]{1,0:T(8,128)(2,1)}, bf16[3072,128]{1,0:T(8,128)(2,1)S(1)}, u32[]{:S(2)}, u32[]{:S(2)}) collective-permute-start(bf16[3072,128]{1,0:T(8,128)(2,1)} %get-tuple-element.432), channel_id=1, source_target_pairs={{0,8},{4,12},{8,16},{12,20},{16,24},{20,28},{1,9},{5,13},{9,17},{1... | collective-permute-start | bytes 2359304 | tf_op jit(solution)/shard_map/ppermute | solution.py:147
  485.3 26.1 %collective-permute-start.16 = (bf16[3072,128]{1,0:T(8,128)(2,1)S(1)}, bf16[3072,128]{1,0:T(8,128)(2,1)S(1)}, u32[]{:S(2)}, u32[]{:S(2)}) collective-permute-start(bf16[3072,128]{1,0:T(8,128)(2,1)S(1)} %get-tuple-element.431), channel_id=1, source_target_pairs={{24,16},{28,20},{16,8},{20,12},{8,0},{12,4},{25,17},{29,21},{17,9}... | collective-permute-start | bytes 2359304 | tf_op jit(solution)/shard_map/ppermute | solution.py:147
  486.6 24.8 %collective-permute-start.17 = (bf16[1024,384]{1,0:T(8,128)(2,1)S(1)}, bf16[1024,384]{1,0:T(8,128)(2,1)S(1)}, u32[]{:S(2)}, u32[]{:S(2)}) collective-permute-start(bf16[1024,384]{1,0:T(8,128)(2,1)S(1)} %add_convert_fusion.11), channel_id=1, source_target_pairs={{0,2},{1,3},{2,0},{3,1},{4,6},{5,7},{6,4},{7,5},{8,10},{9,11},{10,... | collective-permute-start | bytes 2359304 | tf_op jit(solution)/shard_map/ppermute | solution.py:84
  500.0 37.8 %collective-permute-start.21 = (bf16[1024,2048]{1,0:T(8,128)(2,1)}, bf16[1024,2048]{1,0:T(8,128)(2,1)}, u32[]{:S(2)}, u32[]{:S(2)}) collective-permute-start(bf16[1024,2048]{1,0:T(8,128)(2,1)} %get-tuple-element.266), channel_id=1, source_target_pairs={{0,1},{1,0},{2,3},{3,2},{4,5},{5,4},{6,7},{7,6},{8,9},{9,8},{10,11... | collective-permute-start | bytes 12582920 | tf_op jit(solution)/shard_map/ppermute | solution.py:84
  516.0 21.7 %collective-permute-start.18 = (bf16[3328,128]{1,0:T(8,128)(2,1)}, bf16[3328,128]{1,0:T(8,128)(2,1)}, u32[]{:S(2)}, u32[]{:S(2)}) collective-permute-start(bf16[3328,128]{1,0:T(8,128)(2,1)} %get-tuple-element.438), channel_id=1, source_target_pairs={{0,4},{4,0},{8,12},{12,8},{16,20},{20,16},{24,28},{28,24},{1,5},{5... | collective-permute-start | bytes 2555912 | tf_op jit(solution)/shard_map/ppermute | solution.py:84
  536.0 35.9 %collective-permute-start.20 = (bf16[3328,128]{1,0:T(8,128)(2,1)S(1)}, bf16[3328,128]{1,0:T(8,128)(2,1)}, u32[]{:S(2)}, u32[]{:S(2)}) collective-permute-start(bf16[3328,128]{1,0:T(8,128)(2,1)S(1)} %copy-done.19), channel_id=1, source_target_pairs={{0,4},{4,0},{8,12},{12,8},{16,20},{20,16},{24,28},{28,24},{1,5},{5... | collective-permute-start | bytes 2555912 | tf_op jit(solution)/shard_map/ppermute | solution.py:84
  546.1 21.2 %copy-start.25 = (f32[48,1024]{1,0:T(8,128)S(1)}, f32[48,1024]{1,0:T(8,128)}, u32[]{:S(2)}) copy-start(f32[48,1024]{1,0:T(8,128)} %get-tuple-element.284) | copy-start | bytes 589828
  546.2 27.3 %collective-permute-start.22 = (bf16[256,2048]{1,0:T(8,128)(2,1)}, bf16[256,2048]{1,0:T(8,128)(2,1)S(1)}, u32[]{:S(2)}, u32[]{:S(2)}) collective-permute-start(bf16[256,2048]{1,0:T(8,128)(2,1)} %get-tuple-element.446), channel_id=1, source_target_pairs={{0,2},{1,3},{2,0},{3,1},{4,6},{5,7},{6,4},{7,5},{8,10},{9,11},{10,... | collective-permute-start | bytes 3145736 | tf_op jit(solution)/shard_map/ppermute | solution.py:84
  550.2 23.2 %collective-permute-start.19 = (bf16[3328,128]{1,0:T(8,128)(2,1)}, bf16[3328,128]{1,0:T(8,128)(2,1)}, u32[]{:S(2)}, u32[]{:S(2)}) collective-permute-start(bf16[3328,128]{1,0:T(8,128)(2,1)} %fusion.21), channel_id=1, source_target_pairs={{0,8},{4,12},{24,16},{28,20},{1,9},{5,13},{25,17},{29,21},{2,10},{... | collective-permute-start | bytes 2555912 | tf_op jit(solution)/shard_map/ppermute | solution.py:147
  570.0 22.2 %collective-permute-start.27 = (bf16[3328,128]{1,0:T(8,128)(2,1)}, bf16[3328,128]{1,0:T(8,128)(2,1)}, u32[]{:S(2)}, u32[]{:S(2)}) collective-permute-start(bf16[3328,128]{1,0:T(8,128)(2,1)} %get-tuple-element.436), channel_id=1, source_target_pairs={{0,4},{4,0},{8,12},{12,8},{16,20},{20,16},{24,28},{28,24},{1,5},{5... | collective-permute-start | bytes 2555912 | tf_op jit(solution)/shard_map/ppermute | solution.py:84
  570.5 57.4 %collective-permute-start.31 = (bf16[3328,128]{1,0:T(8,128)(2,1)}, bf16[3328,128]{1,0:T(8,128)(2,1)}, u32[]{:S(2)}, u32[]{:S(2)}) collective-permute-start(bf16[3328,128]{1,0:T(8,128)(2,1)} %get-tuple-element.435), channel_id=1, source_target_pairs={{0,4},{4,0},{8,12},{12,8},{16,20},{20,16},{24,28},{28,24},{1,5},{5... | collective-permute-start | bytes 2555912 | tf_op jit(solution)/shard_map/ppermute | solution.py:84
  572.0 26.1 %collective-permute-start.28 = (bf16[256,2048]{1,0:T(8,128)(2,1)S(1)}, bf16[256,2048]{1,0:T(8,128)(2,1)S(1)}, u32[]{:S(2)}, u32[]{:S(2)}) collective-permute-start(bf16[256,2048]{1,0:T(8,128)(2,1)S(1)} %get-tuple-element.445), channel_id=1, source_target_pairs={{0,2},{1,3},{2,0},{3,1},{4,6},{5,7},{6,4},{7,5},{8,10},{9,11},{10,... | collective-permute-start | bytes 3145736 | tf_op jit(solution)/shard_map/ppermute | solution.py:84
  577.3 21.7 %collective-permute-start.25 = (bf16[3328,128]{1,0:T(8,128)(2,1)}, bf16[3328,128]{1,0:T(8,128)(2,1)}, u32[]{:S(2)}, u32[]{:S(2)}) collective-permute-start(bf16[3328,128]{1,0:T(8,128)(2,1)} %fusion.12), channel_id=1, source_target_pairs={{0,8},{4,12},{8,16},{12,20},{1,9},{5,13},{9,17},{13,21},{2,10},{6,... | collective-permute-start | bytes 2555912 | tf_op jit(solution)/shard_map/ppermute | solution.py:147
  582.8 16.3 %collective-permute-start.26 = (bf16[3328,128]{1,0:T(8,128)(2,1)}, bf16[3328,128]{1,0:T(8,128)(2,1)}, u32[]{:S(2)}, u32[]{:S(2)}) collective-permute-start(bf16[3328,128]{1,0:T(8,128)(2,1)} %fusion.12), channel_id=1, source_target_pairs={{24,16},{28,20},{16,8},{20,12},{25,17},{29,21},{17,9},{21,13},{26,... | collective-permute-start | bytes 2555912 | tf_op jit(solution)/shard_map/ppermute | solution.py:147
  592.2 35.9 %collective-permute-start.32 = (bf16[256,2048]{1,0:T(8,128)(2,1)}, bf16[256,2048]{1,0:T(8,128)(2,1)}, u32[]{:S(2)}, u32[]{:S(2)}) collective-permute-start(bf16[256,2048]{1,0:T(8,128)(2,1)} %get-tuple-element.444), channel_id=1, source_target_pairs={{0,2},{1,3},{2,0},{3,1},{4,6},{5,7},{6,4},{7,5},{8,10},{9,11},{10,... | collective-permute-start | bytes 3145736 | tf_op jit(solution)/shard_map/ppermute | solution.py:84
  598.1 62.4 %collective-permute-start.38 = (bf16[256,2048]{1,0:T(8,128)(2,1)}, bf16[256,2048]{1,0:T(8,128)(2,1)}, u32[]{:S(2)}, u32[]{:S(2)}) collective-permute-start(bf16[256,2048]{1,0:T(8,128)(2,1)} %get-tuple-element.443), channel_id=1, source_target_pairs={{0,2},{1,3},{2,0},{3,1},{4,6},{5,7},{6,4},{7,5},{8,10},{9,11},{10,... | collective-permute-start | bytes 3145736 | tf_op jit(solution)/shard_map/ppermute | solution.py:84
  603.4 25.1 %collective-permute-start.29 = (bf16[3328,128]{1,0:T(8,128)(2,1)}, bf16[3328,128]{1,0:T(8,128)(2,1)}, u32[]{:S(2)}, u32[]{:S(2)}) collective-permute-start(bf16[3328,128]{1,0:T(8,128)(2,1)} %get-tuple-element.434), channel_id=1, source_target_pairs={{0,8},{4,12},{8,16},{12,20},{16,24},{20,28},{1,9},{5,13},{9,17},{1... | collective-permute-start | bytes 2555912 | tf_op jit(solution)/shard_map/ppermute | solution.py:147
  612.4 20.1 %collective-permute-start.30 = (bf16[3328,128]{1,0:T(8,128)(2,1)}, bf16[3328,128]{1,0:T(8,128)(2,1)}, u32[]{:S(2)}, u32[]{:S(2)}) collective-permute-start(bf16[3328,128]{1,0:T(8,128)(2,1)} %get-tuple-element.433), channel_id=1, source_target_pairs={{24,16},{28,20},{16,8},{20,12},{8,0},{12,4},{25,17},{29,21},{17,9}... | collective-permute-start | bytes 2555912 | tf_op jit(solution)/shard_map/ppermute | solution.py:147
  628.0 43.0 %collective-permute-start.23 = (bf16[512,2048]{1,0:T(8,128)(2,1)}, bf16[512,2048]{1,0:T(8,128)(2,1)}, u32[]{:S(2)}, u32[]{:S(2)}) collective-permute-start(bf16[512,2048]{1,0:T(8,128)(2,1)} %get-tuple-element.429), channel_id=1, source_target_pairs={{0,1},{1,0},{2,3},{3,2},{4,5},{5,4},{6,7},{7,6},{8,9},{9,8},{10,11... | collective-permute-start | bytes 6291464 | tf_op jit(solution)/shard_map/ppermute | solution.py:84
  628.0 48.9 %collective-permute-start.24 = (bf16[512,2048]{1,0:T(8,128)(2,1)S(1)}, bf16[512,2048]{1,0:T(8,128)(2,1)}, u32[]{:S(2)}, u32[]{:S(2)}) collective-permute-start(bf16[512,2048]{1,0:T(8,128)(2,1)S(1)} %get-tuple-element.430), channel_id=1, source_target_pairs={{0,1},{1,0},{2,3},{3,2},{4,5},{5,4},{6,7},{7,6},{8,9},{9,8},{10,11... | collective-permute-start | bytes 6291464 | tf_op jit(solution)/shard_map/ppermute | solution.py:84
  633.1 23.9 %collective-permute-start.33 = (f32[1,91440]{1,0:T(1,128)S(1)}, f32[1,91440]{1,0:T(1,128)}, u32[]{:S(2)}, u32[]{:S(2)}) collective-permute-start(f32[1,91440]{1,0:T(1,128)S(1)} %broadcast_in_dim.148), channel_id=1, source_target_pairs={{0,16},{4,20},{8,24},{12,28},{16,0},{20,4},{24,8},{28,12},{1,17},{... | collective-permute-start | bytes 1097288 | tf_op jit(solution)/shard_map/ppermute | solution.py:84
  660.5 8.9 %collective-permute-start.34 = (f32[1,50480]{1,0:T(1,128)S(1)}, f32[1,50480]{1,0:T(1,128)S(1)}, u32[]{:S(2)}, u32[]{:S(2)}) collective-permute-start(f32[1,50480]{1,0:T(1,128)S(1)} %broadcast_in_dim.150), channel_id=1, source_target_pairs={{0,8},{4,12},{8,0},{12,4},{16,24},{20,28},{24,16},{28,20},{1,9},{5... | collective-permute-start | bytes 605768 | tf_op jit(solution)/shard_map/ppermute | solution.py:84
  669.3 13.8 %collective-permute-start.39 = (bf16[1024,2048]{1,0:T(8,128)(2,1)}, bf16[1024,2048]{1,0:T(8,128)(2,1)}, u32[]{:S(2)}, u32[]{:S(2)}) collective-permute-start(bf16[1024,2048]{1,0:T(8,128)(2,1)} %add_convert_fusion.own_ref), channel_id=1, source_target_pairs={{0,1},{1,0},{2,3},{3,2},{4,5},{5,4},{6,7},{7,6},{8,9},{9,8},{10,11... | collective-permute-start | bytes 12582920 | tf_op jit(solution)/shard_map/ppermute | solution.py:84
  670.3 5.7 collective-permute-start.35
  676.8 2.0 collective-permute-start.36
  679.1 20.6 %collective-permute-start.37 = (f32[1,85248]{1,0:T(1,128)S(1)}, f32[1,85248]{1,0:T(1,128)S(1)}, u32[]{:S(2)}, u32[]{:S(2)}) collective-permute-start(f32[1,85248]{1,0:T(1,128)S(1)} %reshape_add_fusion), channel_id=1, source_target_pairs={{0,2},{1,3},{2,0},{3,1},{4,6},{5,7},{6,4},{7,5},{8,10},{9,11},{10,... | collective-permute-start | bytes 1022984 | tf_op jit(solution)/shard_map/ppermute | solution.py:84
  (43 other events, 396.7 us)
Sparse Core Ops, SparseCore 0:
  15.5 124.2 all-gather.3
  142.6 90.8 all-gather.5
